TPU v7x, 256 devices: a whole 4x4x8 slice. The times are simulated.
256 devices in a mesh: seq: 32 (over z_hi, y, core), head: 8 (over z_lo, x).
Axes of the slice: x: 4, y: 4, z: 8 (z_hi: 4, z_lo: 2; z = z_hi * 2 + z_lo), core: 2. Of those that a mesh axis runs over, the one named last changes fastest.
Arguments:
- queries: bfloat16 [384, 64, 128], P('seq', 'head'), may hold values from -88 to 88
- prompt_keys: bfloat16 [65536, 8, 128], P('seq', 'head'), may hold values from -4 to 4
- prompt_values: bfloat16 [65536, 8, 128], P('seq', 'head'), may hold values from -6 to 6
- suffix_keys: bfloat16 [384, 8, 1024, 128], P('seq', 'head'), may hold values from -8 to 8
- suffix_values: bfloat16 [384, 8, 1024, 128], P('seq', 'head'), may hold values from -6 to 6
- suffix_lengths: int32 [384], P('seq'), may hold values from 1 to 1024, as said below
- slot_of_sample: int32 [384], replicated, may hold values from 0 to 383, each once
- out_weight: bfloat16 [8192, 5120], P('head', 'seq'), may hold values from -0.0625 to 0.0625
Outputs:
- projected: float32 [384, 5120], P('head', 'seq')
Inputs may be any that keep to these rules, and one draw needn't show every extreme that they name: `suffix_lengths`: slot j is held with the samples of seq index j // 12; some slot has exactly 1024 live tokens. `slot_of_sample`: each slot is named once.
All inputs are finite; a program needn't handle non-finite values.
Results may differ from a plain program's by a relative error of at most 0.006.
Values may be sent and summed in bfloat16 or wider, within the bound.
No kernel may reach another device: no remote copies, remote signals or barrier semaphores. Data moves between devices by JAX's collectives and lax.ppermute only.
A program may use at most 64 MiB of HBM per device.

v0:
```python
import math

import jax
import jax.numpy as jnp
from jax import lax
from jax.sharding import PartitionSpec as P


def partial_softmax(scores, values_block, equation):
    row_max = jnp.max(scores, axis=-1)
    weights = jnp.exp(scores - row_max[..., None])
    row_total = jnp.sum(weights, axis=-1)
    output = jnp.einsum(
        equation, weights.astype(jnp.bfloat16), values_block, preferred_element_type=jnp.float32
    )
    return (output, row_max, row_total)


def per_device(
    queries,
    prompt_keys,
    prompt_values,
    suffix_keys,
    suffix_values,
    suffix_lengths,
    slot_of_sample,
    out_weight,
):
    local_count, heads_local, head_width = queries.shape
    kv_local = prompt_keys.shape[1]
    group_size = heads_local // kv_local
    score_scale = 1.0 / math.sqrt(head_width)
    all_queries = lax.all_gather(queries, "seq", axis=0, tiled=True)
    total_rows = all_queries.shape[0]
    block_rows = math.gcd(total_rows, 64)

    def prefix_block(query_block):
        grouped = query_block.reshape(block_rows, kv_local, group_size, head_width)
        scores = (
            jnp.einsum("bkgd,pkd->bkgp", grouped, prompt_keys, preferred_element_type=jnp.float32)
            * score_scale
        )
        output, row_max, row_total = partial_softmax(scores, prompt_values, "bkgp,pkd->bkgd")
        return (
            output.reshape(block_rows, heads_local, head_width),
            row_max.reshape(block_rows, heads_local),
            row_total.reshape(block_rows, heads_local),
        )

    blocks = all_queries.reshape(total_rows // block_rows, block_rows, heads_local, head_width)
    pre_out, pre_max, pre_total = lax.map(prefix_block, blocks)
    pre_out = pre_out.reshape(total_rows, heads_local, head_width)
    pre_max = pre_max.reshape(total_rows, heads_local)
    pre_total = pre_total.reshape(total_rows, heads_local)
    my_slots = lax.axis_index("seq") * local_count + jnp.arange(local_count, dtype=jnp.int32)
    matches = (slot_of_sample[None, :] == my_slots[:, None]).astype(jnp.int32)
    samples = jnp.sum(matches * jnp.arange(total_rows, dtype=jnp.int32)[None, :], axis=1)
    own_queries = all_queries[samples].reshape(local_count, kv_local, group_size, head_width)
    tail_scores = (
        jnp.einsum("bkgd,bksd->bkgs", own_queries, suffix_keys, preferred_element_type=jnp.float32)
        * score_scale
    )
    positions = jnp.arange(suffix_keys.shape[2], dtype=jnp.int32)
    live_mask = positions[None, None, None, :] < suffix_lengths[:, None, None, None]
    tail_scores = jnp.where(live_mask, tail_scores, jnp.float32(-1e30))
    tail_out, tail_max, tail_total = partial_softmax(tail_scores, suffix_values, "bkgs,bksd->bkgd")
    tail_out = tail_out.reshape(local_count, heads_local, head_width)
    tail_max = tail_max.reshape(local_count, heads_local)
    tail_total = tail_total.reshape(local_count, heads_local)
    old_max = pre_max[samples]
    joint_max = jnp.maximum(old_max, tail_max)
    old_factor = jnp.exp(old_max - joint_max)
    new_factor = jnp.exp(tail_max - joint_max)
    joint_out = pre_out[samples] * old_factor[..., None] + tail_out * new_factor[..., None]
    joint_total = pre_total[samples] * old_factor + tail_total * new_factor
    pre_out = pre_out.at[samples].set(joint_out)
    pre_max = pre_max.at[samples].set(joint_max)
    pre_total = pre_total.at[samples].set(joint_total)
    got_out, got_max, got_total = (
        lax.all_to_all(pre_out[None], "seq", split_axis=1, concat_axis=0, tiled=True),
        lax.all_to_all(pre_max[None], "seq", split_axis=1, concat_axis=0, tiled=True),
        lax.all_to_all(pre_total[None], "seq", split_axis=1, concat_axis=0, tiled=True),
    )
    best = jnp.max(got_max, axis=0)
    factors = jnp.exp(got_max - best[None])
    merged_out = jnp.sum(got_out * factors[..., None], axis=0)
    merged_total = jnp.sum(got_total * factors, axis=0)
    attention = (merged_out / merged_total[..., None]).astype(jnp.bfloat16)
    attention = attention.reshape(local_count, heads_local * head_width)
    terms = jnp.dot(
        lax.all_gather(attention, "seq", axis=0, tiled=True),
        out_weight,
        preferred_element_type=jnp.float32,
    )
    return lax.psum_scatter(terms, "head", scatter_dimension=0, tiled=True)


def solution(mesh):
    placed = (
        P("seq", "head", None),
        P("seq", "head", None),
        P("seq", "head", None),
        P("seq", "head", None, None),
        P("seq", "head", None, None),
        P("seq"),
        P(),
        P("head", "seq"),
    )
    return jax.shard_map(
        per_device, mesh=mesh, in_specs=placed, out_specs=P("head", "seq"), check_vma=False
    )
```

profile of v0, /device:TPU:1, one launch (start us, length us, event | category | flops | bytes accessed | tf_op | source)
XLA Modules:
  0.0 271.1 jit_solution(6006449799806385714)
XLA Ops:
  6.5 54.8 %all_gather.6 = bf16[384,8,128]{2,1,0:T(8,128)(2,1)} all-gather(bf16[12,8,128]{2,1,0:T(8,128)(2,1)} %param.10), channel_id=1, replica_groups=mesh['seq'=32,'head'=8] {'seq'}, dimensions={0}, use_global_device_ids=true | all-gather | bytes 811008 | tf_op jit(solution)/shard_map/all_gather | solution.py:33
  61.4 29.6 %while.14 = (s32[]{:T(128)}, f32[6,64,8,128]{3,2,1,0:T(8,128)}, f32[6,64,8]{2,1,0:T(8,128)S(1)}, f32[6,64,8]{2,1,0:T(8,128)}, bf16[6,64,8,128]{3,2,1,0:T(8,128)(...) while((s32[]{:T(128)}, f32[6,64,8,128]{3,2,1,0:T(8,128)}, ...), condition=%wide.region_3.4_spmd, body=%wide.region_0.3_spmd.sunk | while | flops 545258496 | bytes 16261253 | solution.py:51
  61.4 2.0 bitcast_reduce_fusion.2
  63.4 1.5 fusion.60
  66.3 2.0 bitcast_reduce_fusion.2
  68.3 1.5 fusion.60
  71.2 2.0 bitcast_reduce_fusion.2
  73.2 1.5 fusion.60
  76.1 2.0 bitcast_reduce_fusion.2
  78.1 1.5 fusion.60
  81.1 2.0 bitcast_reduce_fusion.2
  83.0 1.5 fusion.60
  86.0 2.0 bitcast_reduce_fusion.2
  88.0 1.5 fusion.60
  91.7 2.3 gather_fusion.2
  95.8 1.7 fusion.49
  99.0 3.3 %scatter_custom_fusion.2 = f32[384,8]{1,0:T(8,128)} fusion(f32[384,8]{1,0:T(8,128)} %bitcast.118, s32[12]{0:T(128)} %copy-done.6, f32[12,8]{1,0:T(8,128)} %fusion.37, f32[12,8]{1,0:T(8,128)} %get-tuple-element.82, f32[12,8]{1,0:T(8,128)S(1)} %get-tuple-element.81, s32[1024]{0:T(1024)} %copy-done.5), kind=kCustom, calls=%fused_computation.45 | custom fusion | flops 288 | bytes 229760 | tf_op jit(solution)/shard_map/scatter | solution.py:78
  102.3 4.4 %all-to-all-start.2 = ((f32[1,384,8]{2,0,1:T(1,128)}), f32[1,384,8]{2,0,1:T(1,128)}, u32[]{:S(2)}, u32[]{:S(2)}) async-start(f32[1,384,8]{2,0,1:T(1,128)} %bitcast.119), calls=%async_computation.2 | async-start | bytes 393216 | tf_op jit(solution)/shard_map/all_to_all | solution.py:82
  106.6 2.3 scatter_custom_fusion.1
  109.0 2.7 gather_fusion
  111.7 6.6 %all-to-all-done.2 = f32[1,384,8]{2,0,1:T(1,128)} async-done(((f32[1,384,8]{2,0,1:T(1,128)}), f32[1,384,8]{2,0,1:T(1,128)}, u32[]{:S(2)}, u32[]{:S(2)}) %all-to-all-start.2) | async-done | bytes 12320 | tf_op jit(solution)/shard_map/all_to_all | solution.py:82
  118.3 4.4 %all-to-all-start.1 = ((f32[1,384,8]{2,0,1:T(1,128)}), f32[1,384,8]{2,0,1:T(1,128)}, u32[]{:S(2)}, u32[]{:S(2)}) async-start(f32[1,384,8]{2,0,1:T(1,128)} %bitcast.122), calls=%async_computation.1 | async-start | bytes 393216 | tf_op jit(solution)/shard_map/all_to_all | solution.py:81
  122.7 3.1 %fusion.34 = f32[12,8,128]{2,1,0:T(8,128)} fusion(bf16[12,1,1024,128]{3,2,1,0:T(8,128)(2,1)} %param.14, f32[12,8,1024]{2,1,0:T(8,128)S(1)} %get-tuple-element.84, f32[12,8]{1,0:T(8,128)S(1)} %get-tuple-element.83, f32[12,8,128]{2,1,0:T(8,128)} %gather_fusion, f32[12,8]{1,0:T(8,128)} %get-tuple-element.82, f32[12,8]{1,0:T(8,128)S(1)} %get-tuple-element.81), kind=kOutput, calls=%fused_computation.35 | convolution fusion | flops 25399296 | bytes 3638400 | tf_op jit(solution)/shard_map/bkgs,bksd->bkgd/dot_general | solution.py:13
  125.8 2.2 scatter_fusion
  128.0 6.4 %all-to-all-done.1 = f32[1,384,8]{2,0,1:T(1,128)} async-done(((f32[1,384,8]{2,0,1:T(1,128)}), f32[1,384,8]{2,0,1:T(1,128)}, u32[]{:S(2)}, u32[]{:S(2)}) %all-to-all-start.1) | async-done | bytes 12320 | tf_op jit(solution)/shard_map/all_to_all | solution.py:81
  134.4 4.5 %all-to-all-start = ((f32[1,384,8,128]{3,2,0,1:T(8,128)}), f32[1,384,8,128]{3,2,0,1:T(8,128)}, u32[]{:S(2)}, u32[]{:S(2)}) async-start(f32[1,384,8,128]{3,2,0,1:T(8,128)} %bitcast.117), calls=%async_computation | async-start | bytes 3145728 | tf_op jit(solution)/shard_map/all_to_all | solution.py:80
  141.7 37.0 %all-to-all-done = f32[1,384,8,128]{3,2,0,1:T(8,128)} async-done(((f32[1,384,8,128]{3,2,0,1:T(8,128)}), f32[1,384,8,128]{3,2,0,1:T(8,128)}, u32[]{:S(2)}, u32[]{:S(2)}) %all-to-all-start) | async-done | bytes 1572896 | tf_op jit(solution)/shard_map/all_to_all | solution.py:80
  178.8 1.9 multiply_reduce_fusion
  180.8 47.2 %all-gather = bf16[32,12,1024]{2,1,0:T(8,128)(2,1)} all-gather(bf16[1,12,1024]{2,1,0:T(8,128)(2,1)S(1)} %reshape.221), channel_id=1, replica_groups=mesh['seq'=32,'head'=8] {'seq'}, dimensions={0}, use_global_device_ids=true | all-gather | bytes 811008 | tf_op jit(solution)/shard_map/all_gather | solution.py:91
  228.1 2.1 reshape.222
  230.2 2.3 fusion.50
  232.5 31.8 %reduce-scatter.2.cloned.1.call-done = f32[48,160]{1,0:T(8,128)} async-done(((f32[384,160]{1,0:T(8,128)}), f32[48,160]{1,0:T(8,128)}) %reduce-scatter.2.cloned.1.call-update) | async-done | bytes 30736 | tf_op jit(solution)/shard_map/reduce_scatter | solution.py:95
  (63 shorter events, 15.5 us)
Async XLA Ops:
  6.5 89.3 %copy-start = (bf16[12,1,1024,128]{3,2,1,0:T(8,128)(2,1)S(1)}, bf16[12,1,1024,128]{3,2,1,0:T(8,128)(2,1)}, u32[]{:S(2)}) copy-start(bf16[12,1,1024,128]{3,2,1,0:T(8,128)(2,1)} %param.13) | copy-start | bytes 9437188
  61.4 29.6 %copy-start.7 = (s32[384]{0:T(512)S(1)}, s32[384]{0:T(512)}, u32[]{:S(2)}) copy-start(s32[384]{0:T(512)} %param.16) | copy-start | bytes 4612
  61.4 32.6 %copy-start.8 = (s32[12]{0:T(128)S(1)}, s32[12]{0:T(128)}, u32[]{:S(2)}) copy-start(s32[12]{0:T(128)} %param.15) | copy-start | bytes 148
  61.4 2.0 copy-start.1
  66.3 2.0 copy-start.1
  71.2 2.0 copy-start.1
  76.1 2.0 copy-start.1
  81.1 2.0 copy-start.1
  86.0 2.0 copy-start.1
  90.9 3.7 %copy-start.2 = (f32[6,64,8]{2,1,0:T(8,128)}, f32[6,64,8]{2,1,0:T(8,128)S(1)}, u32[]{:S(2)}) copy-start(f32[6,64,8]{2,1,0:T(8,128)S(1)} %get-tuple-element.45) | copy-start | bytes 36868
  91.1 0.5 copy-start.6
  91.7 3.0 %copy-start.5 = (s32[1024]{0:T(1024)}, s32[1024]{0:T(1024)S(1)}, u32[]{:S(2)}) copy-start(s32[1024]{0:T(1024)S(1)} %pad_clamp_fusion) | copy-start | bytes 12292
  95.8 1.8 copy-start.4
  102.3 16.0 %all-to-all-start.2 = ((f32[1,384,8]{2,0,1:T(1,128)}), f32[1,384,8]{2,0,1:T(1,128)}, u32[]{:S(2)}, u32[]{:S(2)}) async-start(f32[1,384,8]{2,0,1:T(1,128)} %bitcast.119), calls=%async_computation.2 | async-start | bytes 393216 | tf_op jit(solution)/shard_map/all_to_all | solution.py:82
  118.3 16.1 %all-to-all-start.1 = ((f32[1,384,8]{2,0,1:T(1,128)}), f32[1,384,8]{2,0,1:T(1,128)}, u32[]{:S(2)}, u32[]{:S(2)}) async-start(f32[1,384,8]{2,0,1:T(1,128)} %bitcast.122), calls=%async_computation.1 | async-start | bytes 393216 | tf_op jit(solution)/shard_map/all_to_all | solution.py:81
  134.4 44.4 %all-to-all-start = ((f32[1,384,8,128]{3,2,0,1:T(8,128)}), f32[1,384,8,128]{3,2,0,1:T(8,128)}, u32[]{:S(2)}, u32[]{:S(2)}) async-start(f32[1,384,8,128]{3,2,0,1:T(8,128)} %bitcast.117), calls=%async_computation | async-start | bytes 3145728 | tf_op jit(solution)/shard_map/all_to_all | solution.py:80
  138.9 125.3 %reduce-scatter.2.cloned.1.call-start = ((), (), s32[]{:S(2)}) async-start(), calls=%async_computation.4 | async-start | bytes 442368 | tf_op jit(solution)/shard_map/reduce_scatter | solution.py:95
  180.7 49.5 %copy-start.3 = (bf16[1024,160]{0,1:T(8,128)(2,1)S(1)}, bf16[1024,160]{0,1:T(8,128)(2,1)}, u32[]{:S(2)}) copy-start(bf16[1024,160]{0,1:T(8,128)(2,1)} %param.17) | copy-start | bytes 983044
Sparse Core Ops, SparseCore 0:
  232.6 31.5 reduce-scatter.1
where the time goes:
time: 276 us; the launch traced here: 271 us
  blocking collectives  102 us (37%)
  waiting for transfers between devices  81.8 us (30%)
  matrix products  28 us (10%)
  local copies, waits for them, and re-layouts  17.5 us (6%)
  other arithmetic  14.8 us (5%)
  between operations  13.5 us (5%)
  starting transfers between devices  13.2 us (5%)
    all_gather x1, blocking collectives, per_device(): all_queries = lax.all_gather(queries, 'seq', axis=0, tiled=True)  54.8 us
    all_gather x1, blocking collectives, per_device(): lax.all_gather(attention, 'seq', axis=0, tiled=True)  47.2 us
    all_to_all x1, waiting for transfers between devices, per_device(): lax.all_to_all(pre_out[None], 'seq', split_axis=1, concat_axis=0, tiled=T...  37 us
    reduce_scatter x1, waiting for transfers between devices, per_device(): return lax.psum_scatter(terms, 'head', scatter_dimension=0, tiled=True)  31.8 us
    dot_general x7, matrix products, partial_softmax(): jnp.einsum(equation, weights.astype(jnp.bfloat16), values_block, preferre...  12.3 us
    dot_general x6, matrix products, prefix_block(): jnp.einsum('bkgd,pkd->bkgp', grouped, prompt_keys, preferred_element_type...  11.7 us
    all_to_all x1, waiting for transfers between devices, per_device(): lax.all_to_all(pre_total[None], 'seq', split_axis=1, concat_axis=0, tiled...  6.63 us
    all_to_all x1, waiting for transfers between devices, per_device(): lax.all_to_all(pre_max[None], 'seq', split_axis=1, concat_axis=0, tiled=T...  6.39 us
  transfers between devices with their start and end apart: 4, of which 4 were waited for; matrix products, arithmetic and copies ran while one was open for 5% of the time, Pallas kernels for 0%

commit v1 on v0

v1 whole, which is shorter than its diff:
```python
import functools
import math

import jax
import jax.numpy as jnp
from jax import lax
from jax.experimental import pallas as pl
from jax.experimental.pallas import tpu as pltpu
from jax.sharding import PartitionSpec as P

Z, Y, C = 4, 4, 2
SEQ = Z * Y * C
HEADS_LOCAL = 8
WIDTH = 128
LOCAL = 12
ROWS = LOCAL * HEADS_LOCAL
CHUNK = Z * ROWS
STATS = 16
PART = CHUNK + STATS
TILES = CHUNK // 128
SUFFIX = 1024
BLOCK = 256
EXPONENT = math.log2(math.e) / math.sqrt(WIDTH)
DEAD = -1e30


def exchange(x, dz, dy, dc):
    def index(z, y, c):
        return (z * Y + y) * C + c

    pairs = [
        (index(z, y, c), index(z ^ dz, y ^ dy, c ^ dc))
        for z in range(Z)
        for y in range(Y)
        for c in range(C)
    ]
    return lax.ppermute(x, "seq", pairs)


def near(x):
    return x.astype(jnp.bfloat16).astype(jnp.float32)


def attention_kernel(
    samples_ref,
    lengths_ref,
    queries_ref,
    keys_ref,
    values_ref,
    tail_keys_ref,
    tail_values_ref,
    first_ref,
    second_ref,
    tail_k,
    tail_v,
    wide,
    scores,
    acc,
    total,
    top,
    sem,
):
    copies = [
        pltpu.make_async_copy(tail_keys_ref, tail_k, sem.at[0]),
        pltpu.make_async_copy(tail_values_ref, tail_v, sem.at[1]),
    ]
    for copy in copies:
        copy.start()
    wide[:, :WIDTH] = values_ref[...]
    wide[:, WIDTH:] = jnp.ones_like(wide[:, WIDTH:])
    nt = (((1,), (1,)), ((), ()))

    def score(block, slot):
        q = queries_ref[pl.ds(block * BLOCK, BLOCK), :]
        scores[slot] = lax.dot_general(q, keys_ref[...], nt, preferred_element_type=jnp.float32)

    def weigh(block, slot):
        s = scores[slot]
        c = near(jnp.max(s, axis=1, keepdims=True) * EXPONENT)
        w = jnp.exp2(s * EXPONENT - c).astype(jnp.bfloat16)
        o = jnp.dot(w, wide[...], preferred_element_type=jnp.float32)
        rows = pl.ds(block * BLOCK, BLOCK)
        acc[rows, :] = o[:, :WIDTH]
        total[rows, :] = o[:, WIDTH:]
        top[rows, :] = jnp.broadcast_to(c, (BLOCK, WIDTH))

    blocks = SEQ * ROWS // BLOCK
    score(0, 0)

    def body(i, carry):
        score(2 * i + 1, 1)
        weigh(2 * i, 0)
        score(jnp.minimum(2 * i + 2, blocks - 1), 0)
        weigh(2 * i + 1, 1)
        return carry

    lax.fori_loop(0, blocks // 2, body, 0)

    for copy in copies:
        copy.wait()
    position = lax.broadcasted_iota(jnp.int32, (HEADS_LOCAL, SUFFIX), 1)
    tails = []
    for j in range(LOCAL):
        row = samples_ref[j]
        base = pl.multiple_of(row // 16 * 16, 16)
        pair = queries_ref[pl.ds(base, 16), :].astype(jnp.float32)
        q = jnp.where(row % 16 == 8, pair[8:], pair[:8]).astype(jnp.bfloat16)
        s = lax.dot_general(q, tail_k[j], nt, preferred_element_type=jnp.float32)
        tails.append(jnp.where(position < lengths_ref[j], s * EXPONENT, DEAD))
    for j in range(LOCAL):
        c = near(jnp.max(tails[j], axis=1, keepdims=True))
        w = jnp.exp2(tails[j] - c)
        t = jnp.sum(w, axis=1, keepdims=True)
        o = jnp.dot(w.astype(jnp.bfloat16), tail_v[j], preferred_element_type=jnp.float32)
        rows = pl.ds(pl.multiple_of(samples_ref[j], 8), 8)
        old = top[rows, :]
        new = jnp.maximum(old, c)
        f, g = jnp.exp2(old - new), jnp.exp2(c - new)
        acc[rows, :] = acc[rows, :] * f + o * g
        total[rows, :] = total[rows, :] * f + t * g
        top[rows, :] = new

    lane = lax.broadcasted_iota(jnp.int32, (128, 128), 1)
    for chunk in range(C * Y):
        part = (first_ref if chunk < Y else second_ref).at[chunk % Y]
        stats = []
        for tile in range(TILES):
            rows = pl.ds(chunk * CHUNK + tile * 128, 128)
            part[pl.ds(tile * 128, 128), :] = acc[rows, :].astype(jnp.bfloat16)
            sums = total[rows, :]
            high = near(sums)
            mixed = jnp.where(lane == 0, top[rows, :], jnp.where(lane == 1, high, sums - high))
            stats.append(jnp.transpose(mixed)[:4])
        stats.append(jnp.zeros((STATS - 4 * TILES, 128), jnp.float32))
        part[pl.ds(CHUNK, STATS), :] = jnp.concatenate(stats, axis=0).astype(jnp.bfloat16)


def merge_tile(parts, tile, offsets=None):
    stats = [part[pl.ds(CHUNK, STATS), :].astype(jnp.float32) for part in parts]
    tops = [s[4 * tile : 4 * tile + 1] for s in stats]
    totals = [s[4 * tile + 1 : 4 * tile + 2] + s[4 * tile + 2 : 4 * tile + 3] for s in stats]
    best = functools.reduce(jnp.maximum, tops)
    factors = [jnp.exp2(t - best) for t in tops]
    whole = functools.reduce(jnp.add, [t * f for t, f in zip(totals, factors)])
    return factors, best, whole


def columns(rows):
    block = jnp.concatenate(rows + [jnp.zeros((128 - len(rows), 128), jnp.float32)], axis=0)
    turned = jnp.transpose(block)
    return [turned[:, i : i + 1] for i in range(len(rows))]


def merge_into(parts, out_ref):
    stats = []
    for tile in range(TILES):
        factors, best, whole = merge_tile(parts, tile)
        rows = pl.ds(tile * 128, 128)
        terms = [p[rows, :].astype(jnp.float32) * f for p, f in zip(parts, columns(factors))]
        out_ref[rows, :] = functools.reduce(jnp.add, terms).astype(jnp.bfloat16)
        high = near(whole)
        stats += [best, high, whole - high, jnp.zeros_like(best)]
    stats.append(jnp.zeros((STATS - 4 * TILES, 128), jnp.float32))
    out_ref[pl.ds(CHUNK, STATS), :] = jnp.concatenate(stats, axis=0).astype(jnp.bfloat16)


def core_kernel(mine_ref, other_ref, *out_refs):
    for dy in range(Y):
        merge_into([mine_ref.at[dy], other_ref.at[dy]], out_refs[dy])


def y_kernel(*refs):
    merge_into(refs[:Y], refs[Y])


def z_kernel(z_ref, *refs):
    parts, out_ref, spread, merged = refs[:Z], refs[Z], refs[Z + 1], refs[Z + 2]
    z = z_ref[0]
    for k, part in enumerate(parts):
        block = [part[pl.ds(CHUNK, STATS), :].astype(jnp.float32)]
        block.append(jnp.zeros((128 - STATS, 128), jnp.float32))
        turned = jnp.transpose(jnp.concatenate(block, axis=0))
        for tile in range(TILES):
            rows = pl.ds(tile * 128, 128)
            c = turned[:, 4 * tile : 4 * tile + 1]
            t = turned[:, 4 * tile + 1 : 4 * tile + 2] + turned[:, 4 * tile + 2 : 4 * tile + 3]
            spread[0, k, rows, :] = jnp.broadcast_to(c, (128, 128))
            spread[1, k, rows, :] = jnp.broadcast_to(t, (128, 128))
    for place in range(Z):
        sums, tops, totals = [], [], []
        for k, part in enumerate(parts):
            rows = pl.ds(pl.multiple_of((z ^ place ^ k) * ROWS, 32), ROWS)
            sums.append(part[rows, :].astype(jnp.float32))
            tops.append(spread[0, k, rows, :])
            totals.append(spread[1, k, rows, :])
        best = functools.reduce(jnp.maximum, tops)
        factors = [jnp.exp2(t - best) for t in tops]
        out = functools.reduce(jnp.add, [s * f for s, f in zip(sums, factors)])
        whole = functools.reduce(jnp.add, [t * f for t, f in zip(totals, factors)])
        merged[pl.ds(place * ROWS, ROWS), :] = out / whole
    for head in range(HEADS_LOCAL):
        rows = merged[pl.ds(head, Z * LOCAL, stride=HEADS_LOCAL), :]
        out_ref[:, head * WIDTH : (head + 1) * WIDTH] = rows.astype(jnp.bfloat16)


def project_kernel(place_ref, mine_ref, other_ref, weight_ref, out_ref, terms):
    weight = weight_ref[...]
    for dc, ref in enumerate((mine_ref, other_ref)):
        for dy in range(Y):
            terms[dc * Y + dy] = jnp.dot(ref[dy], weight, preferred_element_type=jnp.float32)
    y, c = place_ref[1], place_ref[2]
    for there_y in range(Y):
        for there_c in range(C):
            found = terms[(c ^ there_c) * Y + (y ^ there_y)]
            for z in range(Z):
                row = ((z * Y + there_y) * C + there_c) * LOCAL
                out_ref[row : row + LOCAL, :] = found[z * LOCAL : (z + 1) * LOCAL]


VMEM = pl.BlockSpec(memory_space=pltpu.VMEM)
SMEM = pl.BlockSpec(memory_space=pltpu.SMEM)


def per_device(
    queries,
    prompt_keys,
    prompt_values,
    suffix_keys,
    suffix_values,
    suffix_lengths,
    slot_of_sample,
    out_weight,
):
    me = lax.axis_index("seq")
    z, y, c = me // (Y * C), me // C % Y, me % C
    place = jnp.stack([z, y, c]).astype(jnp.int32)
    bf16 = jnp.bfloat16

    mine = queries.reshape(ROWS, WIDTH)
    by_z = jnp.concatenate([mine] + [exchange(mine, d, 0, 0) for d in range(1, Z)])
    by_y = jnp.concatenate([by_z] + [exchange(by_z, 0, d, 0) for d in range(1, Y)])
    every = jnp.concatenate([by_y, exchange(by_y, 0, 0, 1)])

    slots = me * LOCAL + jnp.arange(LOCAL, dtype=jnp.int32)
    matches = (slot_of_sample[None, :] == slots[:, None]).astype(jnp.int32)
    samples = jnp.sum(matches * jnp.arange(SEQ * LOCAL, dtype=jnp.int32)[None, :], axis=1)
    away = (samples // LOCAL) ^ me
    spot = (away % C) * (Y * Z) + (away // C % Y) * Z + away // (Y * C)
    rows = spot * ROWS + samples % LOCAL * HEADS_LOCAL

    half = jax.ShapeDtypeStruct((Y, PART, WIDTH), bf16)
    part = jax.ShapeDtypeStruct((PART, WIDTH), bf16)
    total_rows = SEQ * ROWS
    prompt = prompt_keys.shape[0]
    first, second = pl.pallas_call(
        attention_kernel,
        out_shape=(half, half),
        in_specs=[SMEM, SMEM, VMEM, VMEM, VMEM] + [pl.BlockSpec(memory_space=pl.ANY)] * 2,
        out_specs=(VMEM, VMEM),
        scratch_shapes=[
            pltpu.VMEM((LOCAL, SUFFIX, WIDTH), bf16),
            pltpu.VMEM((LOCAL, SUFFIX, WIDTH), bf16),
            pltpu.VMEM((prompt, 2 * WIDTH), bf16),
            pltpu.VMEM((2, BLOCK, prompt), jnp.float32),
            pltpu.VMEM((total_rows, WIDTH), jnp.float32),
            pltpu.VMEM((total_rows, WIDTH), jnp.float32),
            pltpu.VMEM((total_rows, WIDTH), jnp.float32),
            pltpu.SemaphoreType.DMA((2,)),
        ],
        compiler_params=pltpu.CompilerParams(vmem_limit_bytes=48 * 2**20),
        name="attention",
    )(
        rows.astype(jnp.int32),
        suffix_lengths,
        every,
        prompt_keys.reshape(prompt, WIDTH),
        prompt_values.reshape(prompt, WIDTH),
        suffix_keys.reshape(LOCAL, SUFFIX, WIDTH),
        suffix_values.reshape(LOCAL, SUFFIX, WIDTH),
    )

    arrived = exchange(second, 0, 0, 1)
    by_dy = pl.pallas_call(
        core_kernel,
        out_shape=(part,) * Y,
        in_specs=[VMEM] * 2,
        out_specs=(VMEM,) * Y,
        name="merge_core",
    )(first, arrived)
    merged = pl.pallas_call(
        y_kernel, out_shape=part, in_specs=[VMEM] * Y, out_specs=VMEM, name="merge_y"
    )(by_dy[0], *[exchange(by_dy[d], 0, d, 0) for d in range(1, Y)])
    attention = pl.pallas_call(
        z_kernel,
        out_shape=jax.ShapeDtypeStruct((Z * LOCAL, HEADS_LOCAL * WIDTH), bf16),
        in_specs=[SMEM] + [VMEM] * Z,
        out_specs=VMEM,
        scratch_shapes=[
            pltpu.VMEM((2, Z, CHUNK, 128), jnp.float32),
            pltpu.VMEM((CHUNK, 128), jnp.float32),
        ],
        name="merge_z",
    )(place, merged, *[exchange(merged, d, 0, 0) for d in range(1, Z)])

    ours = jnp.stack([attention] + [exchange(attention, 0, d, 0) for d in range(1, Y)])
    theirs = exchange(ours, 0, 0, 1)
    depth, columns_local = out_weight.shape
    terms = pl.pallas_call(
        project_kernel,
        out_shape=jax.ShapeDtypeStruct((SEQ * LOCAL, columns_local), jnp.float32),
        in_specs=[SMEM] + [VMEM] * 3,
        out_specs=VMEM,
        scratch_shapes=[pltpu.VMEM((C * Y, Z * LOCAL, columns_local), jnp.float32)],
        name="project",
    )(place, ours, theirs, out_weight)
    heads = lax.axis_size("head")
    terms = terms.astype(bf16).reshape(heads, SEQ * LOCAL // heads, columns_local)
    swapped = lax.all_to_all(terms, "head", split_axis=0, concat_axis=0, tiled=True)
    return jnp.sum(swapped.astype(jnp.float32), axis=0)


def solution(mesh):
    placed = (
        P("seq", "head", None),
        P("seq", "head", None),
        P("seq", "head", None),
        P("seq", "head", None, None),
        P("seq", "head", None, None),
        P("seq"),
        P(),
        P("head", "seq"),
    )
    return jax.shard_map(
        per_device, mesh=mesh, in_specs=placed, out_specs=P("head", "seq"), check_vma=False
    )
```

time: 276 us -> 109 us (0.39); the launches traced: 271 us -> 109 us
  blocking collectives: 102 us -> 12 us
  waiting for transfers between devices: 81.8 us -> 26 us
  matrix products: 28 us -> 0 us
  Pallas kernels: 0 us -> 22.3 us
  starting transfers between devices: 13.2 us -> 33.2 us
  between operations: 13.5 us -> 0.12 us
  other arithmetic: 14.8 us -> 4.82 us
  local copies, waits for them, and re-layouts: 17.5 us -> 10.2 us
    all_gather x2 -> x0, blocking collectives: 102 us -> none  [the longest x1 54.8 us: per_device(): all_queries = lax.all_gather(queries, 'seq', axis=0, tiled=True)]
    all_to_all x3 -> x0, waiting for transfers between devices: 50.1 us -> none  [the longest x1 37 us: per_device(): lax.all_to_all(pre_out[None], 'seq', split_axis=1, concat_axis=0, tiled=T...]
    ppermute x0 -> x18, starting transfers between devices: none -> 33.2 us  [exchange(): return lax.ppermute(x, 'seq', pairs)]
    reduce_scatter x1 -> x0, waiting for transfers between devices: 31.8 us -> none  [per_device(): return lax.psum_scatter(terms, 'head', scatter_dimension=0, tiled=True)]
    dot_general x15 -> x0, matrix products: 28 us -> none  [the longest x7 12.3 us: partial_softmax(): jnp.einsum(equation, weights.astype(jnp.bfloat16), values_block, preferre...]
    ppermute x0 -> x18, waiting for transfers between devices: none -> 26 us  [exchange(): return lax.ppermute(x, 'seq', pairs)]
    pallas_call x0 -> x5, Pallas kernels: none -> 22.3 us  [the longest x1 11.9 us: per_device(): pl.pallas_call(attention_kernel, out_shape=(half, half), in_specs=[SMEM,...]
    all_to_all x3 -> x0, starting transfers between devices: 13.2 us -> none  [the longest x1 4.48 us: per_device(): lax.all_to_all(pre_out[None], 'seq', split_axis=1, concat_axis=0, tiled=T...]
  transfers between devices with their start and end apart: 4 -> 18, of which waited for: 4 -> 15; matrix products, arithmetic and copies ran while one was open for 5% -> 3% of each run, Pallas kernels for 0% -> 0%
where the time goes in v1:
time: 109 us
  starting transfers between devices  33.2 us (30%)
  waiting for transfers between devices  26 us (24%)
  Pallas kernels  22.3 us (20%)
  blocking collectives  12 us (11%)
  local copies, waits for them, and re-layouts  10.2 us (9%)
  other arithmetic  4.82 us (4%)
    ppermute x18, starting transfers between devices, exchange(): return lax.ppermute(x, 'seq', pairs)  33.2 us
    ppermute x18, waiting for transfers between devices, exchange(): return lax.ppermute(x, 'seq', pairs)  26 us
    all_to_all x1, blocking collectives, per_device(): lax.all_to_all(terms, 'head', split_axis=0, concat_axis=0, tiled=True)  12 us
    pallas_call x1, Pallas kernels, per_device(): pl.pallas_call(attention_kernel, out_shape=(half, half), in_specs=[SMEM,...  11.9 us
    unnamed x37, local copies, waits for them, and re-layouts  10.1 us
    pallas_call x1, Pallas kernels, per_device(): pl.pallas_call(project_kernel, out_shape=jax.ShapeDtypeStruct((SEQ * LOCA...  2.92 us
    pallas_call x1, Pallas kernels, per_device(): pl.pallas_call(z_kernel, out_shape=jax.ShapeDtypeStruct((Z * LOCAL, HEADS...  2.7 us
    pallas_call x1, Pallas kernels, per_device(): pl.pallas_call(core_kernel, out_shape=(part,) * Y, in_specs=[VMEM] * 2, o...  2.63 us
  transfers between devices with their start and end apart: 18, of which 15 were waited for; matrix products, arithmetic and copies ran while one was open for 3% of the time, Pallas kernels for 0%

profile of v1, /device:TPU:1, one launch (start us, length us, event | category | flops | bytes accessed | tf_op | source)
XLA Modules:
  0.0 108.6 jit_solution(7440151974640434444)
XLA Ops:
  0.0 3.8 %collective-permute-start = (bf16[96,128]{1,0:T(8,128)(2,1)}, bf16[96,128]{1,0:T(8,128)(2,1)S(1)}, u32[]{:S(2)}, u32[]{:S(2)}) collective-permute-start(bf16[96,128]{1,0:T(8,128)(2,1)} %bitcast.24), channel_id=1, source_target_pairs={{0,64},{8,72},{16,80},{24,88},{32,96},{40,104},{48,112},{56,120},{... | collective-permute-start | bytes 73736 | tf_op jit(solution)/shard_map/ppermute | solution.py:37
  3.8 5.1 %collective-permute-start.1 = (bf16[96,128]{1,0:T(8,128)(2,1)}, bf16[96,128]{1,0:T(8,128)(2,1)S(1)}, u32[]{:S(2)}, u32[]{:S(2)}) collective-permute-start(bf16[96,128]{1,0:T(8,128)(2,1)} %bitcast.25), channel_id=1, source_target_pairs={{0,128},{8,136},{16,144},{24,152},{32,160},{40,168},{48,176},{56,1... | collective-permute-start | bytes 73736 | tf_op jit(solution)/shard_map/ppermute | solution.py:37
  10.6 3.3 %collective-permute-done.2 = bf16[96,128]{1,0:T(8,128)(2,1)S(1)} collective-permute-done((bf16[96,128]{1,0:T(8,128)(2,1)}, bf16[96,128]{1,0:T(8,128)(2,1)S(1)}, u32[]{:S(2)}, u32[]{:S(2)}) %collective-permute-start.2) | collective-permute-done | bytes 24608 | tf_op jit(solution)/shard_map/ppermute | solution.py:37
  14.7 1.3 %collective-permute-start.3 = (bf16[384,128]{1,0:T(8,128)(2,1)S(1)}, bf16[384,128]{1,0:T(8,128)(2,1)S(1)}, u32[]{:S(2)}, u32[]{:S(2)}) collective-permute-start(bf16[384,128]{1,0:T(8,128)(2,1)S(1)} %pad_maximum_fusion.1), channel_id=1, source_target_pairs={{0,16},{8,24},{16,0},{24,8},{32,48},{40,56},{48,32},{56,40},{64,80... | collective-permute-start | bytes 294920 | tf_op jit(solution)/shard_map/ppermute | solution.py:37
  16.0 2.6 %collective-permute-start.4 = (bf16[384,128]{1,0:T(8,128)(2,1)S(1)}, bf16[384,128]{1,0:T(8,128)(2,1)S(1)}, u32[]{:S(2)}, u32[]{:S(2)}) collective-permute-start(bf16[384,128]{1,0:T(8,128)(2,1)S(1)} %pad_maximum_fusion.1), channel_id=1, source_target_pairs={{0,32},{8,40},{16,48},{24,56},{32,0},{40,8},{48,16},{56,24},{64,96... | collective-permute-start | bytes 294920 | tf_op jit(solution)/shard_map/ppermute | solution.py:37
  18.7 3.0 %collective-permute-done.4 = bf16[384,128]{1,0:T(8,128)(2,1)S(1)} collective-permute-done((bf16[384,128]{1,0:T(8,128)(2,1)S(1)}, bf16[384,128]{1,0:T(8,128)(2,1)S(1)}, u32[]{:S(2)}, u32[]{:S(2)}) %collective-permute-start.4) | collective-permute-done | bytes 98336 | tf_op jit(solution)/shard_map/ppermute | solution.py:37
  21.7 1.6 %collective-permute-done.5 = bf16[384,128]{1,0:T(8,128)(2,1)S(1)} collective-permute-done((bf16[384,128]{1,0:T(8,128)(2,1)S(1)}, bf16[384,128]{1,0:T(8,128)(2,1)S(1)}, u32[]{:S(2)}, u32[]{:S(2)}) %collective-permute-start.5) | collective-permute-done | bytes 98336 | tf_op jit(solution)/shard_map/ppermute | solution.py:37
  23.3 4.2 %collective-permute-start.6 = (bf16[1536,128]{1,0:T(8,128)(2,1)S(1)}, bf16[1536,128]{1,0:T(8,128)(2,1)S(1)}, u32[]{:S(2)}, u32[]{:S(2)}) collective-permute-start(bf16[1536,128]{1,0:T(8,128)(2,1)S(1)} %get-tuple-element.17), channel_id=1, source_target_pairs={{0,8},{8,0},{16,24},{24,16},{32,40},{40,32},{48,56},{56,48},{64,72... | collective-permute-start | bytes 1179656 | tf_op jit(solution)/shard_map/ppermute | solution.py:37
  28.9 1.9 %copy-done = bf16[12,1,1024,128]{3,2,1,0:T(8,128)(2,1)S(1)} copy-done((bf16[12,1,1024,128]{3,2,1,0:T(8,128)(2,1)S(1)}, bf16[12,1,1024,128]{3,2,1,0:T(8,128)(2,1)}, u32[]{:S(2)}) %copy-start) | copy-done | bytes 3145752
  30.8 1.0 copy-done.1
  31.8 1.0 copy-done.2
  33.5 11.9 %attention.1 = (bf16[4,400,128]{2,1,0:T(8,128)(2,1)S(1)}, bf16[4,400,128]{2,1,0:T(8,128)(2,1)S(1)}) custom-call(s32[12]{0:T(128)S(1)} %fusion.5.samples_ref, s32[12]{0:T(128)S(1)} %copy-done.4, bf16[3072,128]{1,0:T(8,128)(2,1)S(1)} %constant_dynamic-update-slice_fusion.7.queries_ref, bf16[2048,128]{1,0:T(8,128)(2,1)S(1)} %bitcast.16, ...), custom_call_target="tpu_custom_call" | custom-call | tf_op jit(solution)/shard_map/attention/pallas_call | solution.py:255
  46.6 1.4 %collective-permute-done.7.other_ref = bf16[4,400,128]{2,1,0:T(8,128)(2,1)S(1)} collective-permute-done((bf16[4,400,128]{2,1,0:T(8,128)(2,1)S(1)}, bf16[4,400,128]{2,1,0:T(8,128)(2,1)S(1)}, u32[]{:S(2)}, u32[]{:S(2)}) %collective-permute-start.7) | collective-permute-done | bytes 409632 | tf_op jit(solution)/shard_map/ppermute | solution.py:37
  48.7 2.6 %merge_core.1 = (bf16[400,128]{1,0:T(8,128)(2,1)}, bf16[400,128]{1,0:T(8,128)(2,1)}, bf16[400,128]{1,0:T(8,128)(2,1)}, bf16[400,128]{1,0:T(8,128)(2,1)}) custom-call(bf16[4,400,128]{2,1,0:T(8,128)(2,1)} %copy-done.3, bf16[4,400,128]{2,1,0:T(8,128)(2,1)} %copy-done.6), custom_call_target="tpu_custom_call" | custom-call | tf_op jit(solution)/shard_map/merge_core/pallas_call | solution.py:283
  51.7 3.5 %collective-permute-start.9 = (bf16[400,128]{1,0:T(8,128)(2,1)}, bf16[400,128]{1,0:T(8,128)(2,1)S(1)}, u32[]{:S(2)}, u32[]{:S(2)}) collective-permute-start(bf16[400,128]{1,0:T(8,128)(2,1)} %get-tuple-element.15), channel_id=1, source_target_pairs={{0,32},{8,40},{16,48},{24,56},{32,0},{40,8},{48,16},{56,24},{64,96... | collective-permute-start | bytes 307208 | tf_op jit(solution)/shard_map/ppermute | solution.py:37
  55.2 1.7 %collective-permute-done.10.refs_3_ = bf16[400,128]{1,0:T(8,128)(2,1)S(1)} collective-permute-done((bf16[400,128]{1,0:T(8,128)(2,1)}, bf16[400,128]{1,0:T(8,128)(2,1)S(1)}, u32[]{:S(2)}, u32[]{:S(2)}) %collective-permute-start.10) | collective-permute-done | bytes 102432 | tf_op jit(solution)/shard_map/ppermute | solution.py:37
  56.9 2.8 %collective-permute-done.9.refs_2_ = bf16[400,128]{1,0:T(8,128)(2,1)S(1)} collective-permute-done((bf16[400,128]{1,0:T(8,128)(2,1)}, bf16[400,128]{1,0:T(8,128)(2,1)S(1)}, u32[]{:S(2)}, u32[]{:S(2)}) %collective-permute-start.9) | collective-permute-done | bytes 102432 | tf_op jit(solution)/shard_map/ppermute | solution.py:37
  60.3 2.1 %merge_y.1.refs_0_ = bf16[400,128]{1,0:T(8,128)(2,1)} custom-call(bf16[400,128]{1,0:T(8,128)(2,1)} %get-tuple-element.13.refs_0_, bf16[400,128]{1,0:T(8,128)(2,1)} %copy-done.13, bf16[400,128]{1,0:T(8,128)(2,1)} %copy-done.14, bf16[400,128]{1,0:T(8,128)(2,1)} %copy-done.12), custom_call_target="tpu_custom_call" | custom-call | tf_op jit(solution)/shard_map/merge_y/pallas_call | solution.py:290
  62.4 1.2 %collective-permute-start.11 = (bf16[400,128]{1,0:T(8,128)(2,1)}, bf16[400,128]{1,0:T(8,128)(2,1)S(1)}, u32[]{:S(2)}, u32[]{:S(2)}) collective-permute-start(bf16[400,128]{1,0:T(8,128)(2,1)} %merge_y.1.refs_0_), channel_id=1, source_target_pairs={{0,64},{8,72},{16,80},{24,88},{32,96},{40,104},{48,112},{56,120},{... | collective-permute-start | bytes 307208 | tf_op jit(solution)/shard_map/ppermute | solution.py:37
  63.5 1.5 %collective-permute-start.12 = (bf16[400,128]{1,0:T(8,128)(2,1)}, bf16[400,128]{1,0:T(8,128)(2,1)S(1)}, u32[]{:S(2)}, u32[]{:S(2)}) collective-permute-start(bf16[400,128]{1,0:T(8,128)(2,1)} %merge_y.1.refs_0_), channel_id=1, source_target_pairs={{0,128},{8,136},{16,144},{24,152},{32,160},{40,168},{48,176},{56,1... | collective-permute-start | bytes 307208 | tf_op jit(solution)/shard_map/ppermute | solution.py:37
  65.1 3.0 %collective-permute-start.13 = (bf16[400,128]{1,0:T(8,128)(2,1)}, bf16[400,128]{1,0:T(8,128)(2,1)S(1)}, u32[]{:S(2)}, u32[]{:S(2)}) collective-permute-start(bf16[400,128]{1,0:T(8,128)(2,1)} %merge_y.1.refs_0_), channel_id=1, source_target_pairs={{0,192},{8,200},{16,208},{24,216},{32,224},{40,232},{48,240},{56,2... | collective-permute-start | bytes 307208 | tf_op jit(solution)/shard_map/ppermute | solution.py:37
  68.6 2.1 %collective-permute-done.11.refs_1_ = bf16[400,128]{1,0:T(8,128)(2,1)S(1)} collective-permute-done((bf16[400,128]{1,0:T(8,128)(2,1)}, bf16[400,128]{1,0:T(8,128)(2,1)S(1)}, u32[]{:S(2)}, u32[]{:S(2)}) %collective-permute-start.11) | collective-permute-done | bytes 102432 | tf_op jit(solution)/shard_map/ppermute | solution.py:37
  70.7 1.2 %collective-permute-done.12.refs_2_ = bf16[400,128]{1,0:T(8,128)(2,1)S(1)} collective-permute-done((bf16[400,128]{1,0:T(8,128)(2,1)}, bf16[400,128]{1,0:T(8,128)(2,1)S(1)}, u32[]{:S(2)}, u32[]{:S(2)}) %collective-permute-start.12) | collective-permute-done | bytes 102432 | tf_op jit(solution)/shard_map/ppermute | solution.py:37
  71.9 3.3 %collective-permute-done.13.refs_3_ = bf16[400,128]{1,0:T(8,128)(2,1)S(1)} collective-permute-done((bf16[400,128]{1,0:T(8,128)(2,1)}, bf16[400,128]{1,0:T(8,128)(2,1)S(1)}, u32[]{:S(2)}, u32[]{:S(2)}) %collective-permute-start.13) | collective-permute-done | bytes 102432 | tf_op jit(solution)/shard_map/ppermute | solution.py:37
  75.8 2.7 %merge_z.1 = bf16[48,1024]{1,0:T(8,128)(2,1)} custom-call(s32[3]{0:T(128)} %pad_add_fusion.z_ref.place_ref, bf16[400,128]{1,0:T(8,128)(2,1)} %merge_y.1.refs_0_, bf16[400,128]{1,0:T(8,128)(2,1)} %copy-done.9, bf16[400,128]{1,0:T(8,128)(2,1)} %copy-done.10, bf16[400,128]{1,0:T(8,128)(2,1)} %copy-done.11), custom_call_target="tpu_custom_call" | custom-call | tf_op jit(solution)/shard_map/merge_z/pallas_call | solution.py:293
  78.6 4.0 %collective-permute-start.16 = (bf16[48,1024]{1,0:T(8,128)(2,1)}, bf16[48,1024]{1,0:T(8,128)(2,1)S(1)}, u32[]{:S(2)}, u32[]{:S(2)}) collective-permute-start(bf16[48,1024]{1,0:T(8,128)(2,1)} %merge_z.1), channel_id=1, source_target_pairs={{0,48},{8,56},{16,32},{24,40},{32,16},{40,24},{48,0},{56,8},{64,11... | collective-permute-start | bytes 294920 | tf_op jit(solution)/shard_map/ppermute | solution.py:37
  82.5 1.2 %collective-permute-done.15 = bf16[48,1024]{1,0:T(8,128)(2,1)S(1)} collective-permute-done((bf16[48,1024]{1,0:T(8,128)(2,1)}, bf16[48,1024]{1,0:T(8,128)(2,1)S(1)}, u32[]{:S(2)}, u32[]{:S(2)}) %collective-permute-start.15) | collective-permute-done | bytes 98336 | tf_op jit(solution)/shard_map/ppermute | solution.py:37
  83.7 1.9 %collective-permute-done.16 = bf16[48,1024]{1,0:T(8,128)(2,1)S(1)} collective-permute-done((bf16[48,1024]{1,0:T(8,128)(2,1)}, bf16[48,1024]{1,0:T(8,128)(2,1)S(1)}, u32[]{:S(2)}, u32[]{:S(2)}) %collective-permute-start.16) | collective-permute-done | bytes 98336 | tf_op jit(solution)/shard_map/ppermute | solution.py:37
  87.6 2.3 %collective-permute-start.17 = (bf16[4,48,1024]{2,1,0:T(8,128)(2,1)S(1)}, bf16[4,48,1024]{2,1,0:T(8,128)(2,1)S(1)}, u32[]{:S(2)}, u32[]{:S(2)}) collective-permute-start(bf16[4,48,1024]{2,1,0:T(8,128)(2,1)S(1)} %pad_maximum_fusion.mine_ref), channel_id=1, source_target_pairs={{0,8},{8,0},{16,24},{24,16},{32,40},{40,32},{48,56},{56,48},{64,72... | collective-permute-start | bytes 1179656 | tf_op jit(solution)/shard_map/ppermute | solution.py:37
  92.0 2.9 %project.1 = f32[384,160]{1,0:T(8,128)} custom-call(s32[3]{0:T(128)} %pad_add_fusion.z_ref.place_ref, bf16[4,48,1024]{2,1,0:T(8,128)(2,1)} %copy-done.5, bf16[4,48,1024]{2,1,0:T(8,128)(2,1)} %copy-done.7, bf16[1024,160]{1,0:T(8,128)(2,1)} %copy.10.weight_ref), custom_call_target="tpu_custom_call" | custom-call | tf_op jit(solution)/shard_map/project/pallas_call | solution.py:308
  94.9 1.0 convert_element_type.7
  96.0 12.0 %all_to_all.5 = bf16[8,48,160]{2,1,0:T(8,128)(2,1)S(1)} all-to-all(bf16[8,48,160]{2,1,0:T(8,128)(2,1)S(1)} %bitcast.19), channel_id=1, replica_groups=mesh['seq'=32,'head'=8] {'head'}, dimensions={0} | all-to-all | bytes 245760 | tf_op jit(solution)/shard_map/all_to_all | solution.py:318
  (57 shorter events, 13.4 us)
Async XLA Ops:
  0.0 9.7 %collective-permute-start = (bf16[96,128]{1,0:T(8,128)(2,1)}, bf16[96,128]{1,0:T(8,128)(2,1)S(1)}, u32[]{:S(2)}, u32[]{:S(2)}) collective-permute-start(bf16[96,128]{1,0:T(8,128)(2,1)} %bitcast.24), channel_id=1, source_target_pairs={{0,64},{8,72},{16,80},{24,88},{32,96},{40,104},{48,112},{56,120},{... | collective-permute-start | bytes 73736 | tf_op jit(solution)/shard_map/ppermute | solution.py:37
  3.8 6.8 %collective-permute-start.1 = (bf16[96,128]{1,0:T(8,128)(2,1)}, bf16[96,128]{1,0:T(8,128)(2,1)S(1)}, u32[]{:S(2)}, u32[]{:S(2)}) collective-permute-start(bf16[96,128]{1,0:T(8,128)(2,1)} %bitcast.25), channel_id=1, source_target_pairs={{0,128},{8,136},{16,144},{24,152},{32,160},{40,168},{48,176},{56,1... | collective-permute-start | bytes 73736 | tf_op jit(solution)/shard_map/ppermute | solution.py:37
  8.9 5.0 %collective-permute-start.2 = (bf16[96,128]{1,0:T(8,128)(2,1)}, bf16[96,128]{1,0:T(8,128)(2,1)S(1)}, u32[]{:S(2)}, u32[]{:S(2)}) collective-permute-start(bf16[96,128]{1,0:T(8,128)(2,1)} %bitcast.26), channel_id=1, source_target_pairs={{0,192},{8,200},{16,208},{24,216},{32,224},{40,232},{48,240},{56,2... | collective-permute-start | bytes 73736 | tf_op jit(solution)/shard_map/ppermute | solution.py:37
  14.7 4.0 %collective-permute-start.3 = (bf16[384,128]{1,0:T(8,128)(2,1)S(1)}, bf16[384,128]{1,0:T(8,128)(2,1)S(1)}, u32[]{:S(2)}, u32[]{:S(2)}) collective-permute-start(bf16[384,128]{1,0:T(8,128)(2,1)S(1)} %pad_maximum_fusion.1), channel_id=1, source_target_pairs={{0,16},{8,24},{16,0},{24,8},{32,48},{40,56},{48,32},{56,40},{64,80... | collective-permute-start | bytes 294920 | tf_op jit(solution)/shard_map/ppermute | solution.py:37
  16.0 5.7 %collective-permute-start.4 = (bf16[384,128]{1,0:T(8,128)(2,1)S(1)}, bf16[384,128]{1,0:T(8,128)(2,1)S(1)}, u32[]{:S(2)}, u32[]{:S(2)}) collective-permute-start(bf16[384,128]{1,0:T(8,128)(2,1)S(1)} %pad_maximum_fusion.1), channel_id=1, source_target_pairs={{0,32},{8,40},{16,48},{24,56},{32,0},{40,8},{48,16},{56,24},{64,96... | collective-permute-start | bytes 294920 | tf_op jit(solution)/shard_map/ppermute | solution.py:37
  18.6 4.7 %collective-permute-start.5 = (bf16[384,128]{1,0:T(8,128)(2,1)S(1)}, bf16[384,128]{1,0:T(8,128)(2,1)S(1)}, u32[]{:S(2)}, u32[]{:S(2)}) collective-permute-start(bf16[384,128]{1,0:T(8,128)(2,1)S(1)} %pad_maximum_fusion.1), channel_id=1, source_target_pairs={{0,48},{8,56},{16,32},{24,40},{32,16},{40,24},{48,0},{56,8},{64,11... | collective-permute-start | bytes 294920 | tf_op jit(solution)/shard_map/ppermute | solution.py:37
  23.3 5.5 %collective-permute-start.6 = (bf16[1536,128]{1,0:T(8,128)(2,1)S(1)}, bf16[1536,128]{1,0:T(8,128)(2,1)S(1)}, u32[]{:S(2)}, u32[]{:S(2)}) collective-permute-start(bf16[1536,128]{1,0:T(8,128)(2,1)S(1)} %get-tuple-element.17), channel_id=1, source_target_pairs={{0,8},{8,0},{16,24},{24,16},{32,40},{40,32},{48,56},{56,48},{64,72... | collective-permute-start | bytes 1179656 | tf_op jit(solution)/shard_map/ppermute | solution.py:37
  28.9 1.9 %copy-start = (bf16[12,1,1024,128]{3,2,1,0:T(8,128)(2,1)S(1)}, bf16[12,1,1024,128]{3,2,1,0:T(8,128)(2,1)}, u32[]{:S(2)}) copy-start(bf16[12,1,1024,128]{3,2,1,0:T(8,128)(2,1)} %param.11) | copy-start | bytes 9437188
  30.8 1.0 copy-start.1
  31.8 1.0 copy-start.2
  32.9 0.7 copy-start.4
  33.5 56.4 %copy-start.8 = (bf16[1024,160]{0,1:T(8,128)(2,1)S(1)}, bf16[1024,160]{0,1:T(8,128)(2,1)}, u32[]{:S(2)}) copy-start(bf16[1024,160]{0,1:T(8,128)(2,1)} %param.15) | copy-start | bytes 983044
  45.4 0.8 copy-start.3
  46.2 1.7 %collective-permute-start.7 = (bf16[4,400,128]{2,1,0:T(8,128)(2,1)S(1)}, bf16[4,400,128]{2,1,0:T(8,128)(2,1)S(1)}, u32[]{:S(2)}, u32[]{:S(2)}) collective-permute-start(bf16[4,400,128]{2,1,0:T(8,128)(2,1)S(1)} %get-tuple-element.12), channel_id=1, source_target_pairs={{0,8},{8,0},{16,24},{24,16},{32,40},{40,32},{48,56},{56,48},{64,72... | collective-permute-start | bytes 1228808 | tf_op jit(solution)/shard_map/ppermute | solution.py:37
  47.9 0.8 copy-start.6
  51.3 5.5 %collective-permute-start.10 = (bf16[400,128]{1,0:T(8,128)(2,1)}, bf16[400,128]{1,0:T(8,128)(2,1)S(1)}, u32[]{:S(2)}, u32[]{:S(2)}) collective-permute-start(bf16[400,128]{1,0:T(8,128)(2,1)} %get-tuple-element.16), channel_id=1, source_target_pairs={{0,48},{8,56},{16,32},{24,40},{32,16},{40,24},{48,0},{56,8},{64,11... | collective-permute-start | bytes 307208 | tf_op jit(solution)/shard_map/ppermute | solution.py:37
  51.7 5.2 %collective-permute-start.8 = (bf16[400,128]{1,0:T(8,128)(2,1)}, bf16[400,128]{1,0:T(8,128)(2,1)S(1)}, u32[]{:S(2)}, u32[]{:S(2)}) collective-permute-start(bf16[400,128]{1,0:T(8,128)(2,1)} %get-tuple-element.14), channel_id=1, source_target_pairs={{0,16},{8,24},{16,0},{24,8},{32,48},{40,56},{48,32},{56,40},{64,80... | collective-permute-start | bytes 307208 | tf_op jit(solution)/shard_map/ppermute | solution.py:37
  51.7 7.9 %collective-permute-start.9 = (bf16[400,128]{1,0:T(8,128)(2,1)}, bf16[400,128]{1,0:T(8,128)(2,1)S(1)}, u32[]{:S(2)}, u32[]{:S(2)}) collective-permute-start(bf16[400,128]{1,0:T(8,128)(2,1)} %get-tuple-element.15), channel_id=1, source_target_pairs={{0,32},{8,40},{16,48},{24,56},{32,0},{40,8},{48,16},{56,24},{64,96... | collective-permute-start | bytes 307208 | tf_op jit(solution)/shard_map/ppermute | solution.py:37
  56.8 2.8 %copy-start.12 = (bf16[400,128]{1,0:T(8,128)(2,1)}, bf16[400,128]{1,0:T(8,128)(2,1)S(1)}, u32[]{:S(2)}) copy-start(bf16[400,128]{1,0:T(8,128)(2,1)S(1)} %collective-permute-done.10.refs_3_) | copy-start | bytes 307204
  56.8 2.8 %copy-start.13 = (bf16[400,128]{1,0:T(8,128)(2,1)}, bf16[400,128]{1,0:T(8,128)(2,1)S(1)}, u32[]{:S(2)}) copy-start(bf16[400,128]{1,0:T(8,128)(2,1)S(1)} %collective-permute-done.8.refs_1_) | copy-start | bytes 307204
  62.4 8.4 %collective-permute-start.11 = (bf16[400,128]{1,0:T(8,128)(2,1)}, bf16[400,128]{1,0:T(8,128)(2,1)S(1)}, u32[]{:S(2)}, u32[]{:S(2)}) collective-permute-start(bf16[400,128]{1,0:T(8,128)(2,1)} %merge_y.1.refs_0_), channel_id=1, source_target_pairs={{0,64},{8,72},{16,80},{24,88},{32,96},{40,104},{48,112},{56,120},{... | collective-permute-start | bytes 307208 | tf_op jit(solution)/shard_map/ppermute | solution.py:37
  63.5 8.4 %collective-permute-start.12 = (bf16[400,128]{1,0:T(8,128)(2,1)}, bf16[400,128]{1,0:T(8,128)(2,1)S(1)}, u32[]{:S(2)}, u32[]{:S(2)}) collective-permute-start(bf16[400,128]{1,0:T(8,128)(2,1)} %merge_y.1.refs_0_), channel_id=1, source_target_pairs={{0,128},{8,136},{16,144},{24,152},{32,160},{40,168},{48,176},{56,1... | collective-permute-start | bytes 307208 | tf_op jit(solution)/shard_map/ppermute | solution.py:37
  65.1 10.1 %collective-permute-start.13 = (bf16[400,128]{1,0:T(8,128)(2,1)}, bf16[400,128]{1,0:T(8,128)(2,1)S(1)}, u32[]{:S(2)}, u32[]{:S(2)}) collective-permute-start(bf16[400,128]{1,0:T(8,128)(2,1)} %merge_y.1.refs_0_), channel_id=1, source_target_pairs={{0,192},{8,200},{16,208},{24,216},{32,224},{40,232},{48,240},{56,2... | collective-permute-start | bytes 307208 | tf_op jit(solution)/shard_map/ppermute | solution.py:37
  70.7 4.5 %copy-start.9 = (bf16[400,128]{1,0:T(8,128)(2,1)}, bf16[400,128]{1,0:T(8,128)(2,1)S(1)}, u32[]{:S(2)}) copy-start(bf16[400,128]{1,0:T(8,128)(2,1)S(1)} %collective-permute-done.11.refs_1_) | copy-start | bytes 307204
  71.9 3.3 %copy-start.10 = (bf16[400,128]{1,0:T(8,128)(2,1)}, bf16[400,128]{1,0:T(8,128)(2,1)S(1)}, u32[]{:S(2)}) copy-start(bf16[400,128]{1,0:T(8,128)(2,1)S(1)} %collective-permute-done.12.refs_2_) | copy-start | bytes 307204
  75.2 0.7 copy-start.11
  78.5 5.2 %collective-permute-start.15 = (bf16[48,1024]{1,0:T(8,128)(2,1)}, bf16[48,1024]{1,0:T(8,128)(2,1)S(1)}, u32[]{:S(2)}, u32[]{:S(2)}) collective-permute-start(bf16[48,1024]{1,0:T(8,128)(2,1)} %merge_z.1), channel_id=1, source_target_pairs={{0,32},{8,40},{16,48},{24,56},{32,0},{40,8},{48,16},{56,24},{64,96... | collective-permute-start | bytes 294920 | tf_op jit(solution)/shard_map/ppermute | solution.py:37
  78.6 7.1 %collective-permute-start.16 = (bf16[48,1024]{1,0:T(8,128)(2,1)}, bf16[48,1024]{1,0:T(8,128)(2,1)S(1)}, u32[]{:S(2)}, u32[]{:S(2)}) collective-permute-start(bf16[48,1024]{1,0:T(8,128)(2,1)} %merge_z.1), channel_id=1, source_target_pairs={{0,48},{8,56},{16,32},{24,40},{32,16},{40,24},{48,0},{56,8},{64,11... | collective-permute-start | bytes 294920 | tf_op jit(solution)/shard_map/ppermute | solution.py:37
  82.5 4.1 %collective-permute-start.14 = (bf16[48,1024]{1,0:T(8,128)(2,1)}, bf16[48,1024]{1,0:T(8,128)(2,1)S(1)}, u32[]{:S(2)}, u32[]{:S(2)}) collective-permute-start(bf16[48,1024]{1,0:T(8,128)(2,1)} %merge_z.1), channel_id=1, source_target_pairs={{0,16},{8,24},{16,0},{24,8},{32,48},{40,56},{48,32},{56,40},{64,80... | collective-permute-start | bytes 294920 | tf_op jit(solution)/shard_map/ppermute | solution.py:37
  87.6 3.7 %copy-start.5 = (bf16[4,48,1024]{2,1,0:T(8,128)(2,1)}, bf16[4,48,1024]{2,1,0:T(8,128)(2,1)S(1)}, u32[]{:S(2)}) copy-start(bf16[4,48,1024]{2,1,0:T(8,128)(2,1)S(1)} %pad_maximum_fusion.mine_ref) | copy-start | bytes 1179652
  87.6 3.6 %collective-permute-start.17 = (bf16[4,48,1024]{2,1,0:T(8,128)(2,1)S(1)}, bf16[4,48,1024]{2,1,0:T(8,128)(2,1)S(1)}, u32[]{:S(2)}, u32[]{:S(2)}) collective-permute-start(bf16[4,48,1024]{2,1,0:T(8,128)(2,1)S(1)} %pad_maximum_fusion.mine_ref), channel_id=1, source_target_pairs={{0,8},{8,0},{16,24},{24,16},{32,40},{40,32},{48,56},{56,48},{64,72... | collective-permute-start | bytes 1179656 | tf_op jit(solution)/shard_map/ppermute | solution.py:37
  91.3 0.7 copy-start.7
  (1 other events, 0.7 us)

commit v2 on v1

v2 whole, which is shorter than its diff:
```python
import functools
import math

import jax
import jax.numpy as jnp
from jax import lax
from jax.experimental import pallas as pl
from jax.experimental.pallas import tpu as pltpu
from jax.sharding import PartitionSpec as P

Z, Y, C = 4, 4, 2
SEQ = Z * Y * C
HEADS_LOCAL = 8
WIDTH = 128
LOCAL = 12
ROWS = LOCAL * HEADS_LOCAL
CHUNK = Z * ROWS
STATS = 16
PART = CHUNK + STATS
TILES = CHUNK // 128
SUFFIX = 1024
BLOCK = 256
EXPONENT = math.log2(math.e) / math.sqrt(WIDTH)
DEAD = -1e30
AROUND_Z = (0, 1, 3, 2)
AROUND_Y = (2, 1, 3)


def exchange(x, dz, dy, dc):
    def index(z, y, c):
        return (z * Y + y) * C + c

    pairs = [
        (index(z, y, c), index(z ^ dz, y ^ dy, c ^ dc))
        for z in range(Z)
        for y in range(Y)
        for c in range(C)
    ]
    return lax.ppermute(x, "seq", pairs)


def join_kernel(*refs):
    for i, ref in enumerate(refs[:-1]):
        refs[-1][i] = ref[...]


def join_z_kernel(info_ref, *refs):
    z = info_ref[2 * LOCAL]
    for offset, ref in zip(AROUND_Z, refs[:-1]):
        refs[-1][z ^ offset] = ref[...]


def join(kernel, pieces, *scalars):
    return pl.pallas_call(
        kernel,
        out_shape=jax.ShapeDtypeStruct((len(pieces), *pieces[0].shape), pieces[0].dtype),
        in_specs=[SMEM] * len(scalars) + [VMEM] * len(pieces),
        out_specs=VMEM,
        compiler_params=PARAMS,
        name="join",
    )(*scalars, *pieces)


def gather_y(x):
    found = {d: exchange(x, 0, d, 0) for d in AROUND_Y}
    return join(join_kernel, [x] + [found[d] for d in range(1, Y)])


def copy_kernel(in_ref, out_ref):
    out_ref[...] = in_ref[...]


def near(x):
    return x.astype(jnp.bfloat16).astype(jnp.float32)


def attention_kernel(
    info_ref,
    mine_ref,
    other_ref,
    keys_hbm,
    values_hbm,
    tail_keys_hbm,
    tail_values_hbm,
    first_ref,
    second_ref,
    queries_ref,
    keys_ref,
    wide_ref,
    tail_k,
    tail_v,
    scores,
    acc,
    total,
    top,
    sem,
):
    pairs = [
        (keys_hbm, keys_ref),
        (values_hbm, wide_ref.at[:, pl.ds(0, WIDTH)]),
        (tail_keys_hbm, tail_k),
        (tail_values_hbm, tail_v),
    ]
    copies = [pltpu.make_async_copy(a, b, sem.at[i]) for i, (a, b) in enumerate(pairs)]
    for copy in copies:
        copy.start()
    wide_ref[:, WIDTH:] = jnp.ones_like(wide_ref[:, WIDTH:])
    queries_ref[: Y * CHUNK] = mine_ref[...]
    queries_ref[Y * CHUNK :] = other_ref[...]
    nt = (((1,), (1,)), ((), ()))

    def score(block, slot):
        q = queries_ref[pl.ds(block * BLOCK, BLOCK), :]
        scores[slot] = lax.dot_general(q, keys_ref[...], nt, preferred_element_type=jnp.float32)

    def weigh(block, slot):
        s = scores[slot]
        c = near(jnp.max(s, axis=1, keepdims=True) * EXPONENT)
        w = jnp.exp2(s * EXPONENT - c).astype(jnp.bfloat16)
        o = jnp.dot(w, wide_ref[...], preferred_element_type=jnp.float32)
        rows = pl.ds(block * BLOCK, BLOCK)
        acc[rows, :] = o[:, :WIDTH]
        total[rows, :] = o[:, WIDTH:]
        top[rows, :] = jnp.broadcast_to(c, (BLOCK, WIDTH))

    blocks = SEQ * ROWS // BLOCK
    copies[0].wait()
    score(0, 0)
    copies[1].wait()
    for i in range(blocks):
        if i + 1 < blocks:
            score(i + 1, (i + 1) % 2)
        weigh(i, i % 2)

    copies[2].wait()
    copies[3].wait()
    position = lax.broadcasted_iota(jnp.int32, (HEADS_LOCAL, SUFFIX), 1)
    tails = []
    for j in range(LOCAL):
        row = info_ref[j]
        base = pl.multiple_of(row // 16 * 16, 16)
        pair = queries_ref[pl.ds(base, 16), :].astype(jnp.float32)
        q = jnp.where(row % 16 == 8, pair[8:], pair[:8]).astype(jnp.bfloat16)
        s = lax.dot_general(q, tail_k[j], nt, preferred_element_type=jnp.float32)
        tails.append(jnp.where(position < info_ref[LOCAL + j], s * EXPONENT, DEAD))
    for j in range(LOCAL):
        c = near(jnp.max(tails[j], axis=1, keepdims=True))
        w = jnp.exp2(tails[j] - c)
        t = jnp.sum(w, axis=1, keepdims=True)
        o = jnp.dot(w.astype(jnp.bfloat16), tail_v[j], preferred_element_type=jnp.float32)
        rows = pl.ds(pl.multiple_of(info_ref[j], 8), 8)
        old = top[rows, :]
        new = jnp.maximum(old, c)
        f, g = jnp.exp2(old - new), jnp.exp2(c - new)
        acc[rows, :] = acc[rows, :] * f + o * g
        total[rows, :] = total[rows, :] * f + t * g
        top[rows, :] = new

    lane = lax.broadcasted_iota(jnp.int32, (128, 128), 1)
    for chunk in range(C * Y):
        part = (first_ref if chunk < Y else second_ref).at[chunk % Y]
        stats = []
        for tile in range(TILES):
            rows = pl.ds(chunk * CHUNK + tile * 128, 128)
            part[pl.ds(tile * 128, 128), :] = acc[rows, :].astype(part.dtype)
            sums = total[rows, :]
            high = near(sums)
            mixed = jnp.where(lane == 0, top[rows, :], jnp.where(lane == 1, high, sums - high))
            stats.append(jnp.transpose(mixed)[:4])
        stats.append(jnp.zeros((STATS - 4 * TILES, 128), jnp.float32))
        part[pl.ds(CHUNK, STATS), :] = jnp.concatenate(stats, axis=0).astype(part.dtype)


def columns(rows):
    block = jnp.concatenate(rows + [jnp.zeros((128 - len(rows), 128), jnp.float32)], axis=0)
    turned = jnp.transpose(block)
    return [turned[:, i : i + 1] for i in range(len(rows))]


def merge_tile(parts, tile):
    stats = [part[pl.ds(CHUNK, STATS), :].astype(jnp.float32) for part in parts]
    tops = [s[4 * tile : 4 * tile + 1] for s in stats]
    totals = [s[4 * tile + 1 : 4 * tile + 2] + s[4 * tile + 2 : 4 * tile + 3] for s in stats]
    best = functools.reduce(jnp.maximum, tops)
    factors = [jnp.exp2(t - best) for t in tops]
    total = functools.reduce(jnp.add, [t * f for t, f in zip(totals, factors)])
    return factors, best, total


def weighted(parts, tile, factors):
    rows = pl.ds(tile * 128, 128)
    terms = [p[rows, :].astype(jnp.float32) * f for p, f in zip(parts, columns(factors))]
    return functools.reduce(jnp.add, terms)


def merge_into(parts, out_refs):
    stats = []
    for tile in range(TILES):
        factors, best, total = merge_tile(parts, tile)
        out = weighted(parts, tile, factors)
        for ref in out_refs:
            ref[pl.ds(tile * 128, 128), :] = out.astype(ref.dtype)
        high = near(total)
        stats += [best, high, total - high, jnp.zeros_like(best)]
    stats.append(jnp.zeros((STATS - 4 * TILES, 128), jnp.float32))
    for ref in out_refs:
        ref[pl.ds(CHUNK, STATS), :] = jnp.concatenate(stats, axis=0).astype(ref.dtype)


def core_kernel(mine_ref, other_ref, *out_refs):
    for dy in range(Y):
        merge_into([mine_ref.at[dy], other_ref.at[dy]], [out_refs[dy]])


def merge_kernel(*refs):
    merge_into(refs[:-2], refs[-2:])


def finish_kernel(mine_ref, other_ref, out_ref, merged):
    parts = [mine_ref, other_ref]
    for tile in range(TILES):
        factors, _, total = merge_tile(parts, tile)
        merged[pl.ds(tile * 128, 128), :] = weighted(parts, tile, [f / total for f in factors])
    for head in range(HEADS_LOCAL):
        rows = merged[pl.ds(head, Z * LOCAL, stride=HEADS_LOCAL), :]
        out_ref[:, head * WIDTH : (head + 1) * WIDTH] = rows.astype(out_ref.dtype)


def project_kernel(info_ref, mine_ref, other_ref, weight_ref, out_ref, terms):
    weight = weight_ref[...]
    for dc, ref in enumerate((mine_ref, other_ref)):
        for dy in range(Y):
            terms[dc * Y + dy] = lax.dot_general(
                ref[dy], weight, (((1,), (1,)), ((), ())), preferred_element_type=jnp.float32
            )
    y, c = info_ref[2 * LOCAL + 1], info_ref[2 * LOCAL + 2]
    for there_y in range(Y):
        for there_c in range(C):
            found = terms[(c ^ there_c) * Y + (y ^ there_y)]
            for z in range(Z):
                row = ((z * Y + there_y) * C + there_c) * LOCAL
                out_ref[row : row + LOCAL, :] = found[z * LOCAL : (z + 1) * LOCAL].astype(out_ref.dtype)


VMEM = pl.BlockSpec(memory_space=pltpu.VMEM)
SMEM = pl.BlockSpec(memory_space=pltpu.SMEM)
PARAMS = pltpu.CompilerParams(vmem_limit_bytes=32 * 2**20)


def per_device(
    queries,
    prompt_keys,
    prompt_values,
    suffix_keys,
    suffix_values,
    suffix_lengths,
    slot_of_sample,
    out_weight,
):
    me = lax.axis_index("seq")
    z, y, c = me // (Y * C), me // C % Y, me % C
    bf16 = jnp.bfloat16

    slots = me * LOCAL + jnp.arange(LOCAL, dtype=jnp.int32)
    matches = (slot_of_sample[None, :] == slots[:, None]).astype(jnp.int32)
    samples = jnp.sum(matches * jnp.arange(SEQ * LOCAL, dtype=jnp.int32)[None, :], axis=1)
    away = (samples // LOCAL) ^ me
    spot = (away % C) * (Y * Z) + (away // C % Y) * Z + samples // (LOCAL * Y * C)
    rows = spot * ROWS + samples % LOCAL * HEADS_LOCAL
    place = jnp.stack([z, y, c])
    info = jnp.concatenate([rows, suffix_lengths, place]).astype(jnp.int32)

    def shape(dtype, *more):
        return jax.ShapeDtypeStruct((*more, PART, WIDTH), dtype)

    total_rows = SEQ * ROWS
    prompt = prompt_keys.shape[0]
    caches = [
        pltpu.with_memory_space_constraint(x, pltpu.HBM)
        for x in (
            prompt_keys.reshape(prompt, WIDTH),
            prompt_values.reshape(prompt, WIDTH),
            suffix_keys.reshape(LOCAL, SUFFIX, WIDTH),
            suffix_values.reshape(LOCAL, SUFFIX, WIDTH),
        )
    ]
    mine = queries.reshape(ROWS, WIDTH)
    found = [exchange(mine, d, 0, 0) for d in AROUND_Z[1:]]
    held = pl.pallas_call(
        copy_kernel,
        out_shape=jax.ShapeDtypeStruct(mine.shape, bf16),
        in_specs=[VMEM],
        out_specs=VMEM,
        compiler_params=PARAMS,
        name="hold",
    )(mine)
    by_z = join(join_z_kernel, [held] + found, info).reshape(CHUNK, WIDTH)
    by_y = gather_y(by_z).reshape(Y * CHUNK, WIDTH)
    first, second = pl.pallas_call(
        attention_kernel,
        out_shape=(shape(jnp.float32, Y), shape(bf16, Y)),
        in_specs=[SMEM] + [VMEM] * 2 + [pl.BlockSpec(memory_space=pltpu.HBM)] * 4,
        out_specs=(VMEM, VMEM),
        scratch_shapes=[
            pltpu.VMEM((total_rows, WIDTH), bf16),
            pltpu.VMEM((prompt, WIDTH), bf16),
            pltpu.VMEM((prompt, 2 * WIDTH), bf16),
            pltpu.VMEM((LOCAL, SUFFIX, WIDTH), bf16),
            pltpu.VMEM((LOCAL, SUFFIX, WIDTH), bf16),
            pltpu.VMEM((2, BLOCK, prompt), jnp.float32),
            pltpu.VMEM((total_rows, WIDTH), jnp.float32),
            pltpu.VMEM((total_rows, WIDTH), jnp.float32),
            pltpu.VMEM((total_rows, WIDTH), jnp.float32),
            pltpu.SemaphoreType.DMA((4,)),
        ],
        compiler_params=PARAMS,
        name="attention",
    )(info, by_y, exchange(by_y, 0, 0, 1), *caches)

    arrived = exchange(second, 0, 0, 1)
    by_dy = pl.pallas_call(
        core_kernel,
        out_shape=(shape(jnp.float32),) + (shape(bf16),) * (Y - 1),
        in_specs=[VMEM] * 2,
        out_specs=(VMEM,) * Y,
        compiler_params=PARAMS,
        name="merge_core",
    )(first, arrived)

    def merge(name, *parts):
        return pl.pallas_call(
            merge_kernel,
            out_shape=(shape(jnp.float32), shape(bf16)),
            in_specs=[VMEM] * len(parts),
            out_specs=(VMEM,) * 2,
            compiler_params=PARAMS,
            name=name,
        )(*parts)

    kept, sent = merge("merge_y", by_dy[0], *[exchange(by_dy[d], 0, d, 0) for d in AROUND_Y])
    kept, sent = merge("merge_z", kept, exchange(sent, 1, 0, 0))
    attention = pl.pallas_call(
        finish_kernel,
        out_shape=jax.ShapeDtypeStruct((Z * LOCAL, HEADS_LOCAL * WIDTH), bf16),
        in_specs=[VMEM] * 2,
        out_specs=VMEM,
        scratch_shapes=[pltpu.VMEM((CHUNK, WIDTH), jnp.float32)],
        compiler_params=PARAMS,
        name="finish",
    )(kept, exchange(sent, 3, 0, 0))

    ours = gather_y(attention)
    theirs = exchange(ours, 0, 0, 1)
    columns_local = out_weight.shape[1]
    terms = pl.pallas_call(
        project_kernel,
        out_shape=jax.ShapeDtypeStruct((SEQ * LOCAL, columns_local), bf16),
        in_specs=[SMEM] + [VMEM] * 3,
        out_specs=VMEM,
        scratch_shapes=[pltpu.VMEM((C * Y, Z * LOCAL, columns_local), jnp.float32)],
        compiler_params=PARAMS,
        name="project",
    )(info, ours, theirs, out_weight.T)
    heads = lax.axis_size("head")
    terms = terms.reshape(heads, SEQ * LOCAL // heads, columns_local)
    swapped = lax.all_to_all(terms, "head", split_axis=0, concat_axis=0, tiled=True)
    return jnp.sum(swapped.astype(jnp.float32), axis=0)


def solution(mesh):
    placed = (
        P("seq", "head", None),
        P("seq", "head", None),
        P("seq", "head", None),
        P("seq", "head", None, None),
        P("seq", "head", None, None),
        P("seq"),
        P(),
        P("head", "seq"),
    )
    return jax.shard_map(
        per_device, mesh=mesh, in_specs=placed, out_specs=P("head", "seq"), check_vma=False
    )
```

time: 109 us -> 86.9 us (0.80)
  local copies, waits for them, and re-layouts: 10.2 us -> 1.47 us
  Pallas kernels: 22.3 us -> 14.7 us
  starting transfers between devices: 33.2 us -> 28.5 us
  waiting for transfers between devices: 26 us -> 29.3 us
  other arithmetic: 4.82 us -> 1.56 us
    unnamed x37 -> x4, local copies, waits for them, and re-layouts: 10.1 us -> 0.74 us
    pallas_call x4 -> x9, Pallas kernels: 19.3 us -> 13.2 us  [the longest x1 10.6 us: per_device(): pl.pallas_call(attention_kernel, out_shape=(shape(jnp.float32, Y), shape(...]
    ppermute x18 -> x17, starting transfers between devices: 33.2 us -> 28.5 us  [exchange(): return lax.ppermute(x, 'seq', pairs)]
    ppermute x18 -> x17, waiting for transfers between devices: 26 us -> 29.3 us  [exchange(): return lax.ppermute(x, 'seq', pairs)]
    another operation x2 -> x0, other arithmetic: 1.5 us -> none  [the longest x1 0.94 us: per_device(): jnp.stack([attention] + [exchange(attention, 0, d, 0) for d in range(1, Y)])]
    pallas_call x1, Pallas kernels: 2.92 us -> 1.48 us  [per_device(): pl.pallas_call(project_kernel, out_shape=jax.ShapeDtypeStruct((SEQ * LOCA...]
  transfers between devices with their start and end apart: 18 -> 17, of which waited for: 15 -> 14; matrix products, arithmetic and copies ran while one was open for 3% -> 2% of each run, Pallas kernels for 0% -> 0%
where the time goes in v2:
time: 86.9 us; the launch traced here: 86.7 us
  waiting for transfers between devices  29.3 us (34%)
  starting transfers between devices  28.5 us (33%)
  Pallas kernels  14.7 us (17%)
  blocking collectives  11.2 us (13%)
  other arithmetic  1.56 us (2%)
  local copies, waits for them, and re-layouts  1.47 us (2%)
    ppermute x17, waiting for transfers between devices, exchange(): return lax.ppermute(x, 'seq', pairs)  29.3 us
    ppermute x17, starting transfers between devices, exchange(): return lax.ppermute(x, 'seq', pairs)  28.5 us
    all_to_all x1, blocking collectives, per_device(): lax.all_to_all(terms, 'head', split_axis=0, concat_axis=0, tiled=True)  11.2 us
    pallas_call x1, Pallas kernels, per_device(): pl.pallas_call(attention_kernel, out_shape=(shape(jnp.float32, Y), shape(...  10.6 us
  transfers between devices with their start and end apart: 17, of which 14 were waited for; matrix products, arithmetic and copies ran while one was open for 2% of the time, Pallas kernels for 0%

profile of v2, /device:TPU:1, one launch (start us, length us, event | category | flops | bytes accessed | tf_op | source)
XLA Modules:
  0.0 86.7 jit_solution(8710115917353993826)
XLA Ops:
  0.0 7.7 %collective-permute-start.2 = (bf16[96,128]{1,0:T(8,128)(2,1)}, bf16[96,128]{1,0:T(8,128)(2,1)S(1)}, u32[]{:S(2)}, u32[]{:S(2)}) collective-permute-start(bf16[96,128]{1,0:T(8,128)(2,1)} %bitcast.20), channel_id=1, source_target_pairs={{0,128},{8,136},{16,144},{24,152},{32,160},{40,168},{48,176},{56,1... | collective-permute-start | bytes 73736 | tf_op jit(solution)/shard_map/ppermute | solution.py:39
  7.7 1.2 %collective-permute-start = (bf16[96,128]{1,0:T(8,128)(2,1)}, bf16[96,128]{1,0:T(8,128)(2,1)S(1)}, u32[]{:S(2)}, u32[]{:S(2)}) collective-permute-start(bf16[96,128]{1,0:T(8,128)(2,1)} %bitcast.22), channel_id=1, source_target_pairs={{0,64},{8,72},{16,80},{24,88},{32,96},{40,104},{48,112},{56,120},{... | collective-permute-start | bytes 73736 | tf_op jit(solution)/shard_map/ppermute | solution.py:39
  8.9 0.9 select_reduce_fusion
  9.9 0.7 copy-done.1
  10.6 0.7 concatenate.3.info_ref
  11.4 1.4 %collective-permute-done.1.refs_2_ = bf16[96,128]{1,0:T(8,128)(2,1)S(1)} collective-permute-done((bf16[96,128]{1,0:T(8,128)(2,1)}, bf16[96,128]{1,0:T(8,128)(2,1)S(1)}, u32[]{:S(2)}, u32[]{:S(2)}) %collective-permute-start.1) | collective-permute-done | bytes 24608 | tf_op jit(solution)/shard_map/ppermute | solution.py:39
  13.3 2.8 %collective-permute-start.5 = (bf16[384,128]{1,0:T(8,128)(2,1)S(1)}, bf16[384,128]{1,0:T(8,128)(2,1)S(1)}, u32[]{:S(2)}, u32[]{:S(2)}) collective-permute-start(bf16[384,128]{1,0:T(8,128)(2,1)S(1)} %bitcast.15), channel_id=1, source_target_pairs={{0,48},{8,56},{16,32},{24,40},{32,16},{40,24},{48,0},{56,8},{64,11... | collective-permute-start | bytes 294920 | tf_op jit(solution)/shard_map/ppermute | solution.py:39
  16.8 1.9 %collective-permute-done.5.refs_3_ = bf16[384,128]{1,0:T(8,128)(2,1)S(1)} collective-permute-done((bf16[384,128]{1,0:T(8,128)(2,1)S(1)}, bf16[384,128]{1,0:T(8,128)(2,1)S(1)}, u32[]{:S(2)}, u32[]{:S(2)}) %collective-permute-start.5) | collective-permute-done | bytes 98336 | tf_op jit(solution)/shard_map/ppermute | solution.py:39
  18.7 2.5 %collective-permute-done.4.refs_2_ = bf16[384,128]{1,0:T(8,128)(2,1)S(1)} collective-permute-done((bf16[384,128]{1,0:T(8,128)(2,1)S(1)}, bf16[384,128]{1,0:T(8,128)(2,1)S(1)}, u32[]{:S(2)}, u32[]{:S(2)}) %collective-permute-start.4) | collective-permute-done | bytes 98336 | tf_op jit(solution)/shard_map/ppermute | solution.py:39
  21.2 3.7 %collective-permute-start.6 = (bf16[1536,128]{1,0:T(8,128)(2,1)S(1)}, bf16[1536,128]{1,0:T(8,128)(2,1)S(1)}, u32[]{:S(2)}, u32[]{:S(2)}) collective-permute-start(bf16[1536,128]{1,0:T(8,128)(2,1)S(1)} %bitcast.12), channel_id=1, source_target_pairs={{0,8},{8,0},{16,24},{24,16},{32,40},{40,32},{48,56},{56,48},{64,72... | collective-permute-start | bytes 1179656 | tf_op jit(solution)/shard_map/ppermute | solution.py:39
  24.9 1.3 %collective-permute-done.6.other_ref = bf16[1536,128]{1,0:T(8,128)(2,1)S(1)} collective-permute-done((bf16[1536,128]{1,0:T(8,128)(2,1)S(1)}, bf16[1536,128]{1,0:T(8,128)(2,1)S(1)}, u32[]{:S(2)}, u32[]{:S(2)}) %collective-permute-start.6) | collective-permute-done | bytes 393248 | tf_op jit(solution)/shard_map/ppermute | solution.py:39
  26.3 10.6 %attention.1 = (f32[4,400,128]{2,1,0:T(8,128)S(1)}, bf16[4,400,128]{2,1,0:T(8,128)(2,1)S(1)}) custom-call(s32[27]{0:T(128)S(1)} %concatenate.3.info_ref, bf16[1536,128]{1,0:T(8,128)(2,1)S(1)} %bitcast.13, bf16[1536,128]{1,0:T(8,128)(2,1)S(1)} %collective-permute-done.6.other_ref, bf16[2048,128]{1,0:T(8,128)(2,1)} %bitcast.26, bf16[2048,128]{1,0:T(8,128)(2,1)} %bitcast.27, ...), custom_call_target="tpu_custom_call" | custom-call | tf_op jit(solution)/shard_map/attention/pallas_call | solution.py:299
  37.4 1.4 %collective-permute-done.7.other_ref = bf16[4,400,128]{2,1,0:T(8,128)(2,1)S(1)} collective-permute-done((bf16[4,400,128]{2,1,0:T(8,128)(2,1)S(1)}, bf16[4,400,128]{2,1,0:T(8,128)(2,1)S(1)}, u32[]{:S(2)}, u32[]{:S(2)}) %collective-permute-start.7) | collective-permute-done | bytes 409632 | tf_op jit(solution)/shard_map/ppermute | solution.py:39
  38.8 0.9 %merge_core.1 = (f32[400,128]{1,0:T(8,128)S(1)}, bf16[400,128]{1,0:T(8,128)(2,1)S(1)}, bf16[400,128]{1,0:T(8,128)(2,1)S(1)}, bf16[400,128]{1,0:T(8,128)(2,1)S(1)}) custom-call(f32[4,400,128]{2,1,0:T(8,128)S(1)} %get-tuple-element.15.mine_ref, bf16[4,400,128]{2,1,0:T(8,128)(2,1)S(1)} %collective-permute-done.7.other_ref), custom_call_target="tpu_custom_call" | custom-call | tf_op jit(solution)/shard_map/merge_core/pallas_call | solution.py:321
  39.6 1.8 %collective-permute-start.8 = (bf16[400,128]{1,0:T(8,128)(2,1)S(1)}, bf16[400,128]{1,0:T(8,128)(2,1)S(1)}, u32[]{:S(2)}, u32[]{:S(2)}) collective-permute-start(bf16[400,128]{1,0:T(8,128)(2,1)S(1)} %get-tuple-element.18), channel_id=1, source_target_pairs={{0,32},{8,40},{16,48},{24,56},{32,0},{40,8},{48,16},{56,24},{64,96... | collective-permute-start | bytes 307208 | tf_op jit(solution)/shard_map/ppermute | solution.py:39
  41.6 1.3 %collective-permute-start.10 = (bf16[400,128]{1,0:T(8,128)(2,1)S(1)}, bf16[400,128]{1,0:T(8,128)(2,1)S(1)}, u32[]{:S(2)}, u32[]{:S(2)}) collective-permute-start(bf16[400,128]{1,0:T(8,128)(2,1)S(1)} %get-tuple-element.20), channel_id=1, source_target_pairs={{0,48},{8,56},{16,32},{24,40},{32,16},{40,24},{48,0},{56,8},{64,11... | collective-permute-start | bytes 307208 | tf_op jit(solution)/shard_map/ppermute | solution.py:39
  43.0 2.3 %collective-permute-done.8.refs_1_ = bf16[400,128]{1,0:T(8,128)(2,1)S(1)} collective-permute-done((bf16[400,128]{1,0:T(8,128)(2,1)S(1)}, bf16[400,128]{1,0:T(8,128)(2,1)S(1)}, u32[]{:S(2)}, u32[]{:S(2)}) %collective-permute-start.8) | collective-permute-done | bytes 102432 | tf_op jit(solution)/shard_map/ppermute | solution.py:39
  45.3 1.1 %collective-permute-done.9.refs_2_ = bf16[400,128]{1,0:T(8,128)(2,1)S(1)} collective-permute-done((bf16[400,128]{1,0:T(8,128)(2,1)S(1)}, bf16[400,128]{1,0:T(8,128)(2,1)S(1)}, u32[]{:S(2)}, u32[]{:S(2)}) %collective-permute-start.9) | collective-permute-done | bytes 102432 | tf_op jit(solution)/shard_map/ppermute | solution.py:39
  46.4 1.2 %collective-permute-done.10.refs_3_ = bf16[400,128]{1,0:T(8,128)(2,1)S(1)} collective-permute-done((bf16[400,128]{1,0:T(8,128)(2,1)S(1)}, bf16[400,128]{1,0:T(8,128)(2,1)S(1)}, u32[]{:S(2)}, u32[]{:S(2)}) %collective-permute-start.10) | collective-permute-done | bytes 102432 | tf_op jit(solution)/shard_map/ppermute | solution.py:39
  48.1 1.3 %collective-permute-start.11 = (bf16[400,128]{1,0:T(8,128)(2,1)S(1)}, bf16[400,128]{1,0:T(8,128)(2,1)S(1)}, u32[]{:S(2)}, u32[]{:S(2)}) collective-permute-start(bf16[400,128]{1,0:T(8,128)(2,1)S(1)} %get-tuple-element.22), channel_id=1, source_target_pairs={{0,64},{8,72},{16,80},{24,88},{32,96},{40,104},{48,112},{56,120},{... | collective-permute-start | bytes 307208 | tf_op jit(solution)/shard_map/ppermute | solution.py:39
  49.4 6.2 %collective-permute-done.11.refs_1_ = bf16[400,128]{1,0:T(8,128)(2,1)S(1)} collective-permute-done((bf16[400,128]{1,0:T(8,128)(2,1)S(1)}, bf16[400,128]{1,0:T(8,128)(2,1)S(1)}, u32[]{:S(2)}, u32[]{:S(2)}) %collective-permute-start.11) | collective-permute-done | bytes 102432 | tf_op jit(solution)/shard_map/ppermute | solution.py:39
  55.9 0.7 collective-permute-start.12
  56.6 5.1 %collective-permute-done.12.other_ref = bf16[400,128]{1,0:T(8,128)(2,1)S(1)} collective-permute-done((bf16[400,128]{1,0:T(8,128)(2,1)S(1)}, bf16[400,128]{1,0:T(8,128)(2,1)S(1)}, u32[]{:S(2)}, u32[]{:S(2)}) %collective-permute-start.12) | collective-permute-done | bytes 102432 | tf_op jit(solution)/shard_map/ppermute | solution.py:39
  62.1 1.4 %collective-permute-start.15 = (bf16[48,1024]{1,0:T(8,128)(2,1)S(1)}, bf16[48,1024]{1,0:T(8,128)(2,1)S(1)}, u32[]{:S(2)}, u32[]{:S(2)}) collective-permute-start(bf16[48,1024]{1,0:T(8,128)(2,1)S(1)} %finish.1.refs_0_), channel_id=1, source_target_pairs={{0,48},{8,56},{16,32},{24,40},{32,16},{40,24},{48,0},{56,8},{64,11... | collective-permute-start | bytes 294920 | tf_op jit(solution)/shard_map/ppermute | solution.py:39
  63.5 1.1 %collective-permute-start.14 = (bf16[48,1024]{1,0:T(8,128)(2,1)S(1)}, bf16[48,1024]{1,0:T(8,128)(2,1)S(1)}, u32[]{:S(2)}, u32[]{:S(2)}) collective-permute-start(bf16[48,1024]{1,0:T(8,128)(2,1)S(1)} %finish.1.refs_0_), channel_id=1, source_target_pairs={{0,32},{8,40},{16,48},{24,56},{32,0},{40,8},{48,16},{56,24},{64,96... | collective-permute-start | bytes 294920 | tf_op jit(solution)/shard_map/ppermute | solution.py:39
  64.6 0.8 collective-permute-start.13
  65.4 1.4 %collective-permute-done.15.refs_3_ = bf16[48,1024]{1,0:T(8,128)(2,1)S(1)} collective-permute-done((bf16[48,1024]{1,0:T(8,128)(2,1)S(1)}, bf16[48,1024]{1,0:T(8,128)(2,1)S(1)}, u32[]{:S(2)}, u32[]{:S(2)}) %collective-permute-start.15) | collective-permute-done | bytes 98336 | tf_op jit(solution)/shard_map/ppermute | solution.py:39
  66.8 1.6 %collective-permute-done.14.refs_2_ = bf16[48,1024]{1,0:T(8,128)(2,1)S(1)} collective-permute-done((bf16[48,1024]{1,0:T(8,128)(2,1)S(1)}, bf16[48,1024]{1,0:T(8,128)(2,1)S(1)}, u32[]{:S(2)}, u32[]{:S(2)}) %collective-permute-start.14) | collective-permute-done | bytes 98336 | tf_op jit(solution)/shard_map/ppermute | solution.py:39
  68.8 3.3 %collective-permute-start.16 = (bf16[4,48,1024]{2,1,0:T(8,128)(2,1)S(1)}, bf16[4,48,1024]{2,1,0:T(8,128)(2,1)S(1)}, u32[]{:S(2)}, u32[]{:S(2)}) collective-permute-start(bf16[4,48,1024]{2,1,0:T(8,128)(2,1)S(1)} %join.5.mine_ref), channel_id=1, source_target_pairs={{0,8},{8,0},{16,24},{24,16},{32,40},{40,32},{48,56},{56,48},{64,72... | collective-permute-start | bytes 1179656 | tf_op jit(solution)/shard_map/ppermute | solution.py:39
  72.1 1.3 %collective-permute-done.16.other_ref = bf16[4,48,1024]{2,1,0:T(8,128)(2,1)S(1)} collective-permute-done((bf16[4,48,1024]{2,1,0:T(8,128)(2,1)S(1)}, bf16[4,48,1024]{2,1,0:T(8,128)(2,1)S(1)}, u32[]{:S(2)}, u32[]{:S(2)}) %collective-permute-start.16) | collective-permute-done | bytes 393248 | tf_op jit(solution)/shard_map/ppermute | solution.py:39
  73.4 1.5 %project.1 = bf16[384,160]{1,0:T(8,128)(2,1)S(1)} custom-call(s32[27]{0:T(128)S(1)} %concatenate.3.info_ref, bf16[4,48,1024]{2,1,0:T(8,128)(2,1)S(1)} %join.5.mine_ref, bf16[4,48,1024]{2,1,0:T(8,128)(2,1)S(1)} %collective-permute-done.16.other_ref, bf16[160,1024]{1,0:T(8,128)(2,1)S(1)} %bitcast.19), custom_call_target="tpu_custom_call" | custom-call | tf_op jit(solution)/shard_map/project/pallas_call | solution.py:355
  74.9 11.2 %all_to_all.5 = bf16[8,48,160]{2,1,0:T(8,128)(2,1)S(1)} all-to-all(bf16[8,48,160]{2,1,0:T(8,128)(2,1)S(1)} %bitcast.14), channel_id=1, replica_groups=mesh['seq'=32,'head'=8] {'head'}, dimensions={0} | all-to-all | bytes 245760 | tf_op jit(solution)/shard_map/all_to_all | solution.py:366
  (22 shorter events, 4.0 us)
Async XLA Ops:
  0.0 11.3 %collective-permute-start.2 = (bf16[96,128]{1,0:T(8,128)(2,1)}, bf16[96,128]{1,0:T(8,128)(2,1)S(1)}, u32[]{:S(2)}, u32[]{:S(2)}) collective-permute-start(bf16[96,128]{1,0:T(8,128)(2,1)} %bitcast.20), channel_id=1, source_target_pairs={{0,128},{8,136},{16,144},{24,152},{32,160},{40,168},{48,176},{56,1... | collective-permute-start | bytes 73736 | tf_op jit(solution)/shard_map/ppermute | solution.py:39
  7.7 5.0 %collective-permute-start.1 = (bf16[96,128]{1,0:T(8,128)(2,1)}, bf16[96,128]{1,0:T(8,128)(2,1)S(1)}, u32[]{:S(2)}, u32[]{:S(2)}) collective-permute-start(bf16[96,128]{1,0:T(8,128)(2,1)} %bitcast.21), channel_id=1, source_target_pairs={{0,192},{8,200},{16,208},{24,216},{32,224},{40,232},{48,240},{56,2... | collective-permute-start | bytes 73736 | tf_op jit(solution)/shard_map/ppermute | solution.py:39
  7.7 5.0 %collective-permute-start = (bf16[96,128]{1,0:T(8,128)(2,1)}, bf16[96,128]{1,0:T(8,128)(2,1)S(1)}, u32[]{:S(2)}, u32[]{:S(2)}) collective-permute-start(bf16[96,128]{1,0:T(8,128)(2,1)} %bitcast.22), channel_id=1, source_target_pairs={{0,64},{8,72},{16,80},{24,88},{32,96},{40,104},{48,112},{56,120},{... | collective-permute-start | bytes 73736 | tf_op jit(solution)/shard_map/ppermute | solution.py:39
  9.9 0.7 copy-start.1
  13.3 5.4 %collective-permute-start.5 = (bf16[384,128]{1,0:T(8,128)(2,1)S(1)}, bf16[384,128]{1,0:T(8,128)(2,1)S(1)}, u32[]{:S(2)}, u32[]{:S(2)}) collective-permute-start(bf16[384,128]{1,0:T(8,128)(2,1)S(1)} %bitcast.15), channel_id=1, source_target_pairs={{0,48},{8,56},{16,32},{24,40},{32,16},{40,24},{48,0},{56,8},{64,11... | collective-permute-start | bytes 294920 | tf_op jit(solution)/shard_map/ppermute | solution.py:39
  16.1 5.1 %collective-permute-start.4 = (bf16[384,128]{1,0:T(8,128)(2,1)S(1)}, bf16[384,128]{1,0:T(8,128)(2,1)S(1)}, u32[]{:S(2)}, u32[]{:S(2)}) collective-permute-start(bf16[384,128]{1,0:T(8,128)(2,1)S(1)} %bitcast.16), channel_id=1, source_target_pairs={{0,32},{8,40},{16,48},{24,56},{32,0},{40,8},{48,16},{56,24},{64,96... | collective-permute-start | bytes 294920 | tf_op jit(solution)/shard_map/ppermute | solution.py:39
  16.5 4.7 %collective-permute-start.3 = (bf16[384,128]{1,0:T(8,128)(2,1)S(1)}, bf16[384,128]{1,0:T(8,128)(2,1)S(1)}, u32[]{:S(2)}, u32[]{:S(2)}) collective-permute-start(bf16[384,128]{1,0:T(8,128)(2,1)S(1)} %bitcast.17), channel_id=1, source_target_pairs={{0,16},{8,24},{16,0},{24,8},{32,48},{40,56},{48,32},{56,40},{64,80... | collective-permute-start | bytes 294920 | tf_op jit(solution)/shard_map/ppermute | solution.py:39
  21.2 5.1 %collective-permute-start.6 = (bf16[1536,128]{1,0:T(8,128)(2,1)S(1)}, bf16[1536,128]{1,0:T(8,128)(2,1)S(1)}, u32[]{:S(2)}, u32[]{:S(2)}) collective-permute-start(bf16[1536,128]{1,0:T(8,128)(2,1)S(1)} %bitcast.12), channel_id=1, source_target_pairs={{0,8},{8,0},{16,24},{24,16},{32,40},{40,32},{48,56},{56,48},{64,72... | collective-permute-start | bytes 1179656 | tf_op jit(solution)/shard_map/ppermute | solution.py:39
  36.9 36.5 %copy-start = (bf16[1024,160]{0,1:T(8,128)(2,1)S(1)}, bf16[1024,160]{0,1:T(8,128)(2,1)}, u32[]{:S(2)}) copy-start(bf16[1024,160]{0,1:T(8,128)(2,1)} %param.15) | copy-start | bytes 983044
  36.9 1.8 %collective-permute-start.7 = (bf16[4,400,128]{2,1,0:T(8,128)(2,1)S(1)}, bf16[4,400,128]{2,1,0:T(8,128)(2,1)S(1)}, u32[]{:S(2)}, u32[]{:S(2)}) collective-permute-start(bf16[4,400,128]{2,1,0:T(8,128)(2,1)S(1)} %get-tuple-element.16), channel_id=1, source_target_pairs={{0,8},{8,0},{16,24},{24,16},{32,40},{40,32},{48,56},{56,48},{64,72... | collective-permute-start | bytes 1228808 | tf_op jit(solution)/shard_map/ppermute | solution.py:39
  39.6 5.7 %collective-permute-start.8 = (bf16[400,128]{1,0:T(8,128)(2,1)S(1)}, bf16[400,128]{1,0:T(8,128)(2,1)S(1)}, u32[]{:S(2)}, u32[]{:S(2)}) collective-permute-start(bf16[400,128]{1,0:T(8,128)(2,1)S(1)} %get-tuple-element.18), channel_id=1, source_target_pairs={{0,32},{8,40},{16,48},{24,56},{32,0},{40,8},{48,16},{56,24},{64,96... | collective-permute-start | bytes 307208 | tf_op jit(solution)/shard_map/ppermute | solution.py:39
  41.5 5.0 %collective-permute-start.9 = (bf16[400,128]{1,0:T(8,128)(2,1)S(1)}, bf16[400,128]{1,0:T(8,128)(2,1)S(1)}, u32[]{:S(2)}, u32[]{:S(2)}) collective-permute-start(bf16[400,128]{1,0:T(8,128)(2,1)S(1)} %get-tuple-element.19), channel_id=1, source_target_pairs={{0,16},{8,24},{16,0},{24,8},{32,48},{40,56},{48,32},{56,40},{64,80... | collective-permute-start | bytes 307208 | tf_op jit(solution)/shard_map/ppermute | solution.py:39
  41.6 6.0 %collective-permute-start.10 = (bf16[400,128]{1,0:T(8,128)(2,1)S(1)}, bf16[400,128]{1,0:T(8,128)(2,1)S(1)}, u32[]{:S(2)}, u32[]{:S(2)}) collective-permute-start(bf16[400,128]{1,0:T(8,128)(2,1)S(1)} %get-tuple-element.20), channel_id=1, source_target_pairs={{0,48},{8,56},{16,32},{24,40},{32,16},{40,24},{48,0},{56,8},{64,11... | collective-permute-start | bytes 307208 | tf_op jit(solution)/shard_map/ppermute | solution.py:39
  48.1 7.5 %collective-permute-start.11 = (bf16[400,128]{1,0:T(8,128)(2,1)S(1)}, bf16[400,128]{1,0:T(8,128)(2,1)S(1)}, u32[]{:S(2)}, u32[]{:S(2)}) collective-permute-start(bf16[400,128]{1,0:T(8,128)(2,1)S(1)} %get-tuple-element.22), channel_id=1, source_target_pairs={{0,64},{8,72},{16,80},{24,88},{32,96},{40,104},{48,112},{56,120},{... | collective-permute-start | bytes 307208 | tf_op jit(solution)/shard_map/ppermute | solution.py:39
  55.9 5.8 %collective-permute-start.12 = (bf16[400,128]{1,0:T(8,128)(2,1)S(1)}, bf16[400,128]{1,0:T(8,128)(2,1)S(1)}, u32[]{:S(2)}, u32[]{:S(2)}) collective-permute-start(bf16[400,128]{1,0:T(8,128)(2,1)S(1)} %get-tuple-element.24), channel_id=1, source_target_pairs={{0,192},{8,200},{16,208},{24,216},{32,224},{40,232},{48,240},{56,2... | collective-permute-start | bytes 307208 | tf_op jit(solution)/shard_map/ppermute | solution.py:39
  62.1 4.8 %collective-permute-start.15 = (bf16[48,1024]{1,0:T(8,128)(2,1)S(1)}, bf16[48,1024]{1,0:T(8,128)(2,1)S(1)}, u32[]{:S(2)}, u32[]{:S(2)}) collective-permute-start(bf16[48,1024]{1,0:T(8,128)(2,1)S(1)} %finish.1.refs_0_), channel_id=1, source_target_pairs={{0,48},{8,56},{16,32},{24,40},{32,16},{40,24},{48,0},{56,8},{64,11... | collective-permute-start | bytes 294920 | tf_op jit(solution)/shard_map/ppermute | solution.py:39
  63.5 5.0 %collective-permute-start.14 = (bf16[48,1024]{1,0:T(8,128)(2,1)S(1)}, bf16[48,1024]{1,0:T(8,128)(2,1)S(1)}, u32[]{:S(2)}, u32[]{:S(2)}) collective-permute-start(bf16[48,1024]{1,0:T(8,128)(2,1)S(1)} %finish.1.refs_0_), channel_id=1, source_target_pairs={{0,32},{8,40},{16,48},{24,56},{32,0},{40,8},{48,16},{56,24},{64,96... | collective-permute-start | bytes 294920 | tf_op jit(solution)/shard_map/ppermute | solution.py:39
  64.6 4.2 %collective-permute-start.13 = (bf16[48,1024]{1,0:T(8,128)(2,1)S(1)}, bf16[48,1024]{1,0:T(8,128)(2,1)S(1)}, u32[]{:S(2)}, u32[]{:S(2)}) collective-permute-start(bf16[48,1024]{1,0:T(8,128)(2,1)S(1)} %finish.1.refs_0_), channel_id=1, source_target_pairs={{0,16},{8,24},{16,0},{24,8},{32,48},{40,56},{48,32},{56,40},{64,80... | collective-permute-start | bytes 294920 | tf_op jit(solution)/shard_map/ppermute | solution.py:39
  68.8 4.6 %collective-permute-start.16 = (bf16[4,48,1024]{2,1,0:T(8,128)(2,1)S(1)}, bf16[4,48,1024]{2,1,0:T(8,128)(2,1)S(1)}, u32[]{:S(2)}, u32[]{:S(2)}) collective-permute-start(bf16[4,48,1024]{2,1,0:T(8,128)(2,1)S(1)} %join.5.mine_ref), channel_id=1, source_target_pairs={{0,8},{8,0},{16,24},{24,16},{32,40},{40,32},{48,56},{56,48},{64,72... | collective-permute-start | bytes 1179656 | tf_op jit(solution)/shard_map/ppermute | solution.py:39

commit v3 on v2

--- a/solution.py
+++ b/solution.py
@@ -19,9 +19,10 @@
 PART = CHUNK + STATS
 TILES = CHUNK // 128
 SUFFIX = 1024
-BLOCK = 256
+BLOCK = 384
 EXPONENT = math.log2(math.e) / math.sqrt(WIDTH)
 DEAD = -1e30
+GROUP = 4
 AROUND_Z = (0, 1, 3, 2)
 AROUND_Y = (2, 1, 3)
 
@@ -44,21 +45,21 @@
         refs[-1][i] = ref[...]
 
 
-def join_z_kernel(info_ref, *refs):
-    z = info_ref[2 * LOCAL]
+def join_z_kernel(*refs):
+    z = lax.axis_index("seq") // (Y * C)
     for offset, ref in zip(AROUND_Z, refs[:-1]):
         refs[-1][z ^ offset] = ref[...]
 
 
-def join(kernel, pieces, *scalars):
+def join(kernel, pieces):
     return pl.pallas_call(
         kernel,
         out_shape=jax.ShapeDtypeStruct((len(pieces), *pieces[0].shape), pieces[0].dtype),
-        in_specs=[SMEM] * len(scalars) + [VMEM] * len(pieces),
+        in_specs=[VMEM] * len(pieces),
         out_specs=VMEM,
         compiler_params=PARAMS,
         name="join",
-    )(*scalars, *pieces)
+    )(*pieces)
 
 
 def gather_y(x):
@@ -74,27 +75,93 @@
     return x.astype(jnp.bfloat16).astype(jnp.float32)
 
 
-def attention_kernel(
-    info_ref,
-    mine_ref,
-    other_ref,
-    keys_hbm,
-    values_hbm,
-    tail_keys_hbm,
-    tail_values_hbm,
-    first_ref,
-    second_ref,
-    queries_ref,
-    keys_ref,
-    wide_ref,
-    tail_k,
-    tail_v,
-    scores,
-    acc,
-    total,
-    top,
-    sem,
-):
+def attend(half, info_in, queries_ref, keys_ref, wide_ref, tail_k, tail_v, part_ref, scores, acc, total, top, chosen, info_ref, sem):
+    copy = pltpu.make_async_copy(info_in, info_ref, sem.at[0])
+    copy.start()
+    nt = (((1,), (1,)), ((), ()))
+    rows_here = Y * CHUNK
+
+    def score(block, slot):
+        q = queries_ref[pl.ds(block * BLOCK, BLOCK), :]
+        scores[slot] = lax.dot_general(q, keys_ref[...], nt, preferred_element_type=jnp.float32)
+
+    def weigh(block, slot):
+        s = scores[slot]
+        c = near(jnp.max(s, axis=1, keepdims=True) * EXPONENT)
+        w = jnp.exp2(s * EXPONENT - c).astype(jnp.bfloat16)
+        o = jnp.dot(w, wide_ref[...], preferred_element_type=jnp.float32)
+        rows = pl.ds(block * BLOCK, BLOCK)
+        acc[rows, :] = o[:, :WIDTH]
+        total[rows, :] = o[:, WIDTH:]
+        top[rows, :] = jnp.broadcast_to(c, (BLOCK, WIDTH))
+
+    blocks = rows_here // BLOCK
+    score(0, 0)
+    for i in range(blocks):
+        if i + 1 < blocks:
+            score(i + 1, (i + 1) % 2)
+        weigh(i, i % 2)
+
+    copy.wait()
+    spare = pl.ds(rows_here, HEADS_LOCAL)
+    for ref in (acc, total, top):
+        ref[spare, :] = jnp.zeros((HEADS_LOCAL, WIDTH), jnp.float32)
+    for k in range(LOCAL + 1):
+        chosen[k] = 0
+    count = jnp.int32(0)
+    for j in range(LOCAL):
+        chosen[count] = j
+        count = count + (info_ref[j] // rows_here == half).astype(jnp.int32)
+    position = lax.broadcasted_iota(jnp.int32, (HEADS_LOCAL, SUFFIX), 1)
+
+    def group(start):
+        spots, tails, slots = [], [], []
+        for k in range(start, start + GROUP):
+            j = chosen[k]
+            spot = jnp.where(k < count, info_ref[j] - half * rows_here, rows_here)
+            row = jnp.where(k < count, spot, 0)
+            base = pl.multiple_of(row // 16 * 16, 16)
+            pair = queries_ref[pl.ds(base, 16), :].astype(jnp.float32)
+            q = jnp.where(row % 16 == 8, pair[8:], pair[:8]).astype(jnp.bfloat16)
+            s = lax.dot_general(q, tail_k[j], nt, preferred_element_type=jnp.float32)
+            tails.append(jnp.where(position < info_ref[LOCAL + j], s * EXPONENT, DEAD))
+            spots.append(spot)
+            slots.append(j)
+        parts = []
+        for j, s in zip(slots, tails):
+            c = near(jnp.max(s, axis=1, keepdims=True))
+            w = jnp.exp2(s - c)
+            t = jnp.sum(w, axis=1, keepdims=True)
+            o = jnp.dot(w.astype(jnp.bfloat16), tail_v[j], preferred_element_type=jnp.float32)
+            parts.append((c, t, o))
+        for spot, (c, t, o) in zip(spots, parts):
+            rows = pl.ds(pl.multiple_of(spot, 8), HEADS_LOCAL)
+            old = top[rows, :]
+            new = jnp.maximum(old, c)
+            f, g = jnp.exp2(old - new), jnp.exp2(c - new)
+            acc[rows, :] = acc[rows, :] * f + o * g
+            total[rows, :] = total[rows, :] * f + t * g
+            top[rows, :] = new
+
+    for start in range(0, LOCAL, GROUP):
+        pl.when(start < count)(functools.partial(group, start))
+
+    lane = lax.broadcasted_iota(jnp.int32, (128, 128), 1)
+    for chunk in range(Y):
+        part = part_ref.at[chunk]
+        stats = []
+        for tile in range(TILES):
+            rows = pl.ds(chunk * CHUNK + tile * 128, 128)
+            part[pl.ds(tile * 128, 128), :] = acc[rows, :].astype(part.dtype)
+            sums = total[rows, :]
+            high = near(sums)
+            mixed = jnp.where(lane == 0, top[rows, :], jnp.where(lane == 1, high, sums - high))
+            stats.append(jnp.transpose(mixed)[:4])
+        stats.append(jnp.zeros((STATS - 4 * TILES, 128), jnp.float32))
+        part[pl.ds(CHUNK, STATS), :] = jnp.concatenate(stats, axis=0).astype(part.dtype)
+
+
+def prepare_kernel(after_ref, keys_hbm, values_hbm, tail_keys_hbm, tail_values_hbm, keys_ref, wide_ref, tail_k, tail_v, sem):
     pairs = [
         (keys_hbm, keys_ref),
         (values_hbm, wide_ref.at[:, pl.ds(0, WIDTH)]),
@@ -105,70 +172,8 @@
     for copy in copies:
         copy.start()
     wide_ref[:, WIDTH:] = jnp.ones_like(wide_ref[:, WIDTH:])
-    queries_ref[: Y * CHUNK] = mine_ref[...]
-    queries_ref[Y * CHUNK :] = other_ref[...]
-    nt = (((1,), (1,)), ((), ()))
-
-    def score(block, slot):
-        q = queries_ref[pl.ds(block * BLOCK, BLOCK), :]
-        scores[slot] = lax.dot_general(q, keys_ref[...], nt, preferred_element_type=jnp.float32)
-
-    def weigh(block, slot):
-        s = scores[slot]
-        c = near(jnp.max(s, axis=1, keepdims=True) * EXPONENT)
-        w = jnp.exp2(s * EXPONENT - c).astype(jnp.bfloat16)
-        o = jnp.dot(w, wide_ref[...], preferred_element_type=jnp.float32)
-        rows = pl.ds(block * BLOCK, BLOCK)
-        acc[rows, :] = o[:, :WIDTH]
-        total[rows, :] = o[:, WIDTH:]
-        top[rows, :] = jnp.broadcast_to(c, (BLOCK, WIDTH))
-
-    blocks = SEQ * ROWS // BLOCK
-    copies[0].wait()
-    score(0, 0)
-    copies[1].wait()
-    for i in range(blocks):
-        if i + 1 < blocks:
-            score(i + 1, (i + 1) % 2)
-        weigh(i, i % 2)
-
-    copies[2].wait()
-    copies[3].wait()
-    position = lax.broadcasted_iota(jnp.int32, (HEADS_LOCAL, SUFFIX), 1)
-    tails = []
-    for j in range(LOCAL):
-        row = info_ref[j]
-        base = pl.multiple_of(row // 16 * 16, 16)
-        pair = queries_ref[pl.ds(base, 16), :].astype(jnp.float32)
-        q = jnp.where(row % 16 == 8, pair[8:], pair[:8]).astype(jnp.bfloat16)
-        s = lax.dot_general(q, tail_k[j], nt, preferred_element_type=jnp.float32)
-        tails.append(jnp.where(position < info_ref[LOCAL + j], s * EXPONENT, DEAD))
-    for j in range(LOCAL):
-        c = near(jnp.max(tails[j], axis=1, keepdims=True))
-        w = jnp.exp2(tails[j] - c)
-        t = jnp.sum(w, axis=1, keepdims=True)
-        o = jnp.dot(w.astype(jnp.bfloat16), tail_v[j], preferred_element_type=jnp.float32)
-        rows = pl.ds(pl.multiple_of(info_ref[j], 8), 8)
-        old = top[rows, :]
-        new = jnp.maximum(old, c)
-        f, g = jnp.exp2(old - new), jnp.exp2(c - new)
-        acc[rows, :] = acc[rows, :] * f + o * g
-        total[rows, :] = total[rows, :] * f + t * g
-        top[rows, :] = new
-
-    lane = lax.broadcasted_iota(jnp.int32, (128, 128), 1)
-    for chunk in range(C * Y):
-        part = (first_ref if chunk < Y else second_ref).at[chunk % Y]
-        stats = []
-        for tile in range(TILES):
-            rows = pl.ds(chunk * CHUNK + tile * 128, 128)
-            part[pl.ds(tile * 128, 128), :] = acc[rows, :].astype(part.dtype)
-            sums = total[rows, :]
-            high = near(sums)
-            mixed = jnp.where(lane == 0, top[rows, :], jnp.where(lane == 1, high, sums - high))
-            stats.append(jnp.transpose(mixed)[:4])
-        stats.append(jnp.zeros((STATS - 4 * TILES, 128), jnp.float32))
-        part[pl.ds(CHUNK, STATS), :] = jnp.concatenate(stats, axis=0).astype(part.dtype)
+    for copy in copies:
+        copy.wait()
 
 
 def columns(rows):
@@ -226,14 +231,15 @@
         out_ref[:, head * WIDTH : (head + 1) * WIDTH] = rows.astype(out_ref.dtype)
 
 
-def project_kernel(info_ref, mine_ref, other_ref, weight_ref, out_ref, terms):
+def project_kernel(mine_ref, other_ref, weight_ref, out_ref, terms):
     weight = weight_ref[...]
     for dc, ref in enumerate((mine_ref, other_ref)):
         for dy in range(Y):
             terms[dc * Y + dy] = lax.dot_general(
                 ref[dy], weight, (((1,), (1,)), ((), ())), preferred_element_type=jnp.float32
             )
-    y, c = info_ref[2 * LOCAL + 1], info_ref[2 * LOCAL + 2]
+    me = lax.axis_index("seq")
+    y, c = me // C % Y, me % C
     for there_y in range(Y):
         for there_c in range(C):
             found = terms[(c ^ there_c) * Y + (y ^ there_y)]
@@ -258,7 +264,6 @@
     out_weight,
 ):
     me = lax.axis_index("seq")
-    z, y, c = me // (Y * C), me // C % Y, me % C
     bf16 = jnp.bfloat16
 
     slots = me * LOCAL + jnp.arange(LOCAL, dtype=jnp.int32)
@@ -267,13 +272,11 @@
     away = (samples // LOCAL) ^ me
     spot = (away % C) * (Y * Z) + (away // C % Y) * Z + samples // (LOCAL * Y * C)
     rows = spot * ROWS + samples % LOCAL * HEADS_LOCAL
-    place = jnp.stack([z, y, c])
-    info = jnp.concatenate([rows, suffix_lengths, place]).astype(jnp.int32)
+    info = jnp.concatenate([rows, suffix_lengths]).astype(jnp.int32)
 
     def shape(dtype, *more):
         return jax.ShapeDtypeStruct((*more, PART, WIDTH), dtype)
 
-    total_rows = SEQ * ROWS
     prompt = prompt_keys.shape[0]
     caches = [
         pltpu.with_memory_space_constraint(x, pltpu.HBM)
@@ -294,30 +297,48 @@
         compiler_params=PARAMS,
         name="hold",
     )(mine)
-    by_z = join(join_z_kernel, [held] + found, info).reshape(CHUNK, WIDTH)
+    by_z = join(join_z_kernel, [held] + found).reshape(CHUNK, WIDTH)
     by_y = gather_y(by_z).reshape(Y * CHUNK, WIDTH)
-    first, second = pl.pallas_call(
-        attention_kernel,
-        out_shape=(shape(jnp.float32, Y), shape(bf16, Y)),
-        in_specs=[SMEM] + [VMEM] * 2 + [pl.BlockSpec(memory_space=pltpu.HBM)] * 4,
-        out_specs=(VMEM, VMEM),
-        scratch_shapes=[
-            pltpu.VMEM((total_rows, WIDTH), bf16),
-            pltpu.VMEM((prompt, WIDTH), bf16),
-            pltpu.VMEM((prompt, 2 * WIDTH), bf16),
-            pltpu.VMEM((LOCAL, SUFFIX, WIDTH), bf16),
-            pltpu.VMEM((LOCAL, SUFFIX, WIDTH), bf16),
-            pltpu.VMEM((2, BLOCK, prompt), jnp.float32),
-            pltpu.VMEM((total_rows, WIDTH), jnp.float32),
-            pltpu.VMEM((total_rows, WIDTH), jnp.float32),
-            pltpu.VMEM((total_rows, WIDTH), jnp.float32),
-            pltpu.SemaphoreType.DMA((4,)),
-        ],
-        compiler_params=PARAMS,
-        name="attention",
-    )(info, by_y, exchange(by_y, 0, 0, 1), *caches)
-
-    arrived = exchange(second, 0, 0, 1)
+    half_rows = Y * CHUNK
+    scratch = [pltpu.VMEM((2, BLOCK, prompt), jnp.float32)]
+    scratch += [pltpu.VMEM((half_rows + HEADS_LOCAL, WIDTH), jnp.float32)] * 3
+    scratch += [pltpu.SMEM((LOCAL + 4,), jnp.int32), pltpu.SMEM((2 * LOCAL,), jnp.int32)]
+    scratch += [pltpu.SemaphoreType.DMA((1,))]
+    cost = pl.CostEstimate(
+        flops=4 * half_rows * prompt * WIDTH, bytes_accessed=2**23, transcendentals=half_rows * prompt
+    )
+    tail = jax.ShapeDtypeStruct((LOCAL, SUFFIX, WIDTH), bf16)
+    by_core = exchange(by_y, 0, 0, 1)
+    held = pl.pallas_call(
+        prepare_kernel,
+        out_shape=(
+            jax.ShapeDtypeStruct((prompt, WIDTH), bf16),
+            jax.ShapeDtypeStruct((prompt, 2 * WIDTH), bf16),
+            tail,
+            tail,
+        ),
+        in_specs=[VMEM] + [pl.BlockSpec(memory_space=pltpu.HBM)] * 4,
+        out_specs=(VMEM,) * 4,
+        scratch_shapes=[pltpu.SemaphoreType.DMA((4,))],
+        compiler_params=PARAMS,
+        cost_estimate=pl.CostEstimate(flops=0, bytes_accessed=2**23, transcendentals=0),
+        name="prepare",
+    )(by_z, *caches)
+
+    def attend_to(half, queries, dtype):
+        return pl.pallas_call(
+            functools.partial(attend, half),
+            out_shape=shape(dtype, Y),
+            in_specs=[pl.BlockSpec(memory_space=pl.ANY)] + [VMEM] * 5,
+            out_specs=VMEM,
+            scratch_shapes=scratch,
+            compiler_params=PARAMS,
+            cost_estimate=cost,
+            name=f"attention_{half}",
+        )(info, queries, *held)
+
+    arrived = exchange(attend_to(0, by_y, bf16), 0, 0, 1)
+    second = attend_to(1, by_core, jnp.float32)
     by_dy = pl.pallas_call(
         core_kernel,
         out_shape=(shape(jnp.float32),) + (shape(bf16),) * (Y - 1),
@@ -325,7 +346,7 @@
         out_specs=(VMEM,) * Y,
         compiler_params=PARAMS,
         name="merge_core",
-    )(first, arrived)
+    )(second, arrived)
 
     def merge(name, *parts):
         return pl.pallas_call(
@@ -355,12 +376,12 @@
     terms = pl.pallas_call(
         project_kernel,
         out_shape=jax.ShapeDtypeStruct((SEQ * LOCAL, columns_local), bf16),
-        in_specs=[SMEM] + [VMEM] * 3,
+        in_specs=[VMEM] * 3,
         out_specs=VMEM,
         scratch_shapes=[pltpu.VMEM((C * Y, Z * LOCAL, columns_local), jnp.float32)],
         compiler_params=PARAMS,
         name="project",
-    )(info, ours, theirs, out_weight.T)
+    )(theirs, ours, out_weight.T)
     heads = lax.axis_size("head")
     terms = terms.reshape(heads, SEQ * LOCAL // heads, columns_local)
     swapped = lax.all_to_all(terms, "head", split_axis=0, concat_axis=0, tiled=True)

time: 86.9 us -> 83.1 us (0.956)
  waiting for transfers between devices: 29.3 us -> 22.2 us
  Pallas kernels: 14.7 us -> 16.3 us
  starting transfers between devices: 28.5 us -> 30.1 us
    ppermute x17, waiting for transfers between devices: 29.3 us -> 22.2 us  [exchange(): return lax.ppermute(x, 'seq', pairs)]
    pallas_call x1 -> x3, Pallas kernels: 10.6 us -> 13.3 us  [the longest x2 10.1 us: attend_to(): pl.pallas_call(functools.partial(attend, half), out_shape=shape(dtype, Y)...]
    ppermute x17, starting transfers between devices: 28.5 us -> 30.1 us  [exchange(): return lax.ppermute(x, 'seq', pairs)]
  transfers between devices with their start and end apart: 17 -> 17, of which waited for: 14 -> 10; matrix products, arithmetic and copies ran while one was open for 2% -> 2% of each run, Pallas kernels for 0% -> 16%
where the time goes in v3:
time: 83.1 us; the launch traced here: 83.2 us
  starting transfers between devices  30.1 us (36%)
  waiting for transfers between devices  22.2 us (27%)
  Pallas kernels  16.3 us (20%)
  blocking collectives  11.5 us (14%)
  other arithmetic  2.29 us (3%)
    ppermute x17, starting transfers between devices, exchange(): return lax.ppermute(x, 'seq', pairs)  30.1 us
    ppermute x17, waiting for transfers between devices, exchange(): return lax.ppermute(x, 'seq', pairs)  22.2 us
    all_to_all x1, blocking collectives, per_device(): lax.all_to_all(terms, 'head', split_axis=0, concat_axis=0, tiled=True)  11.5 us
    pallas_call x2, Pallas kernels, attend_to(): pl.pallas_call(functools.partial(attend, half), out_shape=shape(dtype, Y)...  10.1 us
    pallas_call x1, Pallas kernels, per_device(): pl.pallas_call(prepare_kernel, out_shape=(jax.ShapeDtypeStruct((prompt, W...  3.21 us
  transfers between devices with their start and end apart: 17, of which 10 were waited for; matrix products, arithmetic and copies ran while one was open for 2% of the time, Pallas kernels for 16%

profile of v3, /device:TPU:1, one launch (start us, length us, event | category | flops | bytes accessed | tf_op | source)
XLA Modules:
  0.0 83.2 jit_solution(16145884307174646848)
XLA Ops:
  0.0 7.7 %collective-permute-start.2 = (bf16[96,128]{1,0:T(8,128)(2,1)}, bf16[96,128]{1,0:T(8,128)(2,1)S(1)}, u32[]{:S(2)}, u32[]{:S(2)}) collective-permute-start(bf16[96,128]{1,0:T(8,128)(2,1)} %bitcast.18), channel_id=1, source_target_pairs={{0,128},{8,136},{16,144},{24,152},{32,160},{40,168},{48,176},{56,1... | collective-permute-start | bytes 73736 | tf_op jit(solution)/shard_map/ppermute | solution.py:40
  7.7 1.2 %collective-permute-start = (bf16[96,128]{1,0:T(8,128)(2,1)}, bf16[96,128]{1,0:T(8,128)(2,1)S(1)}, u32[]{:S(2)}, u32[]{:S(2)}) collective-permute-start(bf16[96,128]{1,0:T(8,128)(2,1)} %bitcast.20), channel_id=1, source_target_pairs={{0,64},{8,72},{16,80},{24,88},{32,96},{40,104},{48,112},{56,120},{... | collective-permute-start | bytes 73736 | tf_op jit(solution)/shard_map/ppermute | solution.py:40
  8.9 0.9 %select_reduce_fusion = s32[12]{0:T(128)S(1)} fusion(s32[384]{0:T(512)} %param.14, s32[12]{0:T(128)S(1)} %iota_add_fusion), kind=kLoop, calls=%fused_computation.1 | loop fusion | flops 13812 | bytes 1632 | tf_op jit(solution)/shard_map/reduce_sum | solution.py:271
  9.9 0.7 copy-done.1
  10.6 2.1 %collective-permute-done.1.refs_2_ = bf16[96,128]{1,0:T(8,128)(2,1)S(1)} collective-permute-done((bf16[96,128]{1,0:T(8,128)(2,1)}, bf16[96,128]{1,0:T(8,128)(2,1)S(1)}, u32[]{:S(2)}, u32[]{:S(2)}) %collective-permute-start.1) | collective-permute-done | bytes 24608 | tf_op jit(solution)/shard_map/ppermute | solution.py:40
  12.8 2.8 %collective-permute-start.5 = (bf16[384,128]{1,0:T(8,128)(2,1)S(1)}, bf16[384,128]{1,0:T(8,128)(2,1)S(1)}, u32[]{:S(2)}, u32[]{:S(2)}) collective-permute-start(bf16[384,128]{1,0:T(8,128)(2,1)S(1)} %bitcast.11), channel_id=1, source_target_pairs={{0,48},{8,56},{16,32},{24,40},{32,16},{40,24},{48,0},{56,8},{64,11... | collective-permute-start | bytes 294920 | tf_op jit(solution)/shard_map/ppermute | solution.py:40
  16.3 0.7 pad_add_fusion.info_in
  17.0 3.2 %prepare.1 = (bf16[2048,128]{1,0:T(8,128)(2,1)S(1)}, bf16[2048,256]{1,0:T(8,128)(2,1)S(1)}, bf16[12,1024,128]{2,1,0:T(8,128)(2,1)S(1)}, bf16[12,1024,128]{2,1,0:T(8,128)(2,1)S(1)}) custom-call(bf16[384,128]{1,0:T(8,128)(2,1)S(1)} %bitcast.14, bf16[2048,128]{1,0:T(8,128)(2,1)} %bitcast.24, bf16[2048,128]{1,0:T(8,128)(2,1)} %bitcast.25, ...), custom_call_target="tpu_custom_call" | custom-call | bytes 8388608 | tf_op jit(solution)/shard_map/prepare/pallas_call | solution.py:312
  20.2 0.4 collective-permute-done.4.refs_2_
  20.7 3.5 %collective-permute-start.6 = (bf16[1536,128]{1,0:T(8,128)(2,1)S(1)}, bf16[1536,128]{1,0:T(8,128)(2,1)S(1)}, u32[]{:S(2)}, u32[]{:S(2)}) collective-permute-start(bf16[1536,128]{1,0:T(8,128)(2,1)S(1)} %bitcast.9), channel_id=1, source_target_pairs={{0,8},{8,0},{16,24},{24,16},{32,40},{40,32},{48,56},{56,48},{64,72... | collective-permute-start | bytes 1179656 | tf_op jit(solution)/shard_map/ppermute | solution.py:40
  24.2 4.7 %attention_0.1 = bf16[4,400,128]{2,1,0:T(8,128)(2,1)S(1)} custom-call(s32[24]{0:T(128)S(1)} %pad_add_fusion.info_in, bf16[1536,128]{1,0:T(8,128)(2,1)S(1)} %bitcast.10, bf16[2048,128]{1,0:T(8,128)(2,1)S(1)} %get-tuple-element.17.keys_ref, bf16[2048,256]{1,0:T(8,128)(2,1)S(1)} %get-tuple-element.18.wide_ref, ...), custom_call_target="tpu_custom_call" | custom-call | flops 1610612736 | bytes 8388608 | tf_op jit(solution)/shard_map/attention_0/pallas_call | solution.py:329
  29.2 5.4 %attention_1.1.mine_ref = f32[4,400,128]{2,1,0:T(8,128)S(1)} custom-call(s32[24]{0:T(128)S(1)} %pad_add_fusion.info_in, bf16[1536,128]{1,0:T(8,128)(2,1)S(1)} %collective-permute-done.6.queries_ref, bf16[2048,128]{1,0:T(8,128)(2,1)S(1)} %get-tuple-element.17.keys_ref, bf16[2048,256]{1,0:T(8,128)(2,1)S(1)} %get-tuple-element.18.wide_ref, ...), custom_call_target="tpu_custom_call" | custom-call | flops 1610612736 | bytes 8388608 | tf_op jit(solution)/shard_map/attention_1/pallas_call | solution.py:329
  34.6 0.9 %merge_core.1 = (f32[400,128]{1,0:T(8,128)S(1)}, bf16[400,128]{1,0:T(8,128)(2,1)S(1)}, bf16[400,128]{1,0:T(8,128)(2,1)S(1)}, bf16[400,128]{1,0:T(8,128)(2,1)S(1)}) custom-call(f32[4,400,128]{2,1,0:T(8,128)S(1)} %attention_1.1.mine_ref, bf16[4,400,128]{2,1,0:T(8,128)(2,1)S(1)} %collective-permute-done.7.other_ref), custom_call_target="tpu_custom_call" | custom-call | tf_op jit(solution)/shard_map/merge_core/pallas_call | solution.py:342
  35.5 2.6 %collective-permute-start.8 = (bf16[400,128]{1,0:T(8,128)(2,1)S(1)}, bf16[400,128]{1,0:T(8,128)(2,1)S(1)}, u32[]{:S(2)}, u32[]{:S(2)}) collective-permute-start(bf16[400,128]{1,0:T(8,128)(2,1)S(1)} %get-tuple-element.22), channel_id=1, source_target_pairs={{0,32},{8,40},{16,48},{24,56},{32,0},{40,8},{48,16},{56,24},{64,96... | collective-permute-start | bytes 307208 | tf_op jit(solution)/shard_map/ppermute | solution.py:40
  38.1 0.4 collective-permute-start.9
  38.8 1.8 %collective-permute-done.8.refs_1_ = bf16[400,128]{1,0:T(8,128)(2,1)S(1)} collective-permute-done((bf16[400,128]{1,0:T(8,128)(2,1)S(1)}, bf16[400,128]{1,0:T(8,128)(2,1)S(1)}, u32[]{:S(2)}, u32[]{:S(2)}) %collective-permute-start.8) | collective-permute-done | bytes 102432 | tf_op jit(solution)/shard_map/ppermute | solution.py:40
  40.6 2.5 %collective-permute-done.9.refs_2_ = bf16[400,128]{1,0:T(8,128)(2,1)S(1)} collective-permute-done((bf16[400,128]{1,0:T(8,128)(2,1)S(1)}, bf16[400,128]{1,0:T(8,128)(2,1)S(1)}, u32[]{:S(2)}, u32[]{:S(2)}) %collective-permute-start.9) | collective-permute-done | bytes 102432 | tf_op jit(solution)/shard_map/ppermute | solution.py:40
  43.2 1.0 %collective-permute-done.10.refs_3_ = bf16[400,128]{1,0:T(8,128)(2,1)S(1)} collective-permute-done((bf16[400,128]{1,0:T(8,128)(2,1)S(1)}, bf16[400,128]{1,0:T(8,128)(2,1)S(1)}, u32[]{:S(2)}, u32[]{:S(2)}) %collective-permute-start.10) | collective-permute-done | bytes 102432 | tf_op jit(solution)/shard_map/ppermute | solution.py:40
  44.2 0.4 merge_y.1
  44.6 2.0 %collective-permute-start.11 = (bf16[400,128]{1,0:T(8,128)(2,1)S(1)}, bf16[400,128]{1,0:T(8,128)(2,1)S(1)}, u32[]{:S(2)}, u32[]{:S(2)}) collective-permute-start(bf16[400,128]{1,0:T(8,128)(2,1)S(1)} %get-tuple-element.26), channel_id=1, source_target_pairs={{0,64},{8,72},{16,80},{24,88},{32,96},{40,104},{48,112},{56,120},{... | collective-permute-start | bytes 307208 | tf_op jit(solution)/shard_map/ppermute | solution.py:40
  46.6 5.3 %collective-permute-done.11.refs_1_ = bf16[400,128]{1,0:T(8,128)(2,1)S(1)} collective-permute-done((bf16[400,128]{1,0:T(8,128)(2,1)S(1)}, bf16[400,128]{1,0:T(8,128)(2,1)S(1)}, u32[]{:S(2)}, u32[]{:S(2)}) %collective-permute-start.11) | collective-permute-done | bytes 102432 | tf_op jit(solution)/shard_map/ppermute | solution.py:40
  52.2 1.6 %collective-permute-start.12 = (bf16[400,128]{1,0:T(8,128)(2,1)S(1)}, bf16[400,128]{1,0:T(8,128)(2,1)S(1)}, u32[]{:S(2)}, u32[]{:S(2)}) collective-permute-start(bf16[400,128]{1,0:T(8,128)(2,1)S(1)} %get-tuple-element.28), channel_id=1, source_target_pairs={{0,192},{8,200},{16,208},{24,216},{32,224},{40,232},{48,240},{56,2... | collective-permute-start | bytes 307208 | tf_op jit(solution)/shard_map/ppermute | solution.py:40
  53.8 4.3 %collective-permute-done.12.other_ref = bf16[400,128]{1,0:T(8,128)(2,1)S(1)} collective-permute-done((bf16[400,128]{1,0:T(8,128)(2,1)S(1)}, bf16[400,128]{1,0:T(8,128)(2,1)S(1)}, u32[]{:S(2)}, u32[]{:S(2)}) %collective-permute-start.12) | collective-permute-done | bytes 102432 | tf_op jit(solution)/shard_map/ppermute | solution.py:40
  58.4 1.7 %collective-permute-start.15 = (bf16[48,1024]{1,0:T(8,128)(2,1)S(1)}, bf16[48,1024]{1,0:T(8,128)(2,1)S(1)}, u32[]{:S(2)}, u32[]{:S(2)}) collective-permute-start(bf16[48,1024]{1,0:T(8,128)(2,1)S(1)} %finish.1.refs_0_), channel_id=1, source_target_pairs={{0,48},{8,56},{16,32},{24,40},{32,16},{40,24},{48,0},{56,8},{64,11... | collective-permute-start | bytes 294920 | tf_op jit(solution)/shard_map/ppermute | solution.py:40
  60.4 1.3 %collective-permute-start.13 = (bf16[48,1024]{1,0:T(8,128)(2,1)S(1)}, bf16[48,1024]{1,0:T(8,128)(2,1)S(1)}, u32[]{:S(2)}, u32[]{:S(2)}) collective-permute-start(bf16[48,1024]{1,0:T(8,128)(2,1)S(1)} %finish.1.refs_0_), channel_id=1, source_target_pairs={{0,16},{8,24},{16,0},{24,8},{32,48},{40,56},{48,32},{56,40},{64,80... | collective-permute-start | bytes 294920 | tf_op jit(solution)/shard_map/ppermute | solution.py:40
  61.7 1.4 %collective-permute-done.15.refs_3_ = bf16[48,1024]{1,0:T(8,128)(2,1)S(1)} collective-permute-done((bf16[48,1024]{1,0:T(8,128)(2,1)S(1)}, bf16[48,1024]{1,0:T(8,128)(2,1)S(1)}, u32[]{:S(2)}, u32[]{:S(2)}) %collective-permute-start.15) | collective-permute-done | bytes 98336 | tf_op jit(solution)/shard_map/ppermute | solution.py:40
  63.1 2.0 %collective-permute-done.14.refs_2_ = bf16[48,1024]{1,0:T(8,128)(2,1)S(1)} collective-permute-done((bf16[48,1024]{1,0:T(8,128)(2,1)S(1)}, bf16[48,1024]{1,0:T(8,128)(2,1)S(1)}, u32[]{:S(2)}, u32[]{:S(2)}) %collective-permute-start.14) | collective-permute-done | bytes 98336 | tf_op jit(solution)/shard_map/ppermute | solution.py:40
  65.1 3.6 %collective-permute-start.16 = (bf16[4,48,1024]{2,1,0:T(8,128)(2,1)S(1)}, bf16[4,48,1024]{2,1,0:T(8,128)(2,1)S(1)}, u32[]{:S(2)}, u32[]{:S(2)}) collective-permute-start(bf16[4,48,1024]{2,1,0:T(8,128)(2,1)S(1)} %join.5.other_ref), channel_id=1, source_target_pairs={{0,8},{8,0},{16,24},{24,16},{32,40},{40,32},{48,56},{56,48},{64,72... | collective-permute-start | bytes 1179656 | tf_op jit(solution)/shard_map/ppermute | solution.py:40
  68.7 1.3 %collective-permute-done.16.mine_ref = bf16[4,48,1024]{2,1,0:T(8,128)(2,1)S(1)} collective-permute-done((bf16[4,48,1024]{2,1,0:T(8,128)(2,1)S(1)}, bf16[4,48,1024]{2,1,0:T(8,128)(2,1)S(1)}, u32[]{:S(2)}, u32[]{:S(2)}) %collective-permute-start.16) | collective-permute-done | bytes 393248 | tf_op jit(solution)/shard_map/ppermute | solution.py:40
  70.1 0.9 %project.1 = bf16[384,160]{1,0:T(8,128)(2,1)S(1)} custom-call(bf16[4,48,1024]{2,1,0:T(8,128)(2,1)S(1)} %collective-permute-done.16.mine_ref, bf16[4,48,1024]{2,1,0:T(8,128)(2,1)S(1)} %join.5.other_ref, bf16[160,1024]{1,0:T(8,128)(2,1)S(1)} %bitcast.17), custom_call_target="tpu_custom_call" | custom-call | tf_op jit(solution)/shard_map/project/pallas_call | solution.py:376
  71.0 11.5 %all_to_all.5 = bf16[8,48,160]{2,1,0:T(8,128)(2,1)S(1)} all-to-all(bf16[8,48,160]{2,1,0:T(8,128)(2,1)S(1)} %bitcast.16), channel_id=1, replica_groups=mesh['seq'=32,'head'=8] {'head'}, dimensions={0} | all-to-all | bytes 245760 | tf_op jit(solution)/shard_map/all_to_all | solution.py:387
  82.5 0.7 convert_reduce_fusion
  (24 shorter events, 2.5 us)
Async XLA Ops:
  0.0 10.6 %collective-permute-start.2 = (bf16[96,128]{1,0:T(8,128)(2,1)}, bf16[96,128]{1,0:T(8,128)(2,1)S(1)}, u32[]{:S(2)}, u32[]{:S(2)}) collective-permute-start(bf16[96,128]{1,0:T(8,128)(2,1)} %bitcast.18), channel_id=1, source_target_pairs={{0,128},{8,136},{16,144},{24,152},{32,160},{40,168},{48,176},{56,1... | collective-permute-start | bytes 73736 | tf_op jit(solution)/shard_map/ppermute | solution.py:40
  7.7 5.0 %collective-permute-start.1 = (bf16[96,128]{1,0:T(8,128)(2,1)}, bf16[96,128]{1,0:T(8,128)(2,1)S(1)}, u32[]{:S(2)}, u32[]{:S(2)}) collective-permute-start(bf16[96,128]{1,0:T(8,128)(2,1)} %bitcast.19), channel_id=1, source_target_pairs={{0,192},{8,200},{16,208},{24,216},{32,224},{40,232},{48,240},{56,2... | collective-permute-start | bytes 73736 | tf_op jit(solution)/shard_map/ppermute | solution.py:40
  7.7 5.0 %collective-permute-start = (bf16[96,128]{1,0:T(8,128)(2,1)}, bf16[96,128]{1,0:T(8,128)(2,1)S(1)}, u32[]{:S(2)}, u32[]{:S(2)}) collective-permute-start(bf16[96,128]{1,0:T(8,128)(2,1)} %bitcast.20), channel_id=1, source_target_pairs={{0,64},{8,72},{16,80},{24,88},{32,96},{40,104},{48,112},{56,120},{... | collective-permute-start | bytes 73736 | tf_op jit(solution)/shard_map/ppermute | solution.py:40
  9.8 0.7 copy-start.1
  12.8 7.5 %collective-permute-start.5 = (bf16[384,128]{1,0:T(8,128)(2,1)S(1)}, bf16[384,128]{1,0:T(8,128)(2,1)S(1)}, u32[]{:S(2)}, u32[]{:S(2)}) collective-permute-start(bf16[384,128]{1,0:T(8,128)(2,1)S(1)} %bitcast.11), channel_id=1, source_target_pairs={{0,48},{8,56},{16,32},{24,40},{32,16},{40,24},{48,0},{56,8},{64,11... | collective-permute-start | bytes 294920 | tf_op jit(solution)/shard_map/ppermute | solution.py:40
  15.6 5.1 %collective-permute-start.4 = (bf16[384,128]{1,0:T(8,128)(2,1)S(1)}, bf16[384,128]{1,0:T(8,128)(2,1)S(1)}, u32[]{:S(2)}, u32[]{:S(2)}) collective-permute-start(bf16[384,128]{1,0:T(8,128)(2,1)S(1)} %bitcast.12), channel_id=1, source_target_pairs={{0,32},{8,40},{16,48},{24,56},{32,0},{40,8},{48,16},{56,24},{64,96... | collective-permute-start | bytes 294920 | tf_op jit(solution)/shard_map/ppermute | solution.py:40
  15.9 4.7 %collective-permute-start.3 = (bf16[384,128]{1,0:T(8,128)(2,1)S(1)}, bf16[384,128]{1,0:T(8,128)(2,1)S(1)}, u32[]{:S(2)}, u32[]{:S(2)}) collective-permute-start(bf16[384,128]{1,0:T(8,128)(2,1)S(1)} %bitcast.13), channel_id=1, source_target_pairs={{0,16},{8,24},{16,0},{24,8},{32,48},{40,56},{48,32},{56,40},{64,80... | collective-permute-start | bytes 294920 | tf_op jit(solution)/shard_map/ppermute | solution.py:40
  20.7 8.5 %collective-permute-start.6 = (bf16[1536,128]{1,0:T(8,128)(2,1)S(1)}, bf16[1536,128]{1,0:T(8,128)(2,1)S(1)}, u32[]{:S(2)}, u32[]{:S(2)}) collective-permute-start(bf16[1536,128]{1,0:T(8,128)(2,1)S(1)} %bitcast.9), channel_id=1, source_target_pairs={{0,8},{8,0},{16,24},{24,16},{32,40},{40,32},{48,56},{56,48},{64,72... | collective-permute-start | bytes 1179656 | tf_op jit(solution)/shard_map/ppermute | solution.py:40
  28.9 5.7 %collective-permute-start.7 = (bf16[4,400,128]{2,1,0:T(8,128)(2,1)S(1)}, bf16[4,400,128]{2,1,0:T(8,128)(2,1)S(1)}, u32[]{:S(2)}, u32[]{:S(2)}) collective-permute-start(bf16[4,400,128]{2,1,0:T(8,128)(2,1)S(1)} %attention_0.1), channel_id=1, source_target_pairs={{0,8},{8,0},{16,24},{24,16},{32,40},{40,32},{48,56},{56,48},{64,72... | collective-permute-start | bytes 1228808 | tf_op jit(solution)/shard_map/ppermute | solution.py:40
  34.6 35.5 %copy-start = (bf16[1024,160]{0,1:T(8,128)(2,1)S(1)}, bf16[1024,160]{0,1:T(8,128)(2,1)}, u32[]{:S(2)}) copy-start(bf16[1024,160]{0,1:T(8,128)(2,1)} %param.15) | copy-start | bytes 983044
  35.5 5.1 %collective-permute-start.8 = (bf16[400,128]{1,0:T(8,128)(2,1)S(1)}, bf16[400,128]{1,0:T(8,128)(2,1)S(1)}, u32[]{:S(2)}, u32[]{:S(2)}) collective-permute-start(bf16[400,128]{1,0:T(8,128)(2,1)S(1)} %get-tuple-element.22), channel_id=1, source_target_pairs={{0,32},{8,40},{16,48},{24,56},{32,0},{40,8},{48,16},{56,24},{64,96... | collective-permute-start | bytes 307208 | tf_op jit(solution)/shard_map/ppermute | solution.py:40
  38.1 5.1 %collective-permute-start.9 = (bf16[400,128]{1,0:T(8,128)(2,1)S(1)}, bf16[400,128]{1,0:T(8,128)(2,1)S(1)}, u32[]{:S(2)}, u32[]{:S(2)}) collective-permute-start(bf16[400,128]{1,0:T(8,128)(2,1)S(1)} %get-tuple-element.23), channel_id=1, source_target_pairs={{0,16},{8,24},{16,0},{24,8},{32,48},{40,56},{48,32},{56,40},{64,80... | collective-permute-start | bytes 307208 | tf_op jit(solution)/shard_map/ppermute | solution.py:40
  38.5 5.7 %collective-permute-start.10 = (bf16[400,128]{1,0:T(8,128)(2,1)S(1)}, bf16[400,128]{1,0:T(8,128)(2,1)S(1)}, u32[]{:S(2)}, u32[]{:S(2)}) collective-permute-start(bf16[400,128]{1,0:T(8,128)(2,1)S(1)} %get-tuple-element.24), channel_id=1, source_target_pairs={{0,48},{8,56},{16,32},{24,40},{32,16},{40,24},{48,0},{56,8},{64,11... | collective-permute-start | bytes 307208 | tf_op jit(solution)/shard_map/ppermute | solution.py:40
  44.6 7.3 %collective-permute-start.11 = (bf16[400,128]{1,0:T(8,128)(2,1)S(1)}, bf16[400,128]{1,0:T(8,128)(2,1)S(1)}, u32[]{:S(2)}, u32[]{:S(2)}) collective-permute-start(bf16[400,128]{1,0:T(8,128)(2,1)S(1)} %get-tuple-element.26), channel_id=1, source_target_pairs={{0,64},{8,72},{16,80},{24,88},{32,96},{40,104},{48,112},{56,120},{... | collective-permute-start | bytes 307208 | tf_op jit(solution)/shard_map/ppermute | solution.py:40
  52.2 5.8 %collective-permute-start.12 = (bf16[400,128]{1,0:T(8,128)(2,1)S(1)}, bf16[400,128]{1,0:T(8,128)(2,1)S(1)}, u32[]{:S(2)}, u32[]{:S(2)}) collective-permute-start(bf16[400,128]{1,0:T(8,128)(2,1)S(1)} %get-tuple-element.28), channel_id=1, source_target_pairs={{0,192},{8,200},{16,208},{24,216},{32,224},{40,232},{48,240},{56,2... | collective-permute-start | bytes 307208 | tf_op jit(solution)/shard_map/ppermute | solution.py:40
  58.4 4.8 %collective-permute-start.15 = (bf16[48,1024]{1,0:T(8,128)(2,1)S(1)}, bf16[48,1024]{1,0:T(8,128)(2,1)S(1)}, u32[]{:S(2)}, u32[]{:S(2)}) collective-permute-start(bf16[48,1024]{1,0:T(8,128)(2,1)S(1)} %finish.1.refs_0_), channel_id=1, source_target_pairs={{0,48},{8,56},{16,32},{24,40},{32,16},{40,24},{48,0},{56,8},{64,11... | collective-permute-start | bytes 294920 | tf_op jit(solution)/shard_map/ppermute | solution.py:40
  60.1 5.0 %collective-permute-start.14 = (bf16[48,1024]{1,0:T(8,128)(2,1)S(1)}, bf16[48,1024]{1,0:T(8,128)(2,1)S(1)}, u32[]{:S(2)}, u32[]{:S(2)}) collective-permute-start(bf16[48,1024]{1,0:T(8,128)(2,1)S(1)} %finish.1.refs_0_), channel_id=1, source_target_pairs={{0,32},{8,40},{16,48},{24,56},{32,0},{40,8},{48,16},{56,24},{64,96... | collective-permute-start | bytes 294920 | tf_op jit(solution)/shard_map/ppermute | solution.py:40
  60.4 4.7 %collective-permute-start.13 = (bf16[48,1024]{1,0:T(8,128)(2,1)S(1)}, bf16[48,1024]{1,0:T(8,128)(2,1)S(1)}, u32[]{:S(2)}, u32[]{:S(2)}) collective-permute-start(bf16[48,1024]{1,0:T(8,128)(2,1)S(1)} %finish.1.refs_0_), channel_id=1, source_target_pairs={{0,16},{8,24},{16,0},{24,8},{32,48},{40,56},{48,32},{56,40},{64,80... | collective-permute-start | bytes 294920 | tf_op jit(solution)/shard_map/ppermute | solution.py:40
  65.1 4.9 %collective-permute-start.16 = (bf16[4,48,1024]{2,1,0:T(8,128)(2,1)S(1)}, bf16[4,48,1024]{2,1,0:T(8,128)(2,1)S(1)}, u32[]{:S(2)}, u32[]{:S(2)}) collective-permute-start(bf16[4,48,1024]{2,1,0:T(8,128)(2,1)S(1)} %join.5.other_ref), channel_id=1, source_target_pairs={{0,8},{8,0},{16,24},{24,16},{32,40},{40,32},{48,56},{56,48},{64,72... | collective-permute-start | bytes 1179656 | tf_op jit(solution)/shard_map/ppermute | solution.py:40

commit v4 on v3

--- a/solution.py
+++ b/solution.py
@@ -19,9 +19,9 @@
 PART = CHUNK + STATS
 TILES = CHUNK // 128
 SUFFIX = 1024
-BLOCK = 384
 EXPONENT = math.log2(math.e) / math.sqrt(WIDTH)
 DEAD = -1e30
+NT = (((1,), (1,)), ((), ()))
 GROUP = 4
 AROUND_Z = (0, 1, 3, 2)
 AROUND_Y = (2, 1, 3)
@@ -75,37 +75,41 @@
     return x.astype(jnp.bfloat16).astype(jnp.float32)
 
 
-def attend(half, info_in, queries_ref, keys_ref, wide_ref, tail_k, tail_v, part_ref, scores, acc, total, top, chosen, info_ref, sem):
-    copy = pltpu.make_async_copy(info_in, info_ref, sem.at[0])
-    copy.start()
-    nt = (((1,), (1,)), ((), ()))
-    rows_here = Y * CHUNK
-
-    def score(block, slot):
-        q = queries_ref[pl.ds(block * BLOCK, BLOCK), :]
-        scores[slot] = lax.dot_general(q, keys_ref[...], nt, preferred_element_type=jnp.float32)
-
-    def weigh(block, slot):
-        s = scores[slot]
+def prefix(queries_ref, places, keys_ref, wide_ref, scores, put):
+    def score(i):
+        q = queries_ref[pl.ds(places[i], CHUNK), :]
+        scores[i % 2] = lax.dot_general(q, keys_ref[...], NT, preferred_element_type=jnp.float32)
+
+    score(0)
+    for i in range(len(places)):
+        if i + 1 < len(places):
+            score(i + 1)
+        s = scores[i % 2]
         c = near(jnp.max(s, axis=1, keepdims=True) * EXPONENT)
         w = jnp.exp2(s * EXPONENT - c).astype(jnp.bfloat16)
         o = jnp.dot(w, wide_ref[...], preferred_element_type=jnp.float32)
-        rows = pl.ds(block * BLOCK, BLOCK)
-        acc[rows, :] = o[:, :WIDTH]
-        total[rows, :] = o[:, WIDTH:]
-        top[rows, :] = jnp.broadcast_to(c, (BLOCK, WIDTH))
-
-    blocks = rows_here // BLOCK
-    score(0, 0)
-    for i in range(blocks):
-        if i + 1 < blocks:
-            score(i + 1, (i + 1) % 2)
-        weigh(i, i % 2)
-
-    copy.wait()
-    spare = pl.ds(rows_here, HEADS_LOCAL)
-    for ref in (acc, total, top):
-        ref[spare, :] = jnp.zeros((HEADS_LOCAL, WIDTH), jnp.float32)
+        put(i, (o[:, :WIDTH], o[:, WIDTH:], jnp.broadcast_to(c, (CHUNK, WIDTH))))
+
+
+def emit(part_ref, acc, total, top, start):
+    lane = lax.broadcasted_iota(jnp.int32, (128, 128), 1)
+    stats = []
+    for tile in range(TILES):
+        rows = pl.ds(start + tile * 128, 128)
+        part_ref[pl.ds(tile * 128, 128), :] = acc[rows, :].astype(part_ref.dtype)
+        sums = total[rows, :]
+        high = near(sums)
+        mixed = jnp.where(lane == 0, top[rows, :], jnp.where(lane == 1, high, sums - high))
+        stats.append(jnp.transpose(mixed)[:4])
+    stats.append(jnp.zeros((STATS - 4 * TILES, 128), jnp.float32))
+    part_ref[pl.ds(CHUNK, STATS), :] = jnp.concatenate(stats, axis=0).astype(part_ref.dtype)
+
+
+def add_suffixes(half, queries_ref, tail_k, tail_v, state, chosen, info_ref):
+    acc, total, top = state
+    rows_here = Y * CHUNK
+    for ref in state:
+        ref[pl.ds(rows_here, HEADS_LOCAL), :] = jnp.zeros((HEADS_LOCAL, WIDTH), jnp.float32)
     for k in range(LOCAL + 1):
         chosen[k] = 0
     count = jnp.int32(0)
@@ -123,7 +127,7 @@
             base = pl.multiple_of(row // 16 * 16, 16)
             pair = queries_ref[pl.ds(base, 16), :].astype(jnp.float32)
             q = jnp.where(row % 16 == 8, pair[8:], pair[:8]).astype(jnp.bfloat16)
-            s = lax.dot_general(q, tail_k[j], nt, preferred_element_type=jnp.float32)
+            s = lax.dot_general(q, tail_k[j], NT, preferred_element_type=jnp.float32)
             tails.append(jnp.where(position < info_ref[LOCAL + j], s * EXPONENT, DEAD))
             spots.append(spot)
             slots.append(j)
@@ -146,32 +150,70 @@
     for start in range(0, LOCAL, GROUP):
         pl.when(start < count)(functools.partial(group, start))
 
-    lane = lax.broadcasted_iota(jnp.int32, (128, 128), 1)
-    for chunk in range(Y):
-        part = part_ref.at[chunk]
-        stats = []
-        for tile in range(TILES):
-            rows = pl.ds(chunk * CHUNK + tile * 128, 128)
-            part[pl.ds(tile * 128, 128), :] = acc[rows, :].astype(part.dtype)
-            sums = total[rows, :]
-            high = near(sums)
-            mixed = jnp.where(lane == 0, top[rows, :], jnp.where(lane == 1, high, sums - high))
-            stats.append(jnp.transpose(mixed)[:4])
-        stats.append(jnp.zeros((STATS - 4 * TILES, 128), jnp.float32))
-        part[pl.ds(CHUNK, STATS), :] = jnp.concatenate(stats, axis=0).astype(part.dtype)
-
-
-def prepare_kernel(after_ref, keys_hbm, values_hbm, tail_keys_hbm, tail_values_hbm, keys_ref, wide_ref, tail_k, tail_v, sem):
-    pairs = [
-        (keys_hbm, keys_ref),
-        (values_hbm, wide_ref.at[:, pl.ds(0, WIDTH)]),
-        (tail_keys_hbm, tail_k),
-        (tail_values_hbm, tail_v),
+
+def own_kernel(queries_ref, keys_ref, wide_ref, acc, total, top, scores):
+    def put(_, found):
+        for ref, value in zip((acc, total, top), found):
+            ref[...] = value
+
+    prefix(queries_ref, [0], keys_ref, wide_ref, scores, put)
+
+
+def first_kernel(info_in, queries_ref, keys_ref, wide_ref, tail_k, tail_v, *refs):
+    begun, part_ref, scores, state, (chosen, info_ref, sem) = refs[:3], refs[3], refs[4], refs[5:8], refs[8:]
+    copy = pltpu.make_async_copy(info_in, info_ref, sem.at[0])
+    copy.start()
+    for ref, old in zip(state, begun):
+        ref[:CHUNK, :] = old[...]
+    places = [CHUNK, 2 * CHUNK, 3 * CHUNK]
+
+    def put(i, found):
+        for ref, value in zip(state, found):
+            ref[pl.ds(places[i], CHUNK), :] = value
+
+    prefix(queries_ref, places, keys_ref, wide_ref, scores, put)
+    copy.wait()
+    add_suffixes(0, queries_ref, tail_k, tail_v, state, chosen, info_ref)
+    for dy in range(Y):
+        emit(part_ref.at[dy], *state, dy * CHUNK)
+
+
+def second_kernel(info_in, queries_ref, keys_ref, wide_ref, tail_k, tail_v, part_ref, scores, *refs):
+    state, (chosen, info_ref, sem) = refs[:3], refs[3:]
+    copy = pltpu.make_async_copy(info_in, info_ref, sem.at[0])
+    copy.start()
+    places = [dy * CHUNK for dy in range(Y)]
+
+    def put(i, found):
+        for ref, value in zip(state, found):
+            ref[pl.ds(places[i], CHUNK), :] = value
+
+    prefix(queries_ref, places, keys_ref, wide_ref, scores, put)
+    copy.wait()
+    add_suffixes(1, queries_ref, tail_k, tail_v, state, chosen, info_ref)
+    for dy in range(Y):
+        emit(part_ref.at[dy], *state, dy * CHUNK)
+
+
+def prepare_kernel(keys_hbm, values_hbm, keys_ref, wide_ref, sem):
+    copies = [
+        pltpu.make_async_copy(keys_hbm, keys_ref, sem.at[0]),
+        pltpu.make_async_copy(values_hbm, wide_ref.at[:, pl.ds(0, WIDTH)], sem.at[1]),
     ]
-    copies = [pltpu.make_async_copy(a, b, sem.at[i]) for i, (a, b) in enumerate(pairs)]
     for copy in copies:
         copy.start()
     wide_ref[:, WIDTH:] = jnp.ones_like(wide_ref[:, WIDTH:])
+    for copy in copies:
+        copy.wait()
+
+
+def fetch_kernel(after_ref, tail_keys_hbm, tail_values_hbm, tail_k, tail_v, sem):
+    copies = [
+        pltpu.make_async_copy(tail_keys_hbm, tail_k, sem.at[0]),
+        pltpu.make_async_copy(tail_values_hbm, tail_v, sem.at[1]),
+    ]
+    for copy in copies:
+        copy.start()
     for copy in copies:
         copy.wait()
 
@@ -299,54 +341,52 @@
     )(mine)
     by_z = join(join_z_kernel, [held] + found).reshape(CHUNK, WIDTH)
     by_y = gather_y(by_z).reshape(Y * CHUNK, WIDTH)
-    half_rows = Y * CHUNK
-    scratch = [pltpu.VMEM((2, BLOCK, prompt), jnp.float32)]
-    scratch += [pltpu.VMEM((half_rows + HEADS_LOCAL, WIDTH), jnp.float32)] * 3
-    scratch += [pltpu.SMEM((LOCAL + 4,), jnp.int32), pltpu.SMEM((2 * LOCAL,), jnp.int32)]
-    scratch += [pltpu.SemaphoreType.DMA((1,))]
-    cost = pl.CostEstimate(
-        flops=4 * half_rows * prompt * WIDTH, bytes_accessed=2**23, transcendentals=half_rows * prompt
+    def call(kernel, name, out, ins, *operands, scratch=(), chunks=0):
+        return pl.pallas_call(
+            kernel,
+            out_shape=out,
+            in_specs=ins + [VMEM] * (len(operands) - len(ins)),
+            out_specs=jax.tree.map(lambda _: VMEM, out),
+            scratch_shapes=list(scratch),
+            compiler_params=PARAMS,
+            cost_estimate=pl.CostEstimate(
+                flops=4 * chunks * CHUNK * prompt * WIDTH,
+                bytes_accessed=2**22,
+                transcendentals=chunks * CHUNK * prompt,
+            ),
+            name=name,
+        )(*operands)
+
+    anywhere = [pl.BlockSpec(memory_space=pl.ANY)]
+    hbm = pl.BlockSpec(memory_space=pltpu.HBM)
+    two = [pltpu.SemaphoreType.DMA((2,))]
+    scores = [pltpu.VMEM((2, CHUNK, prompt), jnp.float32)]
+    state = [pltpu.VMEM((Y * CHUNK + HEADS_LOCAL, WIDTH), jnp.float32)] * 3
+    lists = [pltpu.SMEM((LOCAL + 4,), jnp.int32), pltpu.SMEM((2 * LOCAL,), jnp.int32)]
+    lists += [pltpu.SemaphoreType.DMA((1,))]
+    rows_of = [jax.ShapeDtypeStruct((CHUNK, WIDTH), jnp.float32)] * 3
+    tail = jax.ShapeDtypeStruct((LOCAL, SUFFIX, WIDTH), bf16)
+    prompt_shapes = [
+        jax.ShapeDtypeStruct((prompt, WIDTH), bf16),
+        jax.ShapeDtypeStruct((prompt, 2 * WIDTH), bf16),
+    ]
+    keys, wide = call(prepare_kernel, "prepare", prompt_shapes, [hbm] * 2, *caches[:2], scratch=two)
+    begun = call(own_kernel, "attention_own", rows_of, [], by_z, keys, wide, scratch=scores, chunks=1)
+    tails = call(fetch_kernel, "fetch", [tail, tail], [VMEM, hbm, hbm], begun[0], *caches[2:], scratch=two)
+
+    by_core = exchange(by_y, 0, 0, 1)
+    first = call(
+        first_kernel, "attention_first", shape(bf16, Y), anywhere, info, by_y, keys, wide, *tails, *begun,
+        scratch=scores + state + lists, chunks=3,
     )
-    tail = jax.ShapeDtypeStruct((LOCAL, SUFFIX, WIDTH), bf16)
-    by_core = exchange(by_y, 0, 0, 1)
-    held = pl.pallas_call(
-        prepare_kernel,
-        out_shape=(
-            jax.ShapeDtypeStruct((prompt, WIDTH), bf16),
-            jax.ShapeDtypeStruct((prompt, 2 * WIDTH), bf16),
-            tail,
-            tail,
-        ),
-        in_specs=[VMEM] + [pl.BlockSpec(memory_space=pltpu.HBM)] * 4,
-        out_specs=(VMEM,) * 4,
-        scratch_shapes=[pltpu.SemaphoreType.DMA((4,))],
-        compiler_params=PARAMS,
-        cost_estimate=pl.CostEstimate(flops=0, bytes_accessed=2**23, transcendentals=0),
-        name="prepare",
-    )(by_z, *caches)
-
-    def attend_to(half, queries, dtype):
-        return pl.pallas_call(
-            functools.partial(attend, half),
-            out_shape=shape(dtype, Y),
-            in_specs=[pl.BlockSpec(memory_space=pl.ANY)] + [VMEM] * 5,
-            out_specs=VMEM,
-            scratch_shapes=scratch,
-            compiler_params=PARAMS,
-            cost_estimate=cost,
-            name=f"attention_{half}",
-        )(info, queries, *held)
-
-    arrived = exchange(attend_to(0, by_y, bf16), 0, 0, 1)
-    second = attend_to(1, by_core, jnp.float32)
-    by_dy = pl.pallas_call(
-        core_kernel,
-        out_shape=(shape(jnp.float32),) + (shape(bf16),) * (Y - 1),
-        in_specs=[VMEM] * 2,
-        out_specs=(VMEM,) * Y,
-        compiler_params=PARAMS,
-        name="merge_core",
-    )(second, arrived)
+    arrived = exchange(first, 0, 0, 1)
+    second = call(
+        second_kernel, "attention_second", shape(jnp.float32, Y), anywhere,
+        info, by_core, keys, wide, *tails, scratch=scores + state + lists, chunks=4,
+    )
+    by_dy = call(
+        core_kernel, "merge_core", [shape(jnp.float32)] + [shape(bf16)] * (Y - 1), [], second, arrived
+    )
 
     def merge(name, *parts):
         return pl.pallas_call(

time: 83.1 us -> 89.6 us (1.078)
  waiting for transfers between devices: 22.2 us -> 27.6 us
  Pallas kernels: 16.3 us -> 18.7 us
  blocking collectives: 11.5 us -> 9.74 us
    ppermute x17, waiting for transfers between devices: 22.2 us -> 27.6 us  [exchange(): return lax.ppermute(x, 'seq', pairs)]
    pallas_call x4 -> x6, Pallas kernels: 14.2 us -> 16.6 us  [call(): pl.pallas_call(kernel, out_shape=out, in_specs=ins + [VMEM] * (len(operan...]
    all_to_all x1, blocking collectives: 11.5 us -> 9.74 us  [per_device(): lax.all_to_all(terms, 'head', split_axis=0, concat_axis=0, tiled=True)]
  transfers between devices with their start and end apart: 17 -> 17, of which waited for: 10 -> 10; matrix products, arithmetic and copies ran while one was open for 2% -> 2% of each run, Pallas kernels for 16% -> 18%
where the time goes in v4:
time: 89.6 us; the launch traced here: 89.3 us
  starting transfers between devices  30.1 us (34%)
  waiting for transfers between devices  27.6 us (31%)
  Pallas kernels  18.7 us (21%)
  blocking collectives  9.74 us (11%)
  other arithmetic  2.29 us (3%)
    ppermute x17, starting transfers between devices, exchange(): return lax.ppermute(x, 'seq', pairs)  30.1 us
    ppermute x17, waiting for transfers between devices, exchange(): return lax.ppermute(x, 'seq', pairs)  27.6 us
    pallas_call x6, Pallas kernels, call(): pl.pallas_call(kernel, out_shape=out, in_specs=ins + [VMEM] * (len(operan...  16.6 us
    all_to_all x1, blocking collectives, per_device(): lax.all_to_all(terms, 'head', split_axis=0, concat_axis=0, tiled=True)  9.74 us
  transfers between devices with their start and end apart: 17, of which 10 were waited for; matrix products, arithmetic and copies ran while one was open for 2% of the time, Pallas kernels for 18%

profile of v4, /device:TPU:1, one launch (start us, length us, event | category | flops | bytes accessed | tf_op | source)
XLA Modules:
  0.0 89.3 jit_solution(17753073090205307470)
XLA Ops:
  0.0 3.8 %collective-permute-start = (bf16[96,128]{1,0:T(8,128)(2,1)}, bf16[96,128]{1,0:T(8,128)(2,1)S(1)}, u32[]{:S(2)}, u32[]{:S(2)}) collective-permute-start(bf16[96,128]{1,0:T(8,128)(2,1)} %bitcast.18), channel_id=1, source_target_pairs={{0,64},{8,72},{16,80},{24,88},{32,96},{40,104},{48,112},{56,120},{... | collective-permute-start | bytes 73736 | tf_op jit(solution)/shard_map/ppermute | solution.py:40
  3.8 4.2 %collective-permute-start.1 = (bf16[96,128]{1,0:T(8,128)(2,1)}, bf16[96,128]{1,0:T(8,128)(2,1)S(1)}, u32[]{:S(2)}, u32[]{:S(2)}) collective-permute-start(bf16[96,128]{1,0:T(8,128)(2,1)} %bitcast.19), channel_id=1, source_target_pairs={{0,192},{8,200},{16,208},{24,216},{32,224},{40,232},{48,240},{56,2... | collective-permute-start | bytes 73736 | tf_op jit(solution)/shard_map/ppermute | solution.py:40
  8.0 0.9 %collective-permute-start.2 = (bf16[96,128]{1,0:T(8,128)(2,1)}, bf16[96,128]{1,0:T(8,128)(2,1)S(1)}, u32[]{:S(2)}, u32[]{:S(2)}) collective-permute-start(bf16[96,128]{1,0:T(8,128)(2,1)} %bitcast.20), channel_id=1, source_target_pairs={{0,128},{8,136},{16,144},{24,152},{32,160},{40,168},{48,176},{56,1... | collective-permute-start | bytes 73736 | tf_op jit(solution)/shard_map/ppermute | solution.py:40
  8.9 0.9 select_reduce_fusion
  9.9 0.7 copy-done.1
  10.6 1.2 %prepare.1 = (bf16[2048,128]{1,0:T(8,128)(2,1)S(1)}, bf16[2048,256]{1,0:T(8,128)(2,1)S(1)}) custom-call(bf16[2048,128]{1,0:T(8,128)(2,1)} %bitcast.24, bf16[2048,128]{1,0:T(8,128)(2,1)} %bitcast.25), custom_call_target="tpu_custom_call" | custom-call | bytes 4194304 | tf_op jit(solution)/shard_map/prepare/pallas_call | solution.py:345
  11.8 3.2 %collective-permute-done.2.refs_3_ = bf16[96,128]{1,0:T(8,128)(2,1)S(1)} collective-permute-done((bf16[96,128]{1,0:T(8,128)(2,1)}, bf16[96,128]{1,0:T(8,128)(2,1)S(1)}, u32[]{:S(2)}, u32[]{:S(2)}) %collective-permute-start.2) | collective-permute-done | bytes 24608 | tf_op jit(solution)/shard_map/ppermute | solution.py:40
  15.1 1.4 %collective-permute-start.3 = (bf16[384,128]{1,0:T(8,128)(2,1)S(1)}, bf16[384,128]{1,0:T(8,128)(2,1)S(1)}, u32[]{:S(2)}, u32[]{:S(2)}) collective-permute-start(bf16[384,128]{1,0:T(8,128)(2,1)S(1)} %bitcast.11), channel_id=1, source_target_pairs={{0,16},{8,24},{16,0},{24,8},{32,48},{40,56},{48,32},{56,40},{64,80... | collective-permute-start | bytes 294920 | tf_op jit(solution)/shard_map/ppermute | solution.py:40
  16.5 2.6 %collective-permute-start.4 = (bf16[384,128]{1,0:T(8,128)(2,1)S(1)}, bf16[384,128]{1,0:T(8,128)(2,1)S(1)}, u32[]{:S(2)}, u32[]{:S(2)}) collective-permute-start(bf16[384,128]{1,0:T(8,128)(2,1)S(1)} %bitcast.12), channel_id=1, source_target_pairs={{0,32},{8,40},{16,48},{24,56},{32,0},{40,8},{48,16},{56,24},{64,96... | collective-permute-start | bytes 294920 | tf_op jit(solution)/shard_map/ppermute | solution.py:40
  19.1 0.7 pad_add_fusion.info_in
  19.8 2.3 %collective-permute-done.4.refs_2_ = bf16[384,128]{1,0:T(8,128)(2,1)S(1)} collective-permute-done((bf16[384,128]{1,0:T(8,128)(2,1)S(1)}, bf16[384,128]{1,0:T(8,128)(2,1)S(1)}, u32[]{:S(2)}, u32[]{:S(2)}) %collective-permute-start.4) | collective-permute-done | bytes 98336 | tf_op jit(solution)/shard_map/ppermute | solution.py:40
  22.1 1.9 %collective-permute-done.5.refs_3_ = bf16[384,128]{1,0:T(8,128)(2,1)S(1)} collective-permute-done((bf16[384,128]{1,0:T(8,128)(2,1)S(1)}, bf16[384,128]{1,0:T(8,128)(2,1)S(1)}, u32[]{:S(2)}, u32[]{:S(2)}) %collective-permute-start.5) | collective-permute-done | bytes 98336 | tf_op jit(solution)/shard_map/ppermute | solution.py:40
  24.1 3.6 %collective-permute-start.6 = (bf16[1536,128]{1,0:T(8,128)(2,1)S(1)}, bf16[1536,128]{1,0:T(8,128)(2,1)S(1)}, u32[]{:S(2)}, u32[]{:S(2)}) collective-permute-start(bf16[1536,128]{1,0:T(8,128)(2,1)S(1)} %bitcast.9), channel_id=1, source_target_pairs={{0,8},{8,0},{16,24},{24,16},{32,40},{40,32},{48,56},{56,48},{64,72... | collective-permute-start | bytes 1179656 | tf_op jit(solution)/shard_map/ppermute | solution.py:40
  27.7 1.9 %attention_own.1 = (f32[384,128]{1,0:T(8,128)S(1)}, f32[384,128]{1,0:T(8,128)S(1)}, f32[384,128]{1,0:T(8,128)S(1)}) custom-call(bf16[384,128]{1,0:T(8,128)(2,1)S(1)} %bitcast.15, bf16[2048,128]{1,0:T(8,128)(2,1)S(1)} %get-tuple-element.20.keys_ref, bf16[2048,256]{1,0:T(8,128)(2,1)S(1)} %get-tuple-element.21.wide_ref), custom_call_target="tpu_custom_call" | custom-call | flops 402653184 | bytes 4194304 | tf_op jit(solution)/shard_map/attention_own/pallas_call | solution.py:345
  29.6 2.9 %fetch.1 = (bf16[12,1024,128]{2,1,0:T(8,128)(2,1)S(1)}, bf16[12,1024,128]{2,1,0:T(8,128)(2,1)S(1)}) custom-call(f32[384,128]{1,0:T(8,128)S(1)} %get-tuple-element.22.after_ref.refs_0_, bf16[12,1024,128]{2,1,0:T(8,128)(2,1)} %bitcast.22, bf16[12,1024,128]{2,1,0:T(8,128)(2,1)} %bitcast.23), custom_call_target="tpu_custom_call" | custom-call | bytes 4194304 | tf_op jit(solution)/shard_map/fetch/pallas_call | solution.py:345
  32.5 4.3 %attention_first.1 = bf16[4,400,128]{2,1,0:T(8,128)(2,1)S(1)} custom-call(s32[24]{0:T(128)S(1)} %pad_add_fusion.info_in, bf16[1536,128]{1,0:T(8,128)(2,1)S(1)} %bitcast.10, bf16[2048,128]{1,0:T(8,128)(2,1)S(1)} %get-tuple-element.20.keys_ref, bf16[2048,256]{1,0:T(8,128)(2,1)S(1)} %get-tuple-element.21.wide_ref, ...), custom_call_target="tpu_custom_call" | custom-call | flops 1207959552 | bytes 4194304 | tf_op jit(solution)/shard_map/attention_first/pallas_call | solution.py:345
  37.1 5.4 %attention_second.1.mine_ref = f32[4,400,128]{2,1,0:T(8,128)S(1)} custom-call(s32[24]{0:T(128)S(1)} %pad_add_fusion.info_in, bf16[1536,128]{1,0:T(8,128)(2,1)S(1)} %collective-permute-done.6.queries_ref, bf16[2048,128]{1,0:T(8,128)(2,1)S(1)} %get-tuple-element.20.keys_ref, bf16[2048,256]{1,0:T(8,128)(2,1)S(1)} %get-tuple-element.21.wide_ref, ...), custom_call_target="tpu_custom_call" | custom-call | flops 1610612736 | bytes 4194304 | tf_op jit(solution)/shard_map/attention_second/pallas_call | solution.py:345
  42.6 0.9 merge_core.1
  43.9 0.6 collective-permute-start.8
  44.5 2.3 %collective-permute-start.9 = (bf16[400,128]{1,0:T(8,128)(2,1)S(1)}, bf16[400,128]{1,0:T(8,128)(2,1)S(1)}, u32[]{:S(2)}, u32[]{:S(2)}) collective-permute-start(bf16[400,128]{1,0:T(8,128)(2,1)S(1)} %get-tuple-element.29), channel_id=1, source_target_pairs={{0,16},{8,24},{16,0},{24,8},{32,48},{40,56},{48,32},{56,40},{64,80... | collective-permute-start | bytes 307208 | tf_op jit(solution)/shard_map/ppermute | solution.py:40
  46.8 3.9 %collective-permute-done.10.refs_3_ = bf16[400,128]{1,0:T(8,128)(2,1)S(1)} collective-permute-done((bf16[400,128]{1,0:T(8,128)(2,1)S(1)}, bf16[400,128]{1,0:T(8,128)(2,1)S(1)}, u32[]{:S(2)}, u32[]{:S(2)}) %collective-permute-start.10) | collective-permute-done | bytes 102432 | tf_op jit(solution)/shard_map/ppermute | solution.py:40
  51.6 1.3 %collective-permute-start.11 = (bf16[400,128]{1,0:T(8,128)(2,1)S(1)}, bf16[400,128]{1,0:T(8,128)(2,1)S(1)}, u32[]{:S(2)}, u32[]{:S(2)}) collective-permute-start(bf16[400,128]{1,0:T(8,128)(2,1)S(1)} %get-tuple-element.32), channel_id=1, source_target_pairs={{0,64},{8,72},{16,80},{24,88},{32,96},{40,104},{48,112},{56,120},{... | collective-permute-start | bytes 307208 | tf_op jit(solution)/shard_map/ppermute | solution.py:40
  52.9 4.6 %collective-permute-done.11.refs_1_ = bf16[400,128]{1,0:T(8,128)(2,1)S(1)} collective-permute-done((bf16[400,128]{1,0:T(8,128)(2,1)S(1)}, bf16[400,128]{1,0:T(8,128)(2,1)S(1)}, u32[]{:S(2)}, u32[]{:S(2)}) %collective-permute-start.11) | collective-permute-done | bytes 102432 | tf_op jit(solution)/shard_map/ppermute | solution.py:40
  57.9 5.6 %collective-permute-done.12.other_ref = bf16[400,128]{1,0:T(8,128)(2,1)S(1)} collective-permute-done((bf16[400,128]{1,0:T(8,128)(2,1)S(1)}, bf16[400,128]{1,0:T(8,128)(2,1)S(1)}, u32[]{:S(2)}, u32[]{:S(2)}) %collective-permute-start.12) | collective-permute-done | bytes 102432 | tf_op jit(solution)/shard_map/ppermute | solution.py:40
  64.0 3.3 %collective-permute-start.14 = (bf16[48,1024]{1,0:T(8,128)(2,1)S(1)}, bf16[48,1024]{1,0:T(8,128)(2,1)S(1)}, u32[]{:S(2)}, u32[]{:S(2)}) collective-permute-start(bf16[48,1024]{1,0:T(8,128)(2,1)S(1)} %finish.1.refs_0_), channel_id=1, source_target_pairs={{0,32},{8,40},{16,48},{24,56},{32,0},{40,8},{48,16},{56,24},{64,96... | collective-permute-start | bytes 294920 | tf_op jit(solution)/shard_map/ppermute | solution.py:40
  67.8 2.4 %collective-permute-done.14.refs_2_ = bf16[48,1024]{1,0:T(8,128)(2,1)S(1)} collective-permute-done((bf16[48,1024]{1,0:T(8,128)(2,1)S(1)}, bf16[48,1024]{1,0:T(8,128)(2,1)S(1)}, u32[]{:S(2)}, u32[]{:S(2)}) %collective-permute-start.14) | collective-permute-done | bytes 98336 | tf_op jit(solution)/shard_map/ppermute | solution.py:40
  70.3 1.7 %collective-permute-done.15.refs_3_ = bf16[48,1024]{1,0:T(8,128)(2,1)S(1)} collective-permute-done((bf16[48,1024]{1,0:T(8,128)(2,1)S(1)}, bf16[48,1024]{1,0:T(8,128)(2,1)S(1)}, u32[]{:S(2)}, u32[]{:S(2)}) %collective-permute-start.15) | collective-permute-done | bytes 98336 | tf_op jit(solution)/shard_map/ppermute | solution.py:40
  72.0 4.6 %collective-permute-start.16 = (bf16[4,48,1024]{2,1,0:T(8,128)(2,1)S(1)}, bf16[4,48,1024]{2,1,0:T(8,128)(2,1)S(1)}, u32[]{:S(2)}, u32[]{:S(2)}) collective-permute-start(bf16[4,48,1024]{2,1,0:T(8,128)(2,1)S(1)} %join.5.other_ref), channel_id=1, source_target_pairs={{0,8},{8,0},{16,24},{24,16},{32,40},{40,32},{48,56},{56,48},{64,72... | collective-permute-start | bytes 1179656 | tf_op jit(solution)/shard_map/ppermute | solution.py:40
  76.6 1.3 %collective-permute-done.16.mine_ref = bf16[4,48,1024]{2,1,0:T(8,128)(2,1)S(1)} collective-permute-done((bf16[4,48,1024]{2,1,0:T(8,128)(2,1)S(1)}, bf16[4,48,1024]{2,1,0:T(8,128)(2,1)S(1)}, u32[]{:S(2)}, u32[]{:S(2)}) %collective-permute-start.16) | collective-permute-done | bytes 393248 | tf_op jit(solution)/shard_map/ppermute | solution.py:40
  78.0 0.9 %project.1 = bf16[384,160]{1,0:T(8,128)(2,1)S(1)} custom-call(bf16[4,48,1024]{2,1,0:T(8,128)(2,1)S(1)} %collective-permute-done.16.mine_ref, bf16[4,48,1024]{2,1,0:T(8,128)(2,1)S(1)} %join.5.other_ref, bf16[160,1024]{1,0:T(8,128)(2,1)S(1)} %bitcast.17), custom_call_target="tpu_custom_call" | custom-call | tf_op jit(solution)/shard_map/project/pallas_call | solution.py:416
  78.9 9.7 %all_to_all.5 = bf16[8,48,160]{2,1,0:T(8,128)(2,1)S(1)} all-to-all(bf16[8,48,160]{2,1,0:T(8,128)(2,1)S(1)} %bitcast.16), channel_id=1, replica_groups=mesh['seq'=32,'head'=8] {'head'}, dimensions={0} | all-to-all | bytes 245760 | tf_op jit(solution)/shard_map/all_to_all | solution.py:427
  88.7 0.7 convert_reduce_fusion
  (26 shorter events, 3.2 us)
Async XLA Ops:
  0.0 11.8 %collective-permute-start = (bf16[96,128]{1,0:T(8,128)(2,1)}, bf16[96,128]{1,0:T(8,128)(2,1)S(1)}, u32[]{:S(2)}, u32[]{:S(2)}) collective-permute-start(bf16[96,128]{1,0:T(8,128)(2,1)} %bitcast.18), channel_id=1, source_target_pairs={{0,64},{8,72},{16,80},{24,88},{32,96},{40,104},{48,112},{56,120},{... | collective-permute-start | bytes 73736 | tf_op jit(solution)/shard_map/ppermute | solution.py:40
  3.8 8.0 %collective-permute-start.1 = (bf16[96,128]{1,0:T(8,128)(2,1)}, bf16[96,128]{1,0:T(8,128)(2,1)S(1)}, u32[]{:S(2)}, u32[]{:S(2)}) collective-permute-start(bf16[96,128]{1,0:T(8,128)(2,1)} %bitcast.19), channel_id=1, source_target_pairs={{0,192},{8,200},{16,208},{24,216},{32,224},{40,232},{48,240},{56,2... | collective-permute-start | bytes 73736 | tf_op jit(solution)/shard_map/ppermute | solution.py:40
  8.0 7.0 %collective-permute-start.2 = (bf16[96,128]{1,0:T(8,128)(2,1)}, bf16[96,128]{1,0:T(8,128)(2,1)S(1)}, u32[]{:S(2)}, u32[]{:S(2)}) collective-permute-start(bf16[96,128]{1,0:T(8,128)(2,1)} %bitcast.20), channel_id=1, source_target_pairs={{0,128},{8,136},{16,144},{24,152},{32,160},{40,168},{48,176},{56,1... | collective-permute-start | bytes 73736 | tf_op jit(solution)/shard_map/ppermute | solution.py:40
  9.8 0.7 copy-start.1
  15.1 4.7 %collective-permute-start.3 = (bf16[384,128]{1,0:T(8,128)(2,1)S(1)}, bf16[384,128]{1,0:T(8,128)(2,1)S(1)}, u32[]{:S(2)}, u32[]{:S(2)}) collective-permute-start(bf16[384,128]{1,0:T(8,128)(2,1)S(1)} %bitcast.11), channel_id=1, source_target_pairs={{0,16},{8,24},{16,0},{24,8},{32,48},{40,56},{48,32},{56,40},{64,80... | collective-permute-start | bytes 294920 | tf_op jit(solution)/shard_map/ppermute | solution.py:40
  16.5 5.7 %collective-permute-start.4 = (bf16[384,128]{1,0:T(8,128)(2,1)S(1)}, bf16[384,128]{1,0:T(8,128)(2,1)S(1)}, u32[]{:S(2)}, u32[]{:S(2)}) collective-permute-start(bf16[384,128]{1,0:T(8,128)(2,1)S(1)} %bitcast.12), channel_id=1, source_target_pairs={{0,32},{8,40},{16,48},{24,56},{32,0},{40,8},{48,16},{56,24},{64,96... | collective-permute-start | bytes 294920 | tf_op jit(solution)/shard_map/ppermute | solution.py:40
  19.1 5.0 %collective-permute-start.5 = (bf16[384,128]{1,0:T(8,128)(2,1)S(1)}, bf16[384,128]{1,0:T(8,128)(2,1)S(1)}, u32[]{:S(2)}, u32[]{:S(2)}) collective-permute-start(bf16[384,128]{1,0:T(8,128)(2,1)S(1)} %bitcast.13), channel_id=1, source_target_pairs={{0,48},{8,56},{16,32},{24,40},{32,16},{40,24},{48,0},{56,8},{64,11... | collective-permute-start | bytes 294920 | tf_op jit(solution)/shard_map/ppermute | solution.py:40
  24.1 13.0 %collective-permute-start.6 = (bf16[1536,128]{1,0:T(8,128)(2,1)S(1)}, bf16[1536,128]{1,0:T(8,128)(2,1)S(1)}, u32[]{:S(2)}, u32[]{:S(2)}) collective-permute-start(bf16[1536,128]{1,0:T(8,128)(2,1)S(1)} %bitcast.9), channel_id=1, source_target_pairs={{0,8},{8,0},{16,24},{24,16},{32,40},{40,32},{48,56},{56,48},{64,72... | collective-permute-start | bytes 1179656 | tf_op jit(solution)/shard_map/ppermute | solution.py:40
  36.8 5.8 %collective-permute-start.7 = (bf16[4,400,128]{2,1,0:T(8,128)(2,1)S(1)}, bf16[4,400,128]{2,1,0:T(8,128)(2,1)S(1)}, u32[]{:S(2)}, u32[]{:S(2)}) collective-permute-start(bf16[4,400,128]{2,1,0:T(8,128)(2,1)S(1)} %attention_first.1), channel_id=1, source_target_pairs={{0,8},{8,0},{16,24},{24,16},{32,40},{40,32},{48,56},{56,48},{64,72... | collective-permute-start | bytes 1228808 | tf_op jit(solution)/shard_map/ppermute | solution.py:40
  42.6 35.4 %copy-start = (bf16[1024,160]{0,1:T(8,128)(2,1)S(1)}, bf16[1024,160]{0,1:T(8,128)(2,1)}, u32[]{:S(2)}) copy-start(bf16[1024,160]{0,1:T(8,128)(2,1)} %param.15) | copy-start | bytes 983044
  43.5 7.2 %collective-permute-start.10 = (bf16[400,128]{1,0:T(8,128)(2,1)S(1)}, bf16[400,128]{1,0:T(8,128)(2,1)S(1)}, u32[]{:S(2)}, u32[]{:S(2)}) collective-permute-start(bf16[400,128]{1,0:T(8,128)(2,1)S(1)} %get-tuple-element.30), channel_id=1, source_target_pairs={{0,48},{8,56},{16,32},{24,40},{32,16},{40,24},{48,0},{56,8},{64,11... | collective-permute-start | bytes 307208 | tf_op jit(solution)/shard_map/ppermute | solution.py:40
  43.9 6.8 %collective-permute-start.8 = (bf16[400,128]{1,0:T(8,128)(2,1)S(1)}, bf16[400,128]{1,0:T(8,128)(2,1)S(1)}, u32[]{:S(2)}, u32[]{:S(2)}) collective-permute-start(bf16[400,128]{1,0:T(8,128)(2,1)S(1)} %get-tuple-element.28), channel_id=1, source_target_pairs={{0,32},{8,40},{16,48},{24,56},{32,0},{40,8},{48,16},{56,24},{64,96... | collective-permute-start | bytes 307208 | tf_op jit(solution)/shard_map/ppermute | solution.py:40
  44.5 6.7 %collective-permute-start.9 = (bf16[400,128]{1,0:T(8,128)(2,1)S(1)}, bf16[400,128]{1,0:T(8,128)(2,1)S(1)}, u32[]{:S(2)}, u32[]{:S(2)}) collective-permute-start(bf16[400,128]{1,0:T(8,128)(2,1)S(1)} %get-tuple-element.29), channel_id=1, source_target_pairs={{0,16},{8,24},{16,0},{24,8},{32,48},{40,56},{48,32},{56,40},{64,80... | collective-permute-start | bytes 307208 | tf_op jit(solution)/shard_map/ppermute | solution.py:40
  51.6 5.9 %collective-permute-start.11 = (bf16[400,128]{1,0:T(8,128)(2,1)S(1)}, bf16[400,128]{1,0:T(8,128)(2,1)S(1)}, u32[]{:S(2)}, u32[]{:S(2)}) collective-permute-start(bf16[400,128]{1,0:T(8,128)(2,1)S(1)} %get-tuple-element.32), channel_id=1, source_target_pairs={{0,64},{8,72},{16,80},{24,88},{32,96},{40,104},{48,112},{56,120},{... | collective-permute-start | bytes 307208 | tf_op jit(solution)/shard_map/ppermute | solution.py:40
  57.8 5.7 %collective-permute-start.12 = (bf16[400,128]{1,0:T(8,128)(2,1)S(1)}, bf16[400,128]{1,0:T(8,128)(2,1)S(1)}, u32[]{:S(2)}, u32[]{:S(2)}) collective-permute-start(bf16[400,128]{1,0:T(8,128)(2,1)S(1)} %get-tuple-element.34), channel_id=1, source_target_pairs={{0,192},{8,200},{16,208},{24,216},{32,224},{40,232},{48,240},{56,2... | collective-permute-start | bytes 307208 | tf_op jit(solution)/shard_map/ppermute | solution.py:40
  63.9 3.9 %collective-permute-start.13 = (bf16[48,1024]{1,0:T(8,128)(2,1)S(1)}, bf16[48,1024]{1,0:T(8,128)(2,1)S(1)}, u32[]{:S(2)}, u32[]{:S(2)}) collective-permute-start(bf16[48,1024]{1,0:T(8,128)(2,1)S(1)} %finish.1.refs_0_), channel_id=1, source_target_pairs={{0,16},{8,24},{16,0},{24,8},{32,48},{40,56},{48,32},{56,40},{64,80... | collective-permute-start | bytes 294920 | tf_op jit(solution)/shard_map/ppermute | solution.py:40
  64.0 6.3 %collective-permute-start.14 = (bf16[48,1024]{1,0:T(8,128)(2,1)S(1)}, bf16[48,1024]{1,0:T(8,128)(2,1)S(1)}, u32[]{:S(2)}, u32[]{:S(2)}) collective-permute-start(bf16[48,1024]{1,0:T(8,128)(2,1)S(1)} %finish.1.refs_0_), channel_id=1, source_target_pairs={{0,32},{8,40},{16,48},{24,56},{32,0},{40,8},{48,16},{56,24},{64,96... | collective-permute-start | bytes 294920 | tf_op jit(solution)/shard_map/ppermute | solution.py:40
  67.3 4.7 %collective-permute-start.15 = (bf16[48,1024]{1,0:T(8,128)(2,1)S(1)}, bf16[48,1024]{1,0:T(8,128)(2,1)S(1)}, u32[]{:S(2)}, u32[]{:S(2)}) collective-permute-start(bf16[48,1024]{1,0:T(8,128)(2,1)S(1)} %finish.1.refs_0_), channel_id=1, source_target_pairs={{0,48},{8,56},{16,32},{24,40},{32,16},{40,24},{48,0},{56,8},{64,11... | collective-permute-start | bytes 294920 | tf_op jit(solution)/shard_map/ppermute | solution.py:40
  72.0 6.0 %collective-permute-start.16 = (bf16[4,48,1024]{2,1,0:T(8,128)(2,1)S(1)}, bf16[4,48,1024]{2,1,0:T(8,128)(2,1)S(1)}, u32[]{:S(2)}, u32[]{:S(2)}) collective-permute-start(bf16[4,48,1024]{2,1,0:T(8,128)(2,1)S(1)} %join.5.other_ref), channel_id=1, source_target_pairs={{0,8},{8,0},{16,24},{24,16},{32,40},{40,32},{48,56},{56,48},{64,72... | collective-permute-start | bytes 1179656 | tf_op jit(solution)/shard_map/ppermute | solution.py:40

commit v5 on v4

--- a/solution.py
+++ b/solution.py
@@ -62,9 +62,9 @@
     )(*pieces)
 
 
-def gather_y(x):
+def around_y(x):
     found = {d: exchange(x, 0, d, 0) for d in AROUND_Y}
-    return join(join_kernel, [x] + [found[d] for d in range(1, Y)])
+    return [x] + [found[d] for d in range(1, Y)]
 
 
 def copy_kernel(in_ref, out_ref):
@@ -159,10 +159,15 @@
     prefix(queries_ref, [0], keys_ref, wide_ref, scores, put)
 
 
-def first_kernel(info_in, queries_ref, keys_ref, wide_ref, tail_k, tail_v, *refs):
-    begun, part_ref, scores, state, (chosen, info_ref, sem) = refs[:3], refs[3], refs[4], refs[5:8], refs[8:]
-    copy = pltpu.make_async_copy(info_in, info_ref, sem.at[0])
-    copy.start()
+def first_kernel(info_in, queries_ref, keys_ref, wide_ref, tail_keys_hbm, tail_values_hbm, *refs):
+    begun, (part_ref, tail_k, tail_v, scores), state, (chosen, info_ref, sem) = refs[:3], refs[3:7], refs[7:10], refs[10:]
+    copies = [
+        pltpu.make_async_copy(info_in, info_ref, sem.at[0]),
+        pltpu.make_async_copy(tail_keys_hbm, tail_k, sem.at[1]),
+        pltpu.make_async_copy(tail_values_hbm, tail_v, sem.at[2]),
+    ]
+    for copy in copies:
+        copy.start()
     for ref, old in zip(state, begun):
         ref[:CHUNK, :] = old[...]
     places = [CHUNK, 2 * CHUNK, 3 * CHUNK]
@@ -172,7 +177,8 @@
             ref[pl.ds(places[i], CHUNK), :] = value
 
     prefix(queries_ref, places, keys_ref, wide_ref, scores, put)
-    copy.wait()
+    for copy in copies:
+        copy.wait()
     add_suffixes(0, queries_ref, tail_k, tail_v, state, chosen, info_ref)
     for dy in range(Y):
         emit(part_ref.at[dy], *state, dy * CHUNK)
@@ -203,17 +209,6 @@
     for copy in copies:
         copy.start()
     wide_ref[:, WIDTH:] = jnp.ones_like(wide_ref[:, WIDTH:])
-    for copy in copies:
-        copy.wait()
-
-
-def fetch_kernel(after_ref, tail_keys_hbm, tail_values_hbm, tail_k, tail_v, sem):
-    copies = [
-        pltpu.make_async_copy(tail_keys_hbm, tail_k, sem.at[0]),
-        pltpu.make_async_copy(tail_values_hbm, tail_v, sem.at[1]),
-    ]
-    for copy in copies:
-        copy.start()
     for copy in copies:
         copy.wait()
 
@@ -329,18 +324,6 @@
             suffix_values.reshape(LOCAL, SUFFIX, WIDTH),
         )
     ]
-    mine = queries.reshape(ROWS, WIDTH)
-    found = [exchange(mine, d, 0, 0) for d in AROUND_Z[1:]]
-    held = pl.pallas_call(
-        copy_kernel,
-        out_shape=jax.ShapeDtypeStruct(mine.shape, bf16),
-        in_specs=[VMEM],
-        out_specs=VMEM,
-        compiler_params=PARAMS,
-        name="hold",
-    )(mine)
-    by_z = join(join_z_kernel, [held] + found).reshape(CHUNK, WIDTH)
-    by_y = gather_y(by_z).reshape(Y * CHUNK, WIDTH)
     def call(kernel, name, out, ins, *operands, scratch=(), chunks=0):
         return pl.pallas_call(
             kernel,
@@ -363,7 +346,7 @@
     scores = [pltpu.VMEM((2, CHUNK, prompt), jnp.float32)]
     state = [pltpu.VMEM((Y * CHUNK + HEADS_LOCAL, WIDTH), jnp.float32)] * 3
     lists = [pltpu.SMEM((LOCAL + 4,), jnp.int32), pltpu.SMEM((2 * LOCAL,), jnp.int32)]
-    lists += [pltpu.SemaphoreType.DMA((1,))]
+    lists += [pltpu.SemaphoreType.DMA((3,))]
     rows_of = [jax.ShapeDtypeStruct((CHUNK, WIDTH), jnp.float32)] * 3
     tail = jax.ShapeDtypeStruct((LOCAL, SUFFIX, WIDTH), bf16)
     prompt_shapes = [
@@ -371,13 +354,27 @@
         jax.ShapeDtypeStruct((prompt, 2 * WIDTH), bf16),
     ]
     keys, wide = call(prepare_kernel, "prepare", prompt_shapes, [hbm] * 2, *caches[:2], scratch=two)
+    mine = queries.reshape(ROWS, WIDTH)
+    found = [exchange(mine, d, 0, 0) for d in AROUND_Z[1:]]
+    held = pl.pallas_call(
+        copy_kernel,
+        out_shape=jax.ShapeDtypeStruct(mine.shape, bf16),
+        in_specs=[VMEM],
+        out_specs=VMEM,
+        compiler_params=PARAMS,
+        name="hold",
+    )(mine)
+    found, keys, wide = lax.optimization_barrier((found, keys, wide))
+    by_z = join(join_z_kernel, [held] + found).reshape(CHUNK, WIDTH)
+    pieces = around_y(by_z)
     begun = call(own_kernel, "attention_own", rows_of, [], by_z, keys, wide, scratch=scores, chunks=1)
-    tails = call(fetch_kernel, "fetch", [tail, tail], [VMEM, hbm, hbm], begun[0], *caches[2:], scratch=two)
-
+
+    pieces, begun, info = lax.optimization_barrier((pieces, begun, info))
+    by_y = join(join_kernel, pieces).reshape(Y * CHUNK, WIDTH)
     by_core = exchange(by_y, 0, 0, 1)
-    first = call(
-        first_kernel, "attention_first", shape(bf16, Y), anywhere, info, by_y, keys, wide, *tails, *begun,
-        scratch=scores + state + lists, chunks=3,
+    first, *tails = call(
+        first_kernel, "attention_first", [shape(bf16, Y), tail, tail], anywhere + [VMEM] * 3 + [hbm] * 2,
+        info, by_y, keys, wide, *caches[2:], *begun, scratch=scores + state + lists, chunks=3,
     )
     arrived = exchange(first, 0, 0, 1)
     second = call(
@@ -410,7 +407,7 @@
         name="finish",
     )(kept, exchange(sent, 3, 0, 0))
 
-    ours = gather_y(attention)
+    ours = join(join_kernel, around_y(attention))
     theirs = exchange(ours, 0, 0, 1)
     columns_local = out_weight.shape[1]
     terms = pl.pallas_call(

time: 89.6 us -> 85.6 us (0.955)
  waiting for transfers between devices: 27.6 us -> 23.8 us
  Pallas kernels: 18.7 us -> 16.1 us
  starting transfers between devices: 30.1 us -> 32.1 us
    ppermute x17, waiting for transfers between devices: 27.6 us -> 23.8 us  [exchange(): return lax.ppermute(x, 'seq', pairs)]
    pallas_call x6 -> x5, Pallas kernels: 16.6 us -> 14 us  [call(): pl.pallas_call(kernel, out_shape=out, in_specs=ins + [VMEM] * (len(operan...]
    ppermute x17, starting transfers between devices: 30.1 us -> 32.1 us  [exchange(): return lax.ppermute(x, 'seq', pairs)]
  transfers between devices with their start and end apart: 17 -> 17, of which waited for: 10 -> 10; matrix products, arithmetic and copies ran while one was open for 2% -> 2% of each run, Pallas kernels for 18% -> 15%
where the time goes in v5:
time: 85.6 us; the launch traced here: 84.9 us
  starting transfers between devices  32.1 us (38%)
  waiting for transfers between devices  23.8 us (28%)
  Pallas kernels  16.1 us (19%)
  blocking collectives  9.73 us (11%)
  other arithmetic  2.29 us (3%)
    ppermute x17, starting transfers between devices, exchange(): return lax.ppermute(x, 'seq', pairs)  32.1 us
    ppermute x17, waiting for transfers between devices, exchange(): return lax.ppermute(x, 'seq', pairs)  23.8 us
    pallas_call x5, Pallas kernels, call(): pl.pallas_call(kernel, out_shape=out, in_specs=ins + [VMEM] * (len(operan...  14 us
    all_to_all x1, blocking collectives, per_device(): lax.all_to_all(terms, 'head', split_axis=0, concat_axis=0, tiled=True)  9.73 us
  transfers between devices with their start and end apart: 17, of which 10 were waited for; matrix products, arithmetic and copies ran while one was open for 2% of the time, Pallas kernels for 15%

profile of v5, /device:TPU:1, one launch (start us, length us, event | category | flops | bytes accessed | tf_op | source)
XLA Modules:
  0.0 84.9 jit_solution(8643429406301791108)
XLA Ops:
  0.0 3.8 %collective-permute-start = (bf16[96,128]{1,0:T(8,128)(2,1)}, bf16[96,128]{1,0:T(8,128)(2,1)S(1)}, u32[]{:S(2)}, u32[]{:S(2)}) collective-permute-start(bf16[96,128]{1,0:T(8,128)(2,1)} %bitcast.18), channel_id=1, source_target_pairs={{0,64},{8,72},{16,80},{24,88},{32,96},{40,104},{48,112},{56,120},{... | collective-permute-start | bytes 73736 | tf_op jit(solution)/shard_map/ppermute | solution.py:40
  3.8 4.2 %collective-permute-start.1 = (bf16[96,128]{1,0:T(8,128)(2,1)}, bf16[96,128]{1,0:T(8,128)(2,1)S(1)}, u32[]{:S(2)}, u32[]{:S(2)}) collective-permute-start(bf16[96,128]{1,0:T(8,128)(2,1)} %bitcast.19), channel_id=1, source_target_pairs={{0,192},{8,200},{16,208},{24,216},{32,224},{40,232},{48,240},{56,2... | collective-permute-start | bytes 73736 | tf_op jit(solution)/shard_map/ppermute | solution.py:40
  8.0 0.9 %collective-permute-start.2 = (bf16[96,128]{1,0:T(8,128)(2,1)}, bf16[96,128]{1,0:T(8,128)(2,1)S(1)}, u32[]{:S(2)}, u32[]{:S(2)}) collective-permute-start(bf16[96,128]{1,0:T(8,128)(2,1)} %bitcast.20), channel_id=1, source_target_pairs={{0,128},{8,136},{16,144},{24,152},{32,160},{40,168},{48,176},{56,1... | collective-permute-start | bytes 73736 | tf_op jit(solution)/shard_map/ppermute | solution.py:40
  8.9 0.9 %select_reduce_fusion = s32[12]{0:T(128)S(1)} fusion(s32[384]{0:T(512)} %param.14, s32[12]{0:T(128)S(1)} %iota_add_fusion), kind=kLoop, calls=%fused_computation.1 | loop fusion | flops 13812 | bytes 1632 | tf_op jit(solution)/shard_map/reduce_sum | solution.py:308
  9.9 0.7 copy-done.1
  10.6 1.2 %prepare.1 = (bf16[2048,128]{1,0:T(8,128)(2,1)S(1)}, bf16[2048,256]{1,0:T(8,128)(2,1)S(1)}) custom-call(bf16[2048,128]{1,0:T(8,128)(2,1)} %bitcast.24, bf16[2048,128]{1,0:T(8,128)(2,1)} %bitcast.25), custom_call_target="tpu_custom_call" | custom-call | bytes 4194304 | tf_op jit(solution)/shard_map/prepare/pallas_call | solution.py:328
  11.8 3.2 %collective-permute-done.2.refs_3_ = bf16[96,128]{1,0:T(8,128)(2,1)S(1)} collective-permute-done((bf16[96,128]{1,0:T(8,128)(2,1)}, bf16[96,128]{1,0:T(8,128)(2,1)S(1)}, u32[]{:S(2)}, u32[]{:S(2)}) %collective-permute-start.2) | collective-permute-done | bytes 24608 | tf_op jit(solution)/shard_map/ppermute | solution.py:40
  15.1 1.4 %collective-permute-start.3 = (bf16[384,128]{1,0:T(8,128)(2,1)S(1)}, bf16[384,128]{1,0:T(8,128)(2,1)S(1)}, u32[]{:S(2)}, u32[]{:S(2)}) collective-permute-start(bf16[384,128]{1,0:T(8,128)(2,1)S(1)} %bitcast.11), channel_id=1, source_target_pairs={{0,16},{8,24},{16,0},{24,8},{32,48},{40,56},{48,32},{56,40},{64,80... | collective-permute-start | bytes 294920 | tf_op jit(solution)/shard_map/ppermute | solution.py:40
  16.5 2.6 %collective-permute-start.4 = (bf16[384,128]{1,0:T(8,128)(2,1)S(1)}, bf16[384,128]{1,0:T(8,128)(2,1)S(1)}, u32[]{:S(2)}, u32[]{:S(2)}) collective-permute-start(bf16[384,128]{1,0:T(8,128)(2,1)S(1)} %bitcast.12), channel_id=1, source_target_pairs={{0,32},{8,40},{16,48},{24,56},{32,0},{40,8},{48,16},{56,24},{64,96... | collective-permute-start | bytes 294920 | tf_op jit(solution)/shard_map/ppermute | solution.py:40
  19.1 0.7 pad_add_fusion.info_in
  19.8 1.9 %attention_own.1 = (f32[384,128]{1,0:T(8,128)S(1)}, f32[384,128]{1,0:T(8,128)S(1)}, f32[384,128]{1,0:T(8,128)S(1)}) custom-call(bf16[384,128]{1,0:T(8,128)(2,1)S(1)} %bitcast.14, bf16[2048,128]{1,0:T(8,128)(2,1)S(1)} %get-tuple-element.39.keys_ref, bf16[2048,256]{1,0:T(8,128)(2,1)S(1)} %get-tuple-element.40.wide_ref), custom_call_target="tpu_custom_call" | custom-call | flops 402653184 | bytes 4194304 | tf_op jit(solution)/shard_map/attention_own/pallas_call | solution.py:328
  22.1 1.9 %collective-permute-done.5.refs_3_ = bf16[384,128]{1,0:T(8,128)(2,1)S(1)} collective-permute-done((bf16[384,128]{1,0:T(8,128)(2,1)S(1)}, bf16[384,128]{1,0:T(8,128)(2,1)S(1)}, u32[]{:S(2)}, u32[]{:S(2)}) %collective-permute-start.5) | collective-permute-done | bytes 98336 | tf_op jit(solution)/shard_map/ppermute | solution.py:40
  24.1 3.6 %collective-permute-start.6 = (bf16[1536,128]{1,0:T(8,128)(2,1)S(1)}, bf16[1536,128]{1,0:T(8,128)(2,1)S(1)}, u32[]{:S(2)}, u32[]{:S(2)}) collective-permute-start(bf16[1536,128]{1,0:T(8,128)(2,1)S(1)} %bitcast.9), channel_id=1, source_target_pairs={{0,8},{8,0},{16,24},{24,16},{32,40},{40,32},{48,56},{56,48},{64,72... | collective-permute-start | bytes 1179656 | tf_op jit(solution)/shard_map/ppermute | solution.py:40
  27.7 4.4 %attention_first.1 = (bf16[4,400,128]{2,1,0:T(8,128)(2,1)S(1)}, bf16[12,1024,128]{2,1,0:T(8,128)(2,1)S(1)}, bf16[12,1024,128]{2,1,0:T(8,128)(2,1)S(1)}) custom-call(s32[24]{0:T(128)S(1)} %pad_add_fusion.info_in, bf16[1536,128]{1,0:T(8,128)(2,1)S(1)} %bitcast.10, bf16[2048,128]{1,0:T(8,128)(2,1)S(1)} %get-tuple-element.39.keys_ref, ...), custom_call_target="tpu_custom_call" | custom-call | flops 1207959552 | bytes 4194304 | tf_op jit(solution)/shard_map/attention_first/pallas_call | solution.py:328
  32.4 5.6 %attention_second.1.mine_ref = f32[4,400,128]{2,1,0:T(8,128)S(1)} custom-call(s32[24]{0:T(128)S(1)} %pad_add_fusion.info_in, bf16[1536,128]{1,0:T(8,128)(2,1)S(1)} %collective-permute-done.6.queries_ref, bf16[2048,128]{1,0:T(8,128)(2,1)S(1)} %get-tuple-element.39.keys_ref, bf16[2048,256]{1,0:T(8,128)(2,1)S(1)} %get-tuple-element.40.wide_ref, ...), custom_call_target="tpu_custom_call" | custom-call | flops 1610612736 | bytes 4194304 | tf_op jit(solution)/shard_map/attention_second/pallas_call | solution.py:328
  38.0 0.9 %merge_core.1 = (f32[400,128]{1,0:T(8,128)S(1)}, bf16[400,128]{1,0:T(8,128)(2,1)S(1)}, bf16[400,128]{1,0:T(8,128)(2,1)S(1)}, bf16[400,128]{1,0:T(8,128)(2,1)S(1)}) custom-call(f32[4,400,128]{2,1,0:T(8,128)S(1)} %attention_second.1.mine_ref, bf16[4,400,128]{2,1,0:T(8,128)(2,1)S(1)} %collective-permute-done.7.other_ref), custom_call_target="tpu_custom_call" | custom-call | bytes 4194304 | tf_op jit(solution)/shard_map/merge_core/pallas_call | solution.py:328
  38.9 0.4 collective-permute-start.10
  39.5 2.7 %collective-permute-start.9 = (bf16[400,128]{1,0:T(8,128)(2,1)S(1)}, bf16[400,128]{1,0:T(8,128)(2,1)S(1)}, u32[]{:S(2)}, u32[]{:S(2)}) collective-permute-start(bf16[400,128]{1,0:T(8,128)(2,1)S(1)} %get-tuple-element.57), channel_id=1, source_target_pairs={{0,16},{8,24},{16,0},{24,8},{32,48},{40,56},{48,32},{56,40},{64,80... | collective-permute-start | bytes 307208 | tf_op jit(solution)/shard_map/ppermute | solution.py:40
  42.3 3.2 %collective-permute-done.10.refs_3_ = bf16[400,128]{1,0:T(8,128)(2,1)S(1)} collective-permute-done((bf16[400,128]{1,0:T(8,128)(2,1)S(1)}, bf16[400,128]{1,0:T(8,128)(2,1)S(1)}, u32[]{:S(2)}, u32[]{:S(2)}) %collective-permute-start.10) | collective-permute-done | bytes 102432 | tf_op jit(solution)/shard_map/ppermute | solution.py:40
  45.5 1.1 %collective-permute-done.9.refs_2_ = bf16[400,128]{1,0:T(8,128)(2,1)S(1)} collective-permute-done((bf16[400,128]{1,0:T(8,128)(2,1)S(1)}, bf16[400,128]{1,0:T(8,128)(2,1)S(1)}, u32[]{:S(2)}, u32[]{:S(2)}) %collective-permute-start.9) | collective-permute-done | bytes 102432 | tf_op jit(solution)/shard_map/ppermute | solution.py:40
  47.1 1.3 %collective-permute-start.11 = (bf16[400,128]{1,0:T(8,128)(2,1)S(1)}, bf16[400,128]{1,0:T(8,128)(2,1)S(1)}, u32[]{:S(2)}, u32[]{:S(2)}) collective-permute-start(bf16[400,128]{1,0:T(8,128)(2,1)S(1)} %get-tuple-element.60), channel_id=1, source_target_pairs={{0,64},{8,72},{16,80},{24,88},{32,96},{40,104},{48,112},{56,120},{... | collective-permute-start | bytes 307208 | tf_op jit(solution)/shard_map/ppermute | solution.py:40
  48.3 4.6 %collective-permute-done.11.refs_1_ = bf16[400,128]{1,0:T(8,128)(2,1)S(1)} collective-permute-done((bf16[400,128]{1,0:T(8,128)(2,1)S(1)}, bf16[400,128]{1,0:T(8,128)(2,1)S(1)}, u32[]{:S(2)}, u32[]{:S(2)}) %collective-permute-start.11) | collective-permute-done | bytes 102432 | tf_op jit(solution)/shard_map/ppermute | solution.py:40
  53.4 5.6 %collective-permute-done.12.other_ref = bf16[400,128]{1,0:T(8,128)(2,1)S(1)} collective-permute-done((bf16[400,128]{1,0:T(8,128)(2,1)S(1)}, bf16[400,128]{1,0:T(8,128)(2,1)S(1)}, u32[]{:S(2)}, u32[]{:S(2)}) %collective-permute-start.12) | collective-permute-done | bytes 102432 | tf_op jit(solution)/shard_map/ppermute | solution.py:40
  59.5 1.0 %collective-permute-start.14 = (bf16[48,1024]{1,0:T(8,128)(2,1)S(1)}, bf16[48,1024]{1,0:T(8,128)(2,1)S(1)}, u32[]{:S(2)}, u32[]{:S(2)}) collective-permute-start(bf16[48,1024]{1,0:T(8,128)(2,1)S(1)} %finish.1.refs_0_), channel_id=1, source_target_pairs={{0,32},{8,40},{16,48},{24,56},{32,0},{40,8},{48,16},{56,24},{64,96... | collective-permute-start | bytes 294920 | tf_op jit(solution)/shard_map/ppermute | solution.py:40
  60.4 2.9 %collective-permute-start.15 = (bf16[48,1024]{1,0:T(8,128)(2,1)S(1)}, bf16[48,1024]{1,0:T(8,128)(2,1)S(1)}, u32[]{:S(2)}, u32[]{:S(2)}) collective-permute-start(bf16[48,1024]{1,0:T(8,128)(2,1)S(1)} %finish.1.refs_0_), channel_id=1, source_target_pairs={{0,48},{8,56},{16,32},{24,40},{32,16},{40,24},{48,0},{56,8},{64,11... | collective-permute-start | bytes 294920 | tf_op jit(solution)/shard_map/ppermute | solution.py:40
  63.3 1.2 %collective-permute-done.14.refs_2_ = bf16[48,1024]{1,0:T(8,128)(2,1)S(1)} collective-permute-done((bf16[48,1024]{1,0:T(8,128)(2,1)S(1)}, bf16[48,1024]{1,0:T(8,128)(2,1)S(1)}, u32[]{:S(2)}, u32[]{:S(2)}) %collective-permute-start.14) | collective-permute-done | bytes 98336 | tf_op jit(solution)/shard_map/ppermute | solution.py:40
  64.5 1.0 %collective-permute-done.15.refs_3_ = bf16[48,1024]{1,0:T(8,128)(2,1)S(1)} collective-permute-done((bf16[48,1024]{1,0:T(8,128)(2,1)S(1)}, bf16[48,1024]{1,0:T(8,128)(2,1)S(1)}, u32[]{:S(2)}, u32[]{:S(2)}) %collective-permute-start.15) | collective-permute-done | bytes 98336 | tf_op jit(solution)/shard_map/ppermute | solution.py:40
  65.6 6.6 %collective-permute-start.16 = (bf16[4,48,1024]{2,1,0:T(8,128)(2,1)S(1)}, bf16[4,48,1024]{2,1,0:T(8,128)(2,1)S(1)}, u32[]{:S(2)}, u32[]{:S(2)}) collective-permute-start(bf16[4,48,1024]{2,1,0:T(8,128)(2,1)S(1)} %join.5.other_ref), channel_id=1, source_target_pairs={{0,8},{8,0},{16,24},{24,16},{32,40},{40,32},{48,56},{56,48},{64,72... | collective-permute-start | bytes 1179656 | tf_op jit(solution)/shard_map/ppermute | solution.py:40
  72.2 1.3 %collective-permute-done.16.mine_ref = bf16[4,48,1024]{2,1,0:T(8,128)(2,1)S(1)} collective-permute-done((bf16[4,48,1024]{2,1,0:T(8,128)(2,1)S(1)}, bf16[4,48,1024]{2,1,0:T(8,128)(2,1)S(1)}, u32[]{:S(2)}, u32[]{:S(2)}) %collective-permute-start.16) | collective-permute-done | bytes 393248 | tf_op jit(solution)/shard_map/ppermute | solution.py:40
  73.5 0.9 %project.1 = bf16[384,160]{1,0:T(8,128)(2,1)S(1)} custom-call(bf16[4,48,1024]{2,1,0:T(8,128)(2,1)S(1)} %collective-permute-done.16.mine_ref, bf16[4,48,1024]{2,1,0:T(8,128)(2,1)S(1)} %join.5.other_ref, bf16[160,1024]{1,0:T(8,128)(2,1)S(1)} %bitcast.17), custom_call_target="tpu_custom_call" | custom-call | tf_op jit(solution)/shard_map/project/pallas_call | solution.py:413
  74.5 9.7 %all_to_all.5 = bf16[8,48,160]{2,1,0:T(8,128)(2,1)S(1)} all-to-all(bf16[8,48,160]{2,1,0:T(8,128)(2,1)S(1)} %bitcast.16), channel_id=1, replica_groups=mesh['seq'=32,'head'=8] {'head'}, dimensions={0} | all-to-all | bytes 245760 | tf_op jit(solution)/shard_map/all_to_all | solution.py:424
  84.2 0.7 convert_reduce_fusion
  (25 shorter events, 2.3 us)
Async XLA Ops:
  0.0 11.8 %collective-permute-start = (bf16[96,128]{1,0:T(8,128)(2,1)}, bf16[96,128]{1,0:T(8,128)(2,1)S(1)}, u32[]{:S(2)}, u32[]{:S(2)}) collective-permute-start(bf16[96,128]{1,0:T(8,128)(2,1)} %bitcast.18), channel_id=1, source_target_pairs={{0,64},{8,72},{16,80},{24,88},{32,96},{40,104},{48,112},{56,120},{... | collective-permute-start | bytes 73736 | tf_op jit(solution)/shard_map/ppermute | solution.py:40
  3.8 8.0 %collective-permute-start.1 = (bf16[96,128]{1,0:T(8,128)(2,1)}, bf16[96,128]{1,0:T(8,128)(2,1)S(1)}, u32[]{:S(2)}, u32[]{:S(2)}) collective-permute-start(bf16[96,128]{1,0:T(8,128)(2,1)} %bitcast.19), channel_id=1, source_target_pairs={{0,192},{8,200},{16,208},{24,216},{32,224},{40,232},{48,240},{56,2... | collective-permute-start | bytes 73736 | tf_op jit(solution)/shard_map/ppermute | solution.py:40
  8.0 7.0 %collective-permute-start.2 = (bf16[96,128]{1,0:T(8,128)(2,1)}, bf16[96,128]{1,0:T(8,128)(2,1)S(1)}, u32[]{:S(2)}, u32[]{:S(2)}) collective-permute-start(bf16[96,128]{1,0:T(8,128)(2,1)} %bitcast.20), channel_id=1, source_target_pairs={{0,128},{8,136},{16,144},{24,152},{32,160},{40,168},{48,176},{56,1... | collective-permute-start | bytes 73736 | tf_op jit(solution)/shard_map/ppermute | solution.py:40
  9.8 0.7 copy-start.1
  15.1 6.7 %collective-permute-start.3 = (bf16[384,128]{1,0:T(8,128)(2,1)S(1)}, bf16[384,128]{1,0:T(8,128)(2,1)S(1)}, u32[]{:S(2)}, u32[]{:S(2)}) collective-permute-start(bf16[384,128]{1,0:T(8,128)(2,1)S(1)} %bitcast.11), channel_id=1, source_target_pairs={{0,16},{8,24},{16,0},{24,8},{32,48},{40,56},{48,32},{56,40},{64,80... | collective-permute-start | bytes 294920 | tf_op jit(solution)/shard_map/ppermute | solution.py:40
  16.5 5.7 %collective-permute-start.4 = (bf16[384,128]{1,0:T(8,128)(2,1)S(1)}, bf16[384,128]{1,0:T(8,128)(2,1)S(1)}, u32[]{:S(2)}, u32[]{:S(2)}) collective-permute-start(bf16[384,128]{1,0:T(8,128)(2,1)S(1)} %bitcast.12), channel_id=1, source_target_pairs={{0,32},{8,40},{16,48},{24,56},{32,0},{40,8},{48,16},{56,24},{64,96... | collective-permute-start | bytes 294920 | tf_op jit(solution)/shard_map/ppermute | solution.py:40
  19.1 5.0 %collective-permute-start.5 = (bf16[384,128]{1,0:T(8,128)(2,1)S(1)}, bf16[384,128]{1,0:T(8,128)(2,1)S(1)}, u32[]{:S(2)}, u32[]{:S(2)}) collective-permute-start(bf16[384,128]{1,0:T(8,128)(2,1)S(1)} %bitcast.13), channel_id=1, source_target_pairs={{0,48},{8,56},{16,32},{24,40},{32,16},{40,24},{48,0},{56,8},{64,11... | collective-permute-start | bytes 294920 | tf_op jit(solution)/shard_map/ppermute | solution.py:40
  24.1 8.3 %collective-permute-start.6 = (bf16[1536,128]{1,0:T(8,128)(2,1)S(1)}, bf16[1536,128]{1,0:T(8,128)(2,1)S(1)}, u32[]{:S(2)}, u32[]{:S(2)}) collective-permute-start(bf16[1536,128]{1,0:T(8,128)(2,1)S(1)} %bitcast.9), channel_id=1, source_target_pairs={{0,8},{8,0},{16,24},{24,16},{32,40},{40,32},{48,56},{56,48},{64,72... | collective-permute-start | bytes 1179656 | tf_op jit(solution)/shard_map/ppermute | solution.py:40
  32.1 5.9 %collective-permute-start.7 = (bf16[4,400,128]{2,1,0:T(8,128)(2,1)S(1)}, bf16[4,400,128]{2,1,0:T(8,128)(2,1)S(1)}, u32[]{:S(2)}, u32[]{:S(2)}) collective-permute-start(bf16[4,400,128]{2,1,0:T(8,128)(2,1)S(1)} %get-tuple-element.54), channel_id=1, source_target_pairs={{0,8},{8,0},{16,24},{24,16},{32,40},{40,32},{48,56},{56,48},{64,72... | collective-permute-start | bytes 1228808 | tf_op jit(solution)/shard_map/ppermute | solution.py:40
  38.0 35.5 %copy-start = (bf16[1024,160]{0,1:T(8,128)(2,1)S(1)}, bf16[1024,160]{0,1:T(8,128)(2,1)}, u32[]{:S(2)}) copy-start(bf16[1024,160]{0,1:T(8,128)(2,1)} %param.15) | copy-start | bytes 983044
  38.9 6.6 %collective-permute-start.10 = (bf16[400,128]{1,0:T(8,128)(2,1)S(1)}, bf16[400,128]{1,0:T(8,128)(2,1)S(1)}, u32[]{:S(2)}, u32[]{:S(2)}) collective-permute-start(bf16[400,128]{1,0:T(8,128)(2,1)S(1)} %get-tuple-element.58), channel_id=1, source_target_pairs={{0,48},{8,56},{16,32},{24,40},{32,16},{40,24},{48,0},{56,8},{64,11... | collective-permute-start | bytes 307208 | tf_op jit(solution)/shard_map/ppermute | solution.py:40
  39.3 6.1 %collective-permute-start.8 = (bf16[400,128]{1,0:T(8,128)(2,1)S(1)}, bf16[400,128]{1,0:T(8,128)(2,1)S(1)}, u32[]{:S(2)}, u32[]{:S(2)}) collective-permute-start(bf16[400,128]{1,0:T(8,128)(2,1)S(1)} %get-tuple-element.56), channel_id=1, source_target_pairs={{0,32},{8,40},{16,48},{24,56},{32,0},{40,8},{48,16},{56,24},{64,96... | collective-permute-start | bytes 307208 | tf_op jit(solution)/shard_map/ppermute | solution.py:40
  39.5 7.1 %collective-permute-start.9 = (bf16[400,128]{1,0:T(8,128)(2,1)S(1)}, bf16[400,128]{1,0:T(8,128)(2,1)S(1)}, u32[]{:S(2)}, u32[]{:S(2)}) collective-permute-start(bf16[400,128]{1,0:T(8,128)(2,1)S(1)} %get-tuple-element.57), channel_id=1, source_target_pairs={{0,16},{8,24},{16,0},{24,8},{32,48},{40,56},{48,32},{56,40},{64,80... | collective-permute-start | bytes 307208 | tf_op jit(solution)/shard_map/ppermute | solution.py:40
  47.1 5.9 %collective-permute-start.11 = (bf16[400,128]{1,0:T(8,128)(2,1)S(1)}, bf16[400,128]{1,0:T(8,128)(2,1)S(1)}, u32[]{:S(2)}, u32[]{:S(2)}) collective-permute-start(bf16[400,128]{1,0:T(8,128)(2,1)S(1)} %get-tuple-element.60), channel_id=1, source_target_pairs={{0,64},{8,72},{16,80},{24,88},{32,96},{40,104},{48,112},{56,120},{... | collective-permute-start | bytes 307208 | tf_op jit(solution)/shard_map/ppermute | solution.py:40
  53.3 5.7 %collective-permute-start.12 = (bf16[400,128]{1,0:T(8,128)(2,1)S(1)}, bf16[400,128]{1,0:T(8,128)(2,1)S(1)}, u32[]{:S(2)}, u32[]{:S(2)}) collective-permute-start(bf16[400,128]{1,0:T(8,128)(2,1)S(1)} %get-tuple-element.62), channel_id=1, source_target_pairs={{0,192},{8,200},{16,208},{24,216},{32,224},{40,232},{48,240},{56,2... | collective-permute-start | bytes 307208 | tf_op jit(solution)/shard_map/ppermute | solution.py:40
  59.4 3.9 %collective-permute-start.13 = (bf16[48,1024]{1,0:T(8,128)(2,1)S(1)}, bf16[48,1024]{1,0:T(8,128)(2,1)S(1)}, u32[]{:S(2)}, u32[]{:S(2)}) collective-permute-start(bf16[48,1024]{1,0:T(8,128)(2,1)S(1)} %finish.1.refs_0_), channel_id=1, source_target_pairs={{0,16},{8,24},{16,0},{24,8},{32,48},{40,56},{48,32},{56,40},{64,80... | collective-permute-start | bytes 294920 | tf_op jit(solution)/shard_map/ppermute | solution.py:40
  59.5 5.1 %collective-permute-start.14 = (bf16[48,1024]{1,0:T(8,128)(2,1)S(1)}, bf16[48,1024]{1,0:T(8,128)(2,1)S(1)}, u32[]{:S(2)}, u32[]{:S(2)}) collective-permute-start(bf16[48,1024]{1,0:T(8,128)(2,1)S(1)} %finish.1.refs_0_), channel_id=1, source_target_pairs={{0,32},{8,40},{16,48},{24,56},{32,0},{40,8},{48,16},{56,24},{64,96... | collective-permute-start | bytes 294920 | tf_op jit(solution)/shard_map/ppermute | solution.py:40
  60.4 5.2 %collective-permute-start.15 = (bf16[48,1024]{1,0:T(8,128)(2,1)S(1)}, bf16[48,1024]{1,0:T(8,128)(2,1)S(1)}, u32[]{:S(2)}, u32[]{:S(2)}) collective-permute-start(bf16[48,1024]{1,0:T(8,128)(2,1)S(1)} %finish.1.refs_0_), channel_id=1, source_target_pairs={{0,48},{8,56},{16,32},{24,40},{32,16},{40,24},{48,0},{56,8},{64,11... | collective-permute-start | bytes 294920 | tf_op jit(solution)/shard_map/ppermute | solution.py:40
  65.6 7.9 %collective-permute-start.16 = (bf16[4,48,1024]{2,1,0:T(8,128)(2,1)S(1)}, bf16[4,48,1024]{2,1,0:T(8,128)(2,1)S(1)}, u32[]{:S(2)}, u32[]{:S(2)}) collective-permute-start(bf16[4,48,1024]{2,1,0:T(8,128)(2,1)S(1)} %join.5.other_ref), channel_id=1, source_target_pairs={{0,8},{8,0},{16,24},{24,16},{32,40},{40,32},{48,56},{56,48},{64,72... | collective-permute-start | bytes 1179656 | tf_op jit(solution)/shard_map/ppermute | solution.py:40
